TPU v7x, 256 devices: a whole 4x4x8 slice. The times are simulated.
256 devices in a mesh: role: 4 (over x_lo, core), shard: 64 (over y, z, x_hi).
Axes of the slice: x: 4 (x_hi: 2, x_lo: 2; x = x_hi * 2 + x_lo), y: 4, z: 8, core: 2. Of those that a mesh axis runs over, the one named last changes fastest.
Arguments:
- cls_states: bfloat16 [32768, 768], P(('role', 'shard')), may hold values from -6 to 6
- trainer_in: bfloat16 [4, 3072, 768], P('role', 'shard'), may hold values from -0.21875 to 0.21875
- trainer_out: bfloat16 [4, 3072, 768], P('role', 'shard'), may hold values from -0.109375 to 0.109375
- stale_cache: bfloat16 [65536, 768], P(('role', 'shard')), may hold values from -6 to 6
- block_owner: int32 [16384, 1], P(('role', 'shard')), may hold values from 0 to 63; in each aligned block of 64 rows (0 to 63, 64 to 127, ...) at most 2 rows name the same one
- queries: bfloat16 [256, 768], P(('role', 'shard')), may hold values from -0.4296875 to 0.4296875
- neg_ids: int32 [256, 4096], P('role', 'shard'), may hold values from 0 to 255
- grades: int32 [256, 4096], P('role', 'shard'), may hold values from 0 to 4
Outputs:
- refreshed_cache: bfloat16 [65536, 768], P(('role', 'shard'))
- query_grad: float32 [256, 768], P(('role', 'shard'))
- list_loss: float32 [256], P(('role', 'shard'))
Inputs may be any that keep to these rules, and one draw needn't show every extreme that they name: `block_owner`: among the 64 rows of one device at most 2 name the same owner; in every draw some device names some owner exactly 2 times.
All inputs are finite; a program needn't handle non-finite values.
Results may differ from a plain program's by a relative error of at most 0.013.
Values may be sent and summed in bfloat16 or wider, within the bound.
No kernel may reach another device: no remote copies, remote signals or barrier semaphores. Data moves between devices by JAX's collectives and lax.ppermute only.
A program may use at most 64 MiB of HBM per device.

v0:
```python
import math

import jax
import jax.numpy as jnp
from jax import lax
from jax.sharding import PartitionSpec as P

CAP = 2


EPSILON = 1e-05
LOG_TWO = math.log(2.0)


def broadcast(array, axis, root):
    mine = lax.axis_index(axis) == root
    return lax.psum(jnp.where(mine, array, jnp.zeros_like(array)), axis)


def normalize(resid):
    average = jnp.mean(resid, -1, keepdims=True)
    centred = resid - average
    variance = jnp.mean(centred * centred, -1, keepdims=True)
    return centred * lax.rsqrt(variance + EPSILON)


def ideal_gain(gains):
    length = gains.shape[1]
    levels = jnp.exp2(jnp.arange(4, -1, -1).astype(jnp.float32))
    counts = jnp.sum((gains[:, None, :] == levels[None, :, None]).astype(jnp.float32), -1)
    ends = jnp.cumsum(counts, 1)
    starts = ends - counts
    position = jnp.arange(1, length + 1).astype(jnp.float32)
    table = jnp.concatenate(
        (jnp.zeros((1,), jnp.float32), jnp.cumsum(1.0 / jnp.log2(1.0 + position)))
    )
    places = jnp.arange(length + 1).astype(jnp.float32)

    def lookup(where_at):
        return jnp.sum(jnp.where(where_at[..., None] == places, table, 0.0), -1)

    return jnp.sum(levels[None, :] * (lookup(ends) - lookup(starts)), 1)


def rank_pass(packed):
    items, others = packed
    sigma = jax.nn.sigmoid(others[:, None, :] - items[:, :, None])
    return (0.5 + jnp.sum(sigma, -1), jnp.sum(sigma * (1.0 - sigma), -1))


def cross_pass(packed):
    items, others, weight = packed
    sigma = jax.nn.sigmoid(others[:, None, :] - items[:, :, None])
    return jnp.sum(sigma * (1.0 - sigma) * weight[:, None, :], -1)


def list_weights(gains, ideal, rank):
    logged = jnp.log2(1.0 + rank)
    weight = gains / (ideal[:, None] * LOG_TWO * (1.0 + rank) * logged * logged)
    return (weight, gains / logged)


def per_device(
    cls_states, trainer_in, trainer_out, stale_cache, block_owner, queries, neg_ids, grades
):
    shards = lax.axis_size("shard")
    roles = lax.axis_size("role")
    passages, width = cls_states.shape
    block_rows = passages // shards
    stacked = jnp.concatenate((trainer_in, trainer_out), 0)
    current = broadcast(stacked, "role", roles - 1)
    piece = lax.all_gather(current, "shard", axis=1, tiled=True)
    inner = lax.dot_general(
        cls_states, piece[0], (((1,), (1,)), ((), ())), preferred_element_type=jnp.float32
    )
    hidden = jax.nn.gelu(inner, approximate=False).astype(jnp.bfloat16)
    ffn = jnp.dot(hidden, piece[1], preferred_element_type=jnp.float32)
    fresh = normalize(cls_states.astype(jnp.float32) + ffn).astype(jnp.bfloat16)
    owner = block_owner[:, 0]
    onehot = (owner[:, None] == jnp.arange(shards)[None, :]).astype(jnp.float32)
    earlier = jnp.cumsum(onehot, 0) - onehot
    slot = jnp.sum(earlier * onehot, 1).astype(jnp.int32)
    target = owner * CAP + slot
    placing = (jnp.arange(shards * CAP)[:, None] == target[None, :]).astype(jnp.bfloat16)
    outgoing = jnp.dot(
        placing, fresh.reshape(shards, block_rows * width), preferred_element_type=jnp.float32
    )
    outgoing = outgoing.astype(jnp.bfloat16).reshape(shards, CAP, block_rows, width)
    filled = jnp.sum(placing.astype(jnp.float32), 1).astype(jnp.bfloat16).reshape(shards, CAP)
    arrived, present = (
        lax.all_to_all(outgoing, "shard", split_axis=0, concat_axis=0, tiled=True),
        lax.all_to_all(filled, "shard", split_axis=0, concat_axis=0, tiled=True),
    )
    stale_blocks = stale_cache.reshape(shards, CAP, block_rows, width)
    refreshed = jnp.where(present[:, :, None, None] > 0, arrived, stale_blocks).reshape(-1, width)
    group_queries = lax.all_gather(queries, "shard", axis=0, tiled=True)
    fetched = refreshed[neg_ids]
    scores = jnp.einsum("qjd,qd->qj", fetched, group_queries, preferred_element_type=jnp.float32)
    gains = jnp.exp2(grades.astype(jnp.float32))
    lists, owned = scores.shape
    local_lists = queries.shape[0]
    all_scores, all_gains = (
        lax.all_gather(scores, "shard", axis=1, tiled=True),
        lax.all_gather(gains, "shard", axis=1, tiled=True),
    )
    length = all_scores.shape[1]
    ideal = ideal_gain(all_gains)
    batches = lists // 8
    item_blocks = scores.reshape(batches, 8, owned)
    other_blocks = all_scores.reshape(batches, 8, length)
    rank, slope = lax.map(rank_pass, (item_blocks, other_blocks))
    rank = rank.reshape(lists, owned)
    slope = slope.reshape(lists, owned)
    weight, terms = list_weights(gains, ideal, rank)
    all_weight = lax.all_gather(weight, "shard", axis=1, tiled=True)
    cross = lax.map(cross_pass, (item_blocks, other_blocks, all_weight.reshape(batches, 8, length)))
    cross = cross.reshape(lists, owned)
    score_grad = (cross - weight * slope).astype(jnp.bfloat16)
    totals = lax.psum(jnp.sum(terms, 1), "shard")
    every_loss = 1.0 - totals / ideal
    list_loss = lax.dynamic_slice_in_dim(
        every_loss, lax.axis_index("shard") * local_lists, local_lists, 0
    )
    query_grad = lax.psum_scatter(
        jnp.einsum("qj,qjd->qd", score_grad, fetched, preferred_element_type=jnp.float32),
        "shard",
        scatter_dimension=0,
        tiled=True,
    )
    return (refreshed, query_grad, list_loss)


def solution(mesh):
    return jax.shard_map(
        per_device,
        mesh=mesh,
        in_specs=(
            P(("role", "shard"), None),
            P("role", "shard", None),
            P("role", "shard", None),
            P(("role", "shard"), None),
            P(("role", "shard"), None),
            P(("role", "shard"), None),
            P("role", "shard"),
            P("role", "shard"),
        ),
        out_specs=(P(("role", "shard"), None), P(("role", "shard"), None), P(("role", "shard"))),
        check_vma=False,
    )
```

profile of v0, /device:TPU:2, one launch (start us, length us, event | category | flops | bytes accessed | tf_op | source)
XLA Modules:
  0.0 1427.1 jit_solution(12608442463665940788)
XLA Ops:
  8.9 44.6 %all-reduce.4.cloned.1.call-done = bf16[2,48,768]{2,1,0:T(8,128)(2,1)} async-done(((bf16[2,48,768]{2,1,0:T(8,128)(2,1)}), bf16[2,48,768]{2,1,0:T(8,128)(2,1)}) %all-reduce.4.cloned.1.call-update) | async-done | bytes 147472 | tf_op jit(solution)/shard_map/psum | solution.py:17
  56.7 12.0 all-to-all-start
  70.3 145.8 %all-gather.6.cloned.1.call-done = bf16[2,3072,768]{2,1,0:T(8,128)(2,1)} async-done(((bf16[2,48,768]{2,1,0:T(8,128)(2,1)}), bf16[2,3072,768]{2,1,0:T(8,128)(2,1)}) %all-gather.6.cloned.1.call-update) | async-done | bytes 9437200 | tf_op jit(solution)/shard_map/all_gather | solution.py:72
  216.1 9.4 fusion.101
  227.1 8.8 all-to-all-start.1
  236.3 182.7 %all-gather = bf16[64,1,768]{2,1,0:T(2,128)(2,1)S(1)} all-gather(bf16[1,1,768]{2,1,0:T(2,128)(2,1)S(1)} %bitcast.172), channel_id=1, replica_groups=mesh['role'=4,'shard'=64] {'shard'}, dimensions={0}, use_global_device_ids=true | all-gather | bytes 99840 | tf_op jit(solution)/shard_map/all_gather | solution.py:96
  420.0 17.8 %gather_fusion = bf16[4096,768]{1,0:T(8,128)(2,1)} fusion(bf16[256,768]{1,0:T(8,128)(2,1)S(1)} %reshape.139, s32[4096]{0:T(1024)S(1)} %broadcast_clamp_fusion), kind=kCustom, calls=%fused_computation | custom fusion | bytes 12599296 | tf_op jit(solution)/shard_map/gather | solution.py:97
  437.8 4.5 fusion.56
  443.9 2.2 copy.52
  448.2 104.8 %all-gather.8.cloned.1.call-done = f32[64,4096]{0,1:T(8,128)} async-done(((f32[64,64]{0,1:T(8,128)}), f32[64,4096]{0,1:T(8,128)}) %all-gather.8.cloned.1.call-update) | async-done | bytes 1048592 | tf_op jit(solution)/shard_map/all_gather | solution.py:103
  555.2 26.4 %while.22 = (s32[]{:T(128)}, f32[8,8,64]{2,1,0:T(8,128)S(1)}, f32[8,8,64]{2,1,0:T(8,128)S(1)}, f32[8,8,4096]{2,1,0:T(8,128)S(1)}, f32[8,8,64]{2,1,0:T(8,128)S(1)}, /*index=5*/s32[]{:T(128)}) while((s32[]{:T(128)}, f32[8,8,64]{2,1,0:T(8,128)S(1)}, f32[8,8,64]{2,1,0:T(8,128)S(1)}, f32[8,8,4096]{2,1,0:T(8,128)S(1)}, ...), condition=%wide.region_16.17_spmd, body=%wide.region_13.16_spmd.sunk | while | flops 16776706 | bytes 419921 | solution.py:111
  555.3 3.2 fusion.108
  558.6 3.2 fusion.108
  561.9 3.2 fusion.108
  565.2 3.2 fusion.108
  568.5 3.2 fusion.108
  571.8 3.2 fusion.108
  575.1 3.2 fusion.108
  578.4 3.2 fusion.108
  583.2 181.4 %psum.15 = f32[64]{0:T(128)S(1)} all-reduce(f32[64]{0:T(128)S(1)} %get-tuple-element.99), channel_id=1, replica_groups=mesh['role'=4,'shard'=64] {'shard'}, use_global_device_ids=true, to_apply=%region_22.23 | all-reduce | flops 64 | bytes 512 | tf_op jit(solution)/shard_map/psum | solution.py:119
  764.5 2.2 copy.54
  766.7 23.3 %while.23 = (s32[]{:T(128)}, f32[8,8,64]{2,1,0:T(8,128)S(1)}, f32[8,8,4096]{2,1,0:T(8,128)S(1)}, f32[8,8,64]{2,1,0:T(8,128)S(1)}, f32[8,8,4096]{2,1,0:T(8,128)S(1)}, /*index=5*/s32[]{:T(128)}) while((s32[]{:T(128)}, f32[8,8,64]{2,1,0:T(8,128)S(1)}, f32[8,8,4096]{2,1,0:T(8,128)S(1)}, f32[8,8,64]{2,1,0:T(8,128)S(1)}, ...), condition=%wide.region_19.20_spmd, body=%wide.region_17.19_spmd.sunk | while | flops 16776706 | bytes 802897 | solution.py:116
  766.8 2.9 fusion.109
  769.7 2.9 fusion.109
  772.6 2.9 fusion.109
  775.5 2.9 fusion.109
  778.4 2.9 fusion.109
  781.4 2.9 fusion.109
  784.3 2.9 fusion.109
  787.2 2.9 fusion.109
  790.1 3.7 fusion.63
  795.1 623.2 %all-reduce.6.cloned.1.call-done = f32[64,768]{1,0:T(8,128)} async-done(((f32[64,768]{1,0:T(8,128)}), f32[64,768]{1,0:T(8,128)}) %all-reduce.6.cloned.1.call-update) | async-done | bytes 196624
  (129 shorter events, 20.4 us)
Async XLA Ops:
  7.2 46.3 %all-reduce.4.cloned.1.call-start = ((), (), s32[]{:S(2)}) async-start(), calls=%async_computation.2 | async-start | bytes 294912 | tf_op jit(solution)/shard_map/psum | solution.py:17
  8.8 207.2 %all-gather.6.cloned.1.call-start = ((), (), s32[]{:S(2)}) async-start(), calls=%async_computation.3 | async-start | bytes 9584640 | tf_op jit(solution)/shard_map/all_gather | solution.py:72
  56.7 170.4 %all-to-all-start = ((bf16[64,1,2]{2,1,0:T(2,128)(2,1)}), bf16[64,1,2]{2,1,0:T(2,128)(2,1)S(1)}, u32[]{:S(2)}, u32[]{:S(2)}) async-start(bf16[64,1,2]{2,1,0:T(2,128)(2,1)} %all_to_all.12), calls=%async_computation | async-start | bytes 65536 | tf_op jit(solution)/shard_map/all_to_all | solution.py:92
  68.8 375.2 %all-gather.10.cloned.1.call-start = ((), (), s32[]{:S(2)}) async-start(), calls=%async_computation.5 | async-start | bytes 2129920 | tf_op jit(solution)/shard_map/all_gather | solution.py:104
  225.6 10.4 copy-start.1
  225.8 10.3 copy-start.3
  225.9 10.4 copy-start.4
  227.1 192.1 %all-to-all-start.1 = ((bf16[64,2,2,768]{3,2,1,0:T(2,128)(2,1)}), bf16[64,2,2,768]{3,2,1,0:T(2,128)(2,1)S(1)}, u32[]{:S(2)}, u32[]{:S(2)}) async-start(bf16[64,2,2,768]{3,2,1,0:T(2,128)(2,1)} %reshape.137), calls=%async_computation.1 | async-start | bytes 786432 | tf_op jit(solution)/shard_map/all_to_all | solution.py:91
  236.0 317.0 %all-gather.8.cloned.1.call-start = ((), (), s32[]{:S(2)}) async-start(), calls=%async_computation.4 | async-start | bytes 2129920 | tf_op jit(solution)/shard_map/all_gather | solution.py:103
  420.0 17.8 %copy-start = (bf16[256,768]{1,0:T(8,128)(2,1)}, bf16[256,768]{1,0:T(8,128)(2,1)S(1)}, u32[]{:S(2)}) copy-start(bf16[256,768]{1,0:T(8,128)(2,1)S(1)} %reshape.139) | copy-start | bytes 1179652
  443.0 321.5 %all-gather.12.cloned.1.call-start = ((), (), s32[]{:S(2)}) async-start(), calls=%async_computation.6 | async-start | bytes 2129920 | tf_op jit(solution)/shard_map/all_gather | solution.py:115
  555.2 26.5 %copy-start.2 = (s32[64,64]{1,0:T(8,128)S(1)}, s32[64,64]{1,0:T(8,128)}, u32[]{:S(2)}) copy-start(s32[64,64]{1,0:T(8,128)} %param.19) | copy-start | bytes 49156
  555.2 27.4 %copy-start.5 = (u32[256]{0:T(256)S(1)}, u32[256]{0:T(256)}, u32[]{:S(2)}) copy-start(u32[256]{0:T(256)} %constant.160) | copy-start | bytes 3076
  582.5 835.8 %all-reduce.6.cloned.1.call-start = ((), (), s32[]{:S(2)}) async-start(), calls=%async_computation.7 | async-start | bytes 393216
Sparse Core Ops, SparseCore 0:
  11.2 42.2 all-reduce.3
  57.7 158.3 all-gather.5
  220.3 116.9 all-gather.9
  443.1 109.8 all-gather.7
  582.6 115.7 all-gather.11
  794.6 623.6 all-reduce.5
where the time goes:
time: 1430 us
  waiting for transfers between devices  918 us (64%)
  blocking collectives  364 us (25%)
  other arithmetic  57.3 us (4%)
  local copies, waits for them, and re-layouts  33.1 us (2%)
  starting transfers between devices  21.3 us (1%)
  matrix products  17.9 us (1%)
  between operations  14.4 us (1%)
    unnamed x7, waiting for transfers between devices  623 us
    all_gather x1, blocking collectives, per_device(): group_queries = lax.all_gather(queries, 'shard', axis=0, tiled=True)  183 us
    psum x1, blocking collectives, per_device(): totals = lax.psum(jnp.sum(terms, 1), 'shard')  181 us
    all_gather x1, waiting for transfers between devices, per_device(): piece = lax.all_gather(current, 'shard', axis=1, tiled=True)  146 us
    all_gather x1, waiting for transfers between devices, per_device(): lax.all_gather(scores, 'shard', axis=1, tiled=True)  105 us
    psum x1, waiting for transfers between devices, broadcast(): return lax.psum(jnp.where(mine, array, jnp.zeros_like(array)), axis)  44.6 us
  transfers between devices with their start and end apart: 8, of which 4 were waited for; matrix products, arithmetic and copies ran while one was open for 3% of the time, Pallas kernels for 0%

commit v1 on v0

v1 whole, which is shorter than its diff:
```python
import math

import jax
import jax.numpy as jnp
import numpy as np
from jax import lax
from jax.experimental import pallas as pl
from jax.experimental.pallas import tpu as pltpu
from jax.sharding import PartitionSpec as P

CAP = 2
EPSILON = 1e-05
LOG_TWO = math.log(2.0)
EMPTY = 1024.0

f32 = jnp.float32
bf16 = jnp.bfloat16
LANES = 128


def params():
    return pltpu.CompilerParams(vmem_limit_bytes=48 * 1024 * 1024)


def contract_last(a, b):
    return lax.dot_general(a, b, (((1,), (1,)), ((), ())), preferred_element_type=f32)


def encode_kernel(x_ref, win_ref, wout_ref, own_ref, far_ref, near_ref):
    rows = own_ref.shape[0]
    for k in (1, 3, 2, 0):
        inner = contract_last(x_ref[pl.ds(k * rows, rows), :], win_ref[...])
        hidden = 0.5 * inner * (1.0 + lax.erf(inner * math.sqrt(0.5)))
        part = jnp.dot(hidden.astype(bf16), wout_ref[...], preferred_element_type=f32)
        if k == 0:
            own_ref[...] = part
        elif k == 2:
            far_ref[...] = part
        else:
            near_ref[pl.ds(k // 2 * rows, rows), :] = part.astype(bf16)


def encode(x4, w_in, w_out, rows):
    width = x4.shape[1]
    return pl.pallas_call(
        encode_kernel,
        out_shape=(
            jax.ShapeDtypeStruct((rows, width), f32),
            jax.ShapeDtypeStruct((rows, width), f32),
            jax.ShapeDtypeStruct((2 * rows, width), bf16),
        ),
        compiler_params=params(),
        name="encode",
    )(x4, w_in, w_out)


def place_kernel(cls_ref, own_ref, near_ref, far_ref, owner_ref, query_ref, out_ref):
    rows, width = cls_ref.shape
    blocks = owner_ref.shape[1]
    shards = out_ref.shape[0] // (2 * CAP + 1)
    resid = (
        cls_ref[...].astype(f32)
        + own_ref[...]
        + near_ref[:rows, :].astype(f32)
        + far_ref[...].astype(f32)
    )
    centred = resid - jnp.mean(resid, -1, keepdims=True)
    variance = jnp.mean(centred * centred, -1, keepdims=True)
    fresh = (centred * lax.rsqrt(variance + EPSILON)).astype(bf16)

    owner = owner_ref[...]
    shard_of = lax.broadcasted_iota(jnp.int32, (shards, blocks), 0)
    onehot = (shard_of == owner).astype(f32)
    before = lax.broadcasted_iota(jnp.int32, (blocks, blocks), 0) < lax.broadcasted_iota(
        jnp.int32, (blocks, blocks), 1
    )
    earlier = jnp.dot(onehot.astype(bf16), before.astype(bf16), preferred_element_type=f32)
    slot = jnp.sum(earlier * onehot, 0, keepdims=True)
    first = owner.astype(f32) * 5.0 + slot * 2.0

    stride = 2 * CAP + 1
    total = out_ref.shape[0]
    row = lax.broadcasted_iota(jnp.int32, (total, blocks), 0).astype(f32)
    even = row == first
    odd = row == first + 1.0
    picks = lax.broadcasted_iota(jnp.int32, (blocks, rows), 1)
    base = lax.broadcasted_iota(jnp.int32, (blocks, rows), 0) * 2
    even_rows = (picks == base).astype(bf16)
    odd_rows = (picks == base + 1).astype(bf16)
    placing = jnp.dot(even.astype(bf16), even_rows, preferred_element_type=f32) + jnp.dot(
        odd.astype(bf16), odd_rows, preferred_element_type=f32
    )
    placed = jnp.dot(placing.astype(bf16), fresh, preferred_element_type=f32)
    filled = jnp.sum(placing, 1, keepdims=True) > 0.5
    place = lax.broadcasted_iota(jnp.int32, (total, 1), 0)
    is_query = lax.rem(place, stride) == stride - 1
    query = query_ref[...].astype(f32)
    out = jnp.where(filled, placed, jnp.where(is_query, query, EMPTY))
    out_ref[...] = out.astype(bf16)


def place(cls_states, own, near, far, owner, query, shards):
    width = cls_states.shape[1]
    return pl.pallas_call(
        place_kernel,
        out_shape=jax.ShapeDtypeStruct((shards * (2 * CAP + 1), width), bf16),
        compiler_params=params(),
        name="place",
    )(cls_states, own, near, far, owner, query)


def score_kernel(recv_ref, stale_ref, idsg_ref, refreshed_ref, packed_ref):
    cache_rows, width = stale_ref.shape
    total = recv_ref.shape[0]
    stride = 2 * CAP + 1
    shards = total // stride
    recv = recv_ref[...]
    at = lax.broadcasted_iota(jnp.int32, (cache_rows, total), 0)
    source = lax.broadcasted_iota(jnp.int32, (cache_rows, total), 1)
    wanted = (at // (2 * CAP)) * stride + lax.rem(at, 2 * CAP)
    arrived = jnp.dot((source == wanted).astype(bf16), recv, preferred_element_type=f32)
    lists = lax.broadcasted_iota(jnp.int32, (shards, total), 0)
    origin = lax.broadcasted_iota(jnp.int32, (shards, total), 1)
    queries = jnp.dot(
        (origin == lists * stride + stride - 1).astype(bf16), recv, preferred_element_type=f32
    ).astype(bf16)
    refreshed = jnp.where(arrived > 0.5 * EMPTY, stale_ref[...].astype(f32), arrived).astype(bf16)
    refreshed_ref[...] = refreshed
    scores = contract_last(queries, refreshed)
    ids = idsg_ref[...]
    lane = lax.broadcasted_iota(jnp.int32, ids.shape, 1)
    low = ids & (LANES - 1)
    picked = jnp.zeros(ids.shape, f32)
    for part in range(cache_rows // LANES):
        here = jnp.take_along_axis(scores[:, part * LANES : (part + 1) * LANES], low, axis=1)
        picked = jnp.where(ids // LANES == part, here, picked)
    packed_ref[...] = jnp.where(lane < LANES // 2, picked, ids.astype(f32))


def score(recv, stale, idsg):
    return pl.pallas_call(
        score_kernel,
        out_shape=(
            jax.ShapeDtypeStruct(stale.shape, bf16),
            jax.ShapeDtypeStruct(idsg.shape, f32),
        ),
        compiler_params=params(),
        name="score",
    )(recv, stale, idsg)


HALF = LANES // 2


def spread_down(row):
    return jnp.broadcast_to(row, (LANES, LANES)).T


def pair_kernel(x_ref, discount_ref, grad_ref, loss_ref, half_s, wide_w, columns, down_s, rank_ref):
    x = x_ref[...]
    n_blocks = x.shape[0] // 2
    count = n_blocks * LANES
    top, low = x[:n_blocks], x[n_blocks:]
    lane = lax.broadcasted_iota(jnp.int32, (n_blocks, LANES), 1)
    left = lane < HALF
    scores = jnp.where(left, top, pltpu.roll(low, HALF, 1))
    gains = jnp.exp2(jnp.where(left, pltpu.roll(top, HALF, 1), low))
    position = lax.broadcasted_iota(jnp.int32, (n_blocks, LANES), 0) * LANES + lane

    ordered = jnp.ones((n_blocks, LANES), f32)
    for level in range(1, 5):
        above = jnp.sum((gains > float(2**level) - 0.5).astype(f32))
        ordered = jnp.where(position.astype(f32) < above, float(2**level), ordered)
    ideal = jnp.sum(ordered * discount_ref[...])

    half_s[:n_blocks] = 0.5 * scores
    half_s[n_blocks:] = 0.5 * scores
    span = n_blocks // 2
    groups = LANES // 8

    def sweep(rows_of, term):
        columns[...] = jnp.zeros_like(columns)

        def block(i, _):
            s_i, w_i = rows_of(i)
            acc = [jnp.zeros((8, LANES), f32) for _ in range(groups)]

            def step(k, both, acc):
                s_k = jnp.broadcast_to(half_s[pl.ds(k, 1), :], (8, LANES))
                w_k = None
                if w_i is not None:
                    w_k = jnp.broadcast_to(wide_w[pl.ds(k, 1), :], (8, LANES))
                column = [jnp.zeros((8, LANES), f32) for _ in range(4)]
                out = []
                for g in range(groups):
                    part = slice(8 * g, 8 * g + 8)
                    value = term(s_i[part], s_k, None if w_i is None else w_i[part], w_k)
                    out.append(acc[g] + value)
                    column[g % 4] = column[g % 4] + value
                if both:
                    whole = (column[0] + column[1]) + (column[2] + column[3])
                    columns[k] = columns[k] + whole
                return out

            acc = step(i, False, acc)
            for d in range(1, span):
                acc = step(i + d, True, acc)
            rank_ref[pl.ds(i, 1), :] = jnp.sum(jnp.concatenate(acc, 0).T, 0, keepdims=True)
            return 0

        lax.fori_loop(0, n_blocks, block, 0)

        def opposite(i, _):
            s_i, w_i = rows_of(i)
            k = i + span
            s_k = jnp.broadcast_to(half_s[pl.ds(k, 1), :], (8, LANES))
            w_k = None
            if w_i is not None:
                w_k = jnp.broadcast_to(wide_w[pl.ds(k, 1), :], (8, LANES))
            values = [
                term(
                    s_i[8 * g : 8 * g + 8],
                    s_k,
                    None if w_i is None else w_i[8 * g : 8 * g + 8],
                    w_k,
                )
                for g in range(groups)
            ]
            columns[k] = columns[k] + sum(values)
            across = jnp.sum(jnp.concatenate(values, 0).T, 0, keepdims=True)
            rank_ref[pl.ds(i, 1), :] = rank_ref[pl.ds(i, 1), :] + across
            return 0

        lax.fori_loop(0, span, opposite, 0)
        folded = jnp.sum(columns[...], 1)
        wrapped = jnp.concatenate((folded[n_blocks:], jnp.zeros((span, LANES), f32)), 0)
        return rank_ref[...] - folded[:n_blocks] - wrapped

    def first_rows(i):
        s_i = spread_down(half_s[pl.ds(i, 1), :])
        down_s[i] = s_i
        return s_i, None

    def rank_term(s_i, s_k, w_i, w_k):
        return jnp.tanh(s_k - s_i)

    def first_or_again(i):
        return first_rows(i)

    tanhs = sweep(first_or_again, rank_term)
    rank = 0.5 + 0.5 * count + 0.5 * tanhs
    logged = jnp.log2(1.0 + rank)
    weight = gains / (ideal * LOG_TWO * (1.0 + rank) * logged * logged)
    loss_ref[...] = jnp.full((1, LANES), 1.0 - jnp.sum(gains / logged) / ideal, f32)
    wide_w[:n_blocks] = 0.25 * weight
    wide_w[n_blocks:] = 0.25 * weight

    def second_rows(i):
        return down_s[i], spread_down(wide_w[pl.ds(i, 1), :])

    def cross_term(s_i, s_k, w_i, w_k):
        t = jnp.tanh(s_k - s_i)
        return (w_k - w_i) * (1.0 - t * t)

    grad = sweep(second_rows, cross_term).astype(bf16).astype(f32)
    grad_ref[:n_blocks] = grad
    grad_ref[n_blocks:] = pltpu.roll(grad, HALF, 1)


def pair(x, discount):
    n_blocks = x.shape[0] // 2
    wide = n_blocks + n_blocks // 2
    return pl.pallas_call(
        pair_kernel,
        out_shape=(
            jax.ShapeDtypeStruct(x.shape, f32),
            jax.ShapeDtypeStruct((1, LANES), f32),
        ),
        scratch_shapes=[
            pltpu.VMEM((2 * n_blocks, LANES), f32),
            pltpu.VMEM((2 * n_blocks, LANES), f32),
            pltpu.VMEM((wide, 8, LANES), f32),
            pltpu.VMEM((n_blocks, LANES, LANES), f32),
            pltpu.VMEM((n_blocks, LANES), f32),
        ],
        compiler_params=params(),
        name="pair",
    )(x, discount)


def share_kernel(grad_ref, idsg_ref, refreshed_ref, out_ref, rows_w):
    lists, cache_rows = rows_w.shape
    for g in range(lists // 8):
        part = slice(8 * g, 8 * g + 8)
        grads = grad_ref[part, :]
        ids = idsg_ref[part, :]
        spots = [
            lax.broadcasted_iota(jnp.int32, (8, LANES), 1) + LANES * p
            for p in range(cache_rows // LANES)
        ]
        acc = [jnp.zeros((8, LANES), f32) for _ in spots]
        for j in range(HALF):
            id_j = jnp.broadcast_to(ids[:, j : j + 1], (8, LANES))
            grad_j = jnp.broadcast_to(grads[:, j : j + 1], (8, LANES))
            acc = [a + jnp.where(id_j == spot, grad_j, 0.0) for a, spot in zip(acc, spots)]
        for p, a in enumerate(acc):
            rows_w[part, p * LANES : (p + 1) * LANES] = a
    weights = rows_w[...]
    high = weights.astype(bf16)
    rest = (weights - high.astype(f32)).astype(bf16)
    refreshed = refreshed_ref[...]
    out_ref[...] = jnp.dot(high, refreshed, preferred_element_type=f32) + jnp.dot(
        rest, refreshed, preferred_element_type=f32
    )


def share(grads, idsg, refreshed):
    return pl.pallas_call(
        share_kernel,
        out_shape=jax.ShapeDtypeStruct((grads.shape[0], refreshed.shape[1]), f32),
        scratch_shapes=[pltpu.VMEM((grads.shape[0], refreshed.shape[0]), f32)],
        compiler_params=params(),
        name="share",
    )(grads, idsg, refreshed)


def turned(places, axis, by):
    pairs = []
    for start in range(math.prod(places)):
        coords = list(np.unravel_index(start, places))
        coords[axis] = (coords[axis] + by) % places[axis]
        pairs.append((start, int(np.ravel_multi_index(coords, places))))
    return pairs


SHARD_GRID = (4, 8, 2)


def collect(block, axis):
    return [block] + [
        lax.ppermute(block, "shard", turned(SHARD_GRID, axis, by))
        for by in range(1, SHARD_GRID[axis])
    ]


def current_projections(trainer_in, trainer_out):
    roles = lax.axis_size("role")
    units = trainer_in.shape[1]
    share_units = units // roles
    role = lax.axis_index("role")
    both = jnp.stack((trainer_in[0], trainer_out[0]), 0)
    parts = [both[:, k * share_units : (k + 1) * share_units] for k in range(roles)]
    mine = parts[roles - 1]
    arrived = [lax.ppermute(parts[k], "role", [(roles - 1, k)]) for k in range(roles - 1)]
    for k in range(roles - 1):
        mine = jnp.where(role == k, arrived[k], mine)
    pair_ = jnp.concatenate(collect(mine, 2), 1)
    half_in, half_out = pair_[0], pair_[1]
    in_y = jnp.concatenate(collect(half_in, 0), 0)
    out_z = jnp.stack(collect(half_out, 1), 0)
    in_zy = jnp.stack(collect(in_y, 1), 0)
    out_yz = jnp.stack(collect(out_z, 0), 0)
    width = in_zy.shape[-1]
    out_zy = out_yz.transpose(1, 0, 2, 3)
    return in_zy.reshape(-1, width), out_zy.reshape(-1, width)


def per_device(
    cls_states, trainer_in, trainer_out, stale_cache, block_owner, queries, neg_ids, grades
):
    shards = lax.axis_size("shard")
    passages, width = cls_states.shape
    near = [(0, 1), (1, 0), (2, 3), (3, 2)]
    across = [(0, 2), (1, 3), (2, 0), (3, 1)]
    diagonal = [(0, 3), (1, 2), (2, 1), (3, 0)]
    x4 = jnp.concatenate(
        [cls_states] + [lax.ppermute(cls_states, "role", p) for p in (near, across, diagonal)], 0
    )
    w_in, w_out = current_projections(trainer_in, trainer_out)
    own, far, to_near = encode(x4, w_in, w_out, passages)
    from_near = lax.ppermute(to_near, "role", near)
    to_far = (far + from_near[passages:].astype(f32)).astype(bf16)
    from_far = lax.ppermute(to_far, "role", across)
    outgoing = place(
        cls_states, own, from_near, from_far, block_owner.reshape(1, -1), queries, shards
    )
    rows = outgoing.shape[0] // shards
    arrived = lax.all_to_all(
        outgoing.reshape(shards, rows, width), "shard", split_axis=0, concat_axis=0, tiled=True
    )
    idsg = jnp.concatenate((neg_ids, grades), 1)
    refreshed, packed = score(arrived.reshape(-1, width), stale_cache, idsg)
    packed = lax.all_to_all(packed, "shard", split_axis=0, concat_axis=0, tiled=True)
    count = shards * neg_ids.shape[1]
    position = np.arange(1, count + 1, dtype=np.float64)
    discount = (1.0 / np.log2(1.0 + position)).astype(np.float32).reshape(-1, LANES)
    grads, loss = pair(packed, jnp.asarray(discount))
    grads = lax.all_to_all(grads, "shard", split_axis=0, concat_axis=0, tiled=True)
    shares = share(grads, idsg, refreshed)
    shares = lax.all_to_all(shares, "shard", split_axis=0, concat_axis=0, tiled=True)
    return refreshed, jnp.sum(shares, 0, keepdims=True), loss[0, :1]


def solution(mesh):
    return jax.shard_map(
        per_device,
        mesh=mesh,
        in_specs=(
            P(("role", "shard"), None),
            P("role", "shard", None),
            P("role", "shard", None),
            P(("role", "shard"), None),
            P(("role", "shard"), None),
            P(("role", "shard"), None),
            P("role", "shard"),
            P("role", "shard"),
        ),
        out_specs=(P(("role", "shard"), None), P(("role", "shard"), None), P(("role", "shard"))),
        check_vma=False,
    )
```

time: 1430 us -> 222 us (0.16)
  waiting for transfers between devices: 918 us -> 64.6 us
  blocking collectives: 364 us -> 49.3 us
  other arithmetic: 57.3 us -> 0.54 us
  starting transfers between devices: 21.3 us -> 65.7 us
  Pallas kernels: 0 us -> 35.3 us
  local copies, waits for them, and re-layouts: 33.1 us -> 5.14 us
  matrix products: 17.9 us -> 0 us
    unnamed x7 -> x0, waiting for transfers between devices: 623 us -> none
    all_gather x4 -> x0, waiting for transfers between devices: 251 us -> none  [the longest x1 146 us: per_device(): piece = lax.all_gather(current, 'shard', axis=1, tiled=True)]
    all_gather x1 -> x0, blocking collectives: 183 us -> none  [per_device(): group_queries = lax.all_gather(queries, 'shard', axis=0, tiled=True)]
    psum x1 -> x0, blocking collectives: 181 us -> none  [per_device(): totals = lax.psum(jnp.sum(terms, 1), 'shard')]
    ppermute x0 -> x29, starting transfers between devices: none -> 56.9 us  [the longest x21 46.1 us: collect(): lax.ppermute(block, 'shard', turned(SHARD_GRID, axis, by))]
    reduce_sum x23 -> x1, other arithmetic: 52 us -> 0.15 us  [per_device(): return (refreshed, jnp.sum(shares, 0, keepdims=True), loss[0, :1])]
    all_to_all x0 -> x3, blocking collectives: none -> 49.3 us  [the longest x1 17.5 us: per_device(): lax.all_to_all(packed, 'shard', split_axis=0, concat_axis=0, tiled=True)]
    psum x1 -> x0, waiting for transfers between devices: 44.6 us -> none  [broadcast(): return lax.psum(jnp.where(mine, array, jnp.zeros_like(array)), axis)]
  transfers between devices with their start and end apart: 8 -> 30, of which waited for: 4 -> 12; matrix products, arithmetic and copies ran while one was open for 3% -> 0% of each run, Pallas kernels for 0% -> 0%
where the time goes in v1:
time: 222 us
  starting transfers between devices  65.7 us (30%)
  waiting for transfers between devices  64.6 us (29%)
  blocking collectives  49.3 us (22%)
  Pallas kernels  35.3 us (16%)
  local copies, waits for them, and re-layouts  5.14 us (2%)
    ppermute x21, starting transfers between devices, collect(): lax.ppermute(block, 'shard', turned(SHARD_GRID, axis, by))  46.1 us
    ppermute x21, waiting for transfers between devices, collect(): lax.ppermute(block, 'shard', turned(SHARD_GRID, axis, by))  32.9 us
    pallas_call x1, Pallas kernels, pair(): pl.pallas_call(pair_kernel, out_shape=(jax.ShapeDtypeStruct(x.shape, f32)...  28.5 us
    all_to_all x1, waiting for transfers between devices, per_device(): lax.all_to_all(outgoing.reshape(shards, rows, width), 'shard', split_axis...  24.3 us
    all_to_all x1, blocking collectives, per_device(): lax.all_to_all(packed, 'shard', split_axis=0, concat_axis=0, tiled=True)  17.5 us
    all_to_all x1, blocking collectives, per_device(): lax.all_to_all(shares, 'shard', split_axis=0, concat_axis=0, tiled=True)  16.2 us
    all_to_all x1, blocking collectives, per_device(): lax.all_to_all(grads, 'shard', split_axis=0, concat_axis=0, tiled=True)  15.7 us
    all_to_all x1, starting transfers between devices, per_device(): lax.all_to_all(outgoing.reshape(shards, rows, width), 'shard', split_axis...  8.8 us
  transfers between devices with their start and end apart: 30, of which 12 were waited for; matrix products, arithmetic and copies ran while one was open for 0% of the time, Pallas kernels for 0%

profile of v1, /device:TPU:2, one launch (start us, length us, event | category | flops | bytes accessed | tf_op | source)
XLA Modules:
  0.0 221.6 jit_solution(2853973651708979659)
XLA Ops:
  5.6 2.2 collective-permute-start.6
  7.9 3.7 %collective-permute-done.6 = bf16[2,12,768]{2,1,0:T(8,128)(2,1)S(1)} collective-permute-done((bf16[2,12,768]{2,1,0:T(8,128)(2,1)S(1)}, bf16[2,12,768]{2,1,0:T(8,128)(2,1)S(1)}, u32[]{:S(2)}, u32[]{:S(2)}) %collective-permute-start.6) | collective-permute-done | bytes 36896 | tf_op jit(solution)/shard_map/ppermute | solution.py:341
  11.5 2.0 collective-permute-start.17
  15.0 3.7 %collective-permute-start.1 = (bf16[128,768]{1,0:T(8,128)(2,1)}, bf16[128,768]{1,0:T(8,128)(2,1)S(1)}, u32[]{:S(2)}, u32[]{:S(2)}) collective-permute-start(bf16[128,768]{1,0:T(8,128)(2,1)} %cls_ref.1), channel_id=1, source_target_pairs={{0,128},{64,192},{128,0},{192,64},{1,129},{65,193},{129,1},{193,65... | collective-permute-start | bytes 589832 | tf_op jit(solution)/shard_map/ppermute | solution.py:377
  18.6 3.3 %collective-permute-start.18 = (bf16[24,768]{1,0:T(8,128)(2,1)S(1)}, bf16[24,768]{1,0:T(8,128)(2,1)S(1)}, u32[]{:S(2)}, u32[]{:S(2)}) collective-permute-start(bf16[24,768]{1,0:T(8,128)(2,1)S(1)} %get-tuple-element.20), channel_id=1, source_target_pairs={{0,4},{1,5},{2,6},{3,7},{4,8},{5,9},{6,10},{7,11},{8,12},{9,13},{1... | collective-permute-start | bytes 110600 | tf_op jit(solution)/shard_map/ppermute | solution.py:341
  21.9 4.0 %collective-permute-start.19 = (bf16[24,768]{1,0:T(8,128)(2,1)S(1)}, bf16[24,768]{1,0:T(8,128)(2,1)S(1)}, u32[]{:S(2)}, u32[]{:S(2)}) collective-permute-start(bf16[24,768]{1,0:T(8,128)(2,1)S(1)} %get-tuple-element.20), channel_id=1, source_target_pairs={{0,6},{1,7},{2,8},{3,9},{4,10},{5,11},{6,12},{7,13},{8,14},{9,15},... | collective-permute-start | bytes 110600 | tf_op jit(solution)/shard_map/ppermute | solution.py:341
  26.5 4.9 %collective-permute-start.21 = (bf16[24,768]{1,0:T(8,128)(2,1)S(1)}, bf16[24,768]{1,0:T(8,128)(2,1)S(1)}, u32[]{:S(2)}, u32[]{:S(2)}) collective-permute-start(bf16[24,768]{1,0:T(8,128)(2,1)S(1)} %get-tuple-element.20), channel_id=1, source_target_pairs={{0,10},{1,11},{2,12},{3,13},{4,14},{5,15},{6,0},{7,1},{8,2},{9,3},... | collective-permute-start | bytes 110600 | tf_op jit(solution)/shard_map/ppermute | solution.py:341
  31.4 2.7 %collective-permute-start.22 = (bf16[24,768]{1,0:T(8,128)(2,1)S(1)}, bf16[24,768]{1,0:T(8,128)(2,1)S(1)}, u32[]{:S(2)}, u32[]{:S(2)}) collective-permute-start(bf16[24,768]{1,0:T(8,128)(2,1)S(1)} %get-tuple-element.20), channel_id=1, source_target_pairs={{0,12},{1,13},{2,14},{3,15},{4,0},{5,1},{6,2},{7,3},{8,4},{9,5},{1... | collective-permute-start | bytes 110600 | tf_op jit(solution)/shard_map/ppermute | solution.py:341
  34.1 2.4 %collective-permute-start.23 = (bf16[24,768]{1,0:T(8,128)(2,1)S(1)}, bf16[24,768]{1,0:T(8,128)(2,1)S(1)}, u32[]{:S(2)}, u32[]{:S(2)}) collective-permute-start(bf16[24,768]{1,0:T(8,128)(2,1)S(1)} %get-tuple-element.20), channel_id=1, source_target_pairs={{0,14},{1,15},{2,0},{3,1},{4,2},{5,3},{6,4},{7,5},{8,6},{9,7},{10,... | collective-permute-start | bytes 110600 | tf_op jit(solution)/shard_map/ppermute | solution.py:341
  38.1 2.9 %collective-permute-start.8 = (bf16[24,768]{1,0:T(8,128)(2,1)S(1)}, bf16[24,768]{1,0:T(8,128)(2,1)S(1)}, u32[]{:S(2)}, u32[]{:S(2)}) collective-permute-start(bf16[24,768]{1,0:T(8,128)(2,1)S(1)} %get-tuple-element.22), channel_id=1, source_target_pairs={{0,32},{1,33},{2,34},{3,35},{4,36},{5,37},{6,38},{7,39},{8,40},{9,... | collective-permute-start | bytes 110600 | tf_op jit(solution)/shard_map/ppermute | solution.py:341
  45.3 2.5 %collective-permute-start.25 = (bf16[8,24,768]{2,1,0:T(8,128)(2,1)S(1)}, bf16[8,24,768]{2,1,0:T(8,128)(2,1)S(1)}, u32[]{:S(2)}, u32[]{:S(2)}) collective-permute-start(bf16[8,24,768]{2,1,0:T(8,128)(2,1)S(1)} %constant_dynamic-update-slice_fusion.2), channel_id=1, source_target_pairs={{0,32},{1,33},{2,34},{3,35},{4,36},{5,37},{6,38},{7,39},{8,40},{9,... | collective-permute-start | bytes 884744 | tf_op jit(solution)/shard_map/ppermute | solution.py:341
  49.4 3.1 %collective-permute-start.11 = (bf16[96,768]{1,0:T(8,128)(2,1)S(1)}, bf16[96,768]{1,0:T(8,128)(2,1)S(1)}, u32[]{:S(2)}, u32[]{:S(2)}) collective-permute-start(bf16[96,768]{1,0:T(8,128)(2,1)S(1)} %pad_maximum_fusion.1), channel_id=1, source_target_pairs={{0,4},{1,5},{2,6},{3,7},{4,8},{5,9},{6,10},{7,11},{8,12},{9,13},{1... | collective-permute-start | bytes 442376 | tf_op jit(solution)/shard_map/ppermute | solution.py:341
  52.5 2.8 %collective-permute-start.12 = (bf16[96,768]{1,0:T(8,128)(2,1)S(1)}, bf16[96,768]{1,0:T(8,128)(2,1)S(1)}, u32[]{:S(2)}, u32[]{:S(2)}) collective-permute-start(bf16[96,768]{1,0:T(8,128)(2,1)S(1)} %pad_maximum_fusion.1), channel_id=1, source_target_pairs={{0,6},{1,7},{2,8},{3,9},{4,10},{5,11},{6,12},{7,13},{8,14},{9,15},... | collective-permute-start | bytes 442376 | tf_op jit(solution)/shard_map/ppermute | solution.py:341
  55.3 8.8 %collective-permute-done.11 = bf16[96,768]{1,0:T(8,128)(2,1)S(1)} collective-permute-done((bf16[96,768]{1,0:T(8,128)(2,1)S(1)}, bf16[96,768]{1,0:T(8,128)(2,1)S(1)}, u32[]{:S(2)}, u32[]{:S(2)}) %collective-permute-start.11) | collective-permute-done | bytes 147488 | tf_op jit(solution)/shard_map/ppermute | solution.py:341
  64.1 4.7 %collective-permute-start.13 = (bf16[96,768]{1,0:T(8,128)(2,1)S(1)}, bf16[96,768]{1,0:T(8,128)(2,1)S(1)}, u32[]{:S(2)}, u32[]{:S(2)}) collective-permute-start(bf16[96,768]{1,0:T(8,128)(2,1)S(1)} %pad_maximum_fusion.1), channel_id=1, source_target_pairs={{0,8},{1,9},{2,10},{3,11},{4,12},{5,13},{6,14},{7,15},{8,0},{9,1},... | collective-permute-start | bytes 442376 | tf_op jit(solution)/shard_map/ppermute | solution.py:341
  68.9 2.4 %collective-permute-done.12 = bf16[96,768]{1,0:T(8,128)(2,1)S(1)} collective-permute-done((bf16[96,768]{1,0:T(8,128)(2,1)S(1)}, bf16[96,768]{1,0:T(8,128)(2,1)S(1)}, u32[]{:S(2)}, u32[]{:S(2)}) %collective-permute-start.12) | collective-permute-done | bytes 147488 | tf_op jit(solution)/shard_map/ppermute | solution.py:341
  71.2 1.9 collective-permute-start.14
  73.1 2.9 %collective-permute-done.13 = bf16[96,768]{1,0:T(8,128)(2,1)S(1)} collective-permute-done((bf16[96,768]{1,0:T(8,128)(2,1)S(1)}, bf16[96,768]{1,0:T(8,128)(2,1)S(1)}, u32[]{:S(2)}, u32[]{:S(2)}) %collective-permute-start.13) | collective-permute-done | bytes 147488 | tf_op jit(solution)/shard_map/ppermute | solution.py:341
  76.1 8.9 %collective-permute-done.14 = bf16[96,768]{1,0:T(8,128)(2,1)S(1)} collective-permute-done((bf16[96,768]{1,0:T(8,128)(2,1)S(1)}, bf16[96,768]{1,0:T(8,128)(2,1)S(1)}, u32[]{:S(2)}, u32[]{:S(2)}) %collective-permute-start.14) | collective-permute-done | bytes 147488 | tf_op jit(solution)/shard_map/ppermute | solution.py:341
  85.0 3.3 %collective-permute-done.15 = bf16[96,768]{1,0:T(8,128)(2,1)S(1)} collective-permute-done((bf16[96,768]{1,0:T(8,128)(2,1)S(1)}, bf16[96,768]{1,0:T(8,128)(2,1)S(1)}, u32[]{:S(2)}, u32[]{:S(2)}) %collective-permute-start.15) | collective-permute-done | bytes 147488 | tf_op jit(solution)/shard_map/ppermute | solution.py:341
  88.3 1.8 collective-permute-done.16
  90.5 2.9 %encode.1 = (f32[128,768]{1,0:T(8,128)S(1)}, f32[128,768]{1,0:T(8,128)S(1)}, bf16[256,768]{1,0:T(8,128)(2,1)S(1)}) custom-call(bf16[512,768]{1,0:T(8,128)(2,1)S(1)} %pad_maximum_fusion.x_ref, bf16[768,768]{1,0:T(8,128)(2,1)S(1)} %bitcast.55, bf16[768,768]{1,0:T(8,128)(2,1)S(1)} %bitcast.54), custom_call_target="tpu_custom_call" | custom-call | tf_op jit(solution)/shard_map/encode/pallas_call | solution.py:45
  93.4 1.7 collective-permute-done.27.near_ref
  95.2 2.9 %collective-permute-start.28 = (bf16[128,768]{1,0:T(8,128)(2,1)S(1)}, bf16[128,768]{1,0:T(8,128)(2,1)S(1)}, u32[]{:S(2)}, u32[]{:S(2)}) collective-permute-start(bf16[128,768]{1,0:T(8,128)(2,1)S(1)} %add_convert_fusion), channel_id=1, source_target_pairs={{0,128},{64,192},{128,0},{192,64},{1,129},{65,193},{129,1},{193,65... | collective-permute-start | bytes 589832 | tf_op jit(solution)/shard_map/ppermute | solution.py:383
  98.1 5.2 %collective-permute-done.28.far_ref = bf16[128,768]{1,0:T(8,128)(2,1)S(1)} collective-permute-done((bf16[128,768]{1,0:T(8,128)(2,1)S(1)}, bf16[128,768]{1,0:T(8,128)(2,1)S(1)}, u32[]{:S(2)}, u32[]{:S(2)}) %collective-permute-start.28) | collective-permute-done | bytes 196640 | tf_op jit(solution)/shard_map/ppermute | solution.py:383
  105.0 8.8 %all-to-all-start = ((bf16[64,5,768]{2,1,0:T(8,128)(2,1)}), bf16[64,5,768]{2,1,0:T(8,128)(2,1)S(1)}, u32[]{:S(2)}, u32[]{:S(2)}) async-start(bf16[64,5,768]{2,1,0:T(8,128)(2,1)} %reshape.30), calls=%async_computation | async-start | bytes 1572864 | tf_op jit(solution)/shard_map/all_to_all | solution.py:388
  114.0 24.3 %all-to-all-done = bf16[64,5,768]{2,1,0:T(8,128)(2,1)S(1)} async-done(((bf16[64,5,768]{2,1,0:T(8,128)(2,1)}), bf16[64,5,768]{2,1,0:T(8,128)(2,1)S(1)}, u32[]{:S(2)}, u32[]{:S(2)}) %all-to-all-start) | async-done | bytes 491552 | tf_op jit(solution)/shard_map/all_to_all | solution.py:388
  139.8 17.5 %all_to_all.36 = f32[64,1,128]{2,1,0:T(1,128)S(1)} all-to-all(f32[64,1,128]{2,1,0:T(1,128)S(1)} %bitcast.60), channel_id=1, replica_groups=mesh['role'=4,'shard'=64] {'shard'}, dimensions={0} | all-to-all | bytes 65536 | tf_op jit(solution)/shard_map/all_to_all | solution.py:393
  157.3 28.5 %pair.1 = (f32[64,128]{1,0:T(8,128)S(1)}, f32[1,128]{1,0:T(1,128)}) custom-call(f32[64,128]{1,0:T(8,128)S(1)} %bitcast.58, f32[32,128]{1,0:T(8,128)S(1)} %copy-done.3), custom_call_target="tpu_custom_call" | custom-call | tf_op jit(solution)/shard_map/pair/pallas_call | solution.py:273
  185.8 15.7 %all_to_all.37 = f32[64,1,128]{2,1,0:T(1,128)S(1)} all-to-all(f32[64,1,128]{2,1,0:T(1,128)S(1)} %bitcast.59), channel_id=1, replica_groups=mesh['role'=4,'shard'=64] {'shard'}, dimensions={0} | all-to-all | bytes 65536 | tf_op jit(solution)/shard_map/all_to_all | solution.py:398
  202.5 2.0 share.1
  204.7 16.2 %all_to_all.38 = f32[64,1,768]{2,1,0:T(1,128)S(1)} all-to-all(f32[64,1,768]{2,1,0:T(1,128)S(1)} %copy.17), channel_id=1, replica_groups=mesh['role'=4,'shard'=64] {'shard'}, dimensions={0} | all-to-all | bytes 393216 | tf_op jit(solution)/shard_map/all_to_all | solution.py:400
  (83 shorter events, 20.2 us)
Async XLA Ops:
  0.6 41.8 %copy-start = (bf16[128,768]{1,0:T(8,128)(2,1)S(1)}, bf16[128,768]{1,0:T(8,128)(2,1)}, u32[]{:S(2)}) copy-start(bf16[128,768]{1,0:T(8,128)(2,1)} %cls_ref.1) | copy-start | bytes 589828
  2.5 3.1 %collective-permute-start.3 = (bf16[2,12,768]{2,1,0:T(8,128)(2,1)S(1)}, bf16[2,12,768]{2,1,0:T(8,128)(2,1)S(1)}, u32[]{:S(2)}, u32[]{:S(2)}) collective-permute-start(bf16[2,12,768]{2,1,0:T(8,128)(2,1)S(1)} %get-tuple-element.19), channel_id=1, source_target_pairs={{192,128},{193,129},{194,130},{195,131},{196,132},{197,133},{198,1... | collective-permute-start | bytes 110600 | tf_op jit(solution)/shard_map/ppermute | solution.py:354
  3.8 1.8 collective-permute-start.4
  4.5 1.2 collective-permute-start.5
  5.6 5.9 %collective-permute-start.6 = (bf16[2,12,768]{2,1,0:T(8,128)(2,1)S(1)}, bf16[2,12,768]{2,1,0:T(8,128)(2,1)S(1)}, u32[]{:S(2)}, u32[]{:S(2)}) collective-permute-start(bf16[2,12,768]{2,1,0:T(8,128)(2,1)S(1)} %fusion.1), channel_id=1, source_target_pairs={{0,1},{1,0},{2,3},{3,2},{4,5},{5,4},{6,7},{7,6},{8,9},{9,8},{10,11... | collective-permute-start | bytes 110600 | tf_op jit(solution)/shard_map/ppermute | solution.py:341
  11.5 14.4 %collective-permute-start.17 = (bf16[24,768]{1,0:T(8,128)(2,1)S(1)}, bf16[24,768]{1,0:T(8,128)(2,1)S(1)}, u32[]{:S(2)}, u32[]{:S(2)}) collective-permute-start(bf16[24,768]{1,0:T(8,128)(2,1)S(1)} %get-tuple-element.20), channel_id=1, source_target_pairs={{0,2},{1,3},{2,4},{3,5},{4,6},{5,7},{6,8},{7,9},{8,10},{9,11},{10,... | collective-permute-start | bytes 110600 | tf_op jit(solution)/shard_map/ppermute | solution.py:341
  13.5 31.8 %collective-permute-start = (bf16[128,768]{1,0:T(8,128)(2,1)}, bf16[128,768]{1,0:T(8,128)(2,1)S(1)}, u32[]{:S(2)}, u32[]{:S(2)}) collective-permute-start(bf16[128,768]{1,0:T(8,128)(2,1)} %cls_ref.1), channel_id=1, source_target_pairs={{0,64},{64,0},{128,192},{192,128},{1,65},{65,1},{129,193},{193,129... | collective-permute-start | bytes 589832 | tf_op jit(solution)/shard_map/ppermute | solution.py:377
  15.0 32.8 %collective-permute-start.1 = (bf16[128,768]{1,0:T(8,128)(2,1)}, bf16[128,768]{1,0:T(8,128)(2,1)S(1)}, u32[]{:S(2)}, u32[]{:S(2)}) collective-permute-start(bf16[128,768]{1,0:T(8,128)(2,1)} %cls_ref.1), channel_id=1, source_target_pairs={{0,128},{64,192},{128,0},{192,64},{1,129},{65,193},{129,1},{193,65... | collective-permute-start | bytes 589832 | tf_op jit(solution)/shard_map/ppermute | solution.py:377
  18.6 7.9 %collective-permute-start.18 = (bf16[24,768]{1,0:T(8,128)(2,1)S(1)}, bf16[24,768]{1,0:T(8,128)(2,1)S(1)}, u32[]{:S(2)}, u32[]{:S(2)}) collective-permute-start(bf16[24,768]{1,0:T(8,128)(2,1)S(1)} %get-tuple-element.20), channel_id=1, source_target_pairs={{0,4},{1,5},{2,6},{3,7},{4,8},{5,9},{6,10},{7,11},{8,12},{9,13},{1... | collective-permute-start | bytes 110600 | tf_op jit(solution)/shard_map/ppermute | solution.py:341
  21.9 9.5 %collective-permute-start.19 = (bf16[24,768]{1,0:T(8,128)(2,1)S(1)}, bf16[24,768]{1,0:T(8,128)(2,1)S(1)}, u32[]{:S(2)}, u32[]{:S(2)}) collective-permute-start(bf16[24,768]{1,0:T(8,128)(2,1)S(1)} %get-tuple-element.20), channel_id=1, source_target_pairs={{0,6},{1,7},{2,8},{3,9},{4,10},{5,11},{6,12},{7,13},{8,14},{9,15},... | collective-permute-start | bytes 110600 | tf_op jit(solution)/shard_map/ppermute | solution.py:341
  25.9 8.2 %collective-permute-start.20 = (bf16[24,768]{1,0:T(8,128)(2,1)S(1)}, bf16[24,768]{1,0:T(8,128)(2,1)S(1)}, u32[]{:S(2)}, u32[]{:S(2)}) collective-permute-start(bf16[24,768]{1,0:T(8,128)(2,1)S(1)} %get-tuple-element.20), channel_id=1, source_target_pairs={{0,8},{1,9},{2,10},{3,11},{4,12},{5,13},{6,14},{7,15},{8,0},{9,1},... | collective-permute-start | bytes 110600 | tf_op jit(solution)/shard_map/ppermute | solution.py:341
  26.5 10.1 %collective-permute-start.21 = (bf16[24,768]{1,0:T(8,128)(2,1)S(1)}, bf16[24,768]{1,0:T(8,128)(2,1)S(1)}, u32[]{:S(2)}, u32[]{:S(2)}) collective-permute-start(bf16[24,768]{1,0:T(8,128)(2,1)S(1)} %get-tuple-element.20), channel_id=1, source_target_pairs={{0,10},{1,11},{2,12},{3,13},{4,14},{5,15},{6,0},{7,1},{8,2},{9,3},... | collective-permute-start | bytes 110600 | tf_op jit(solution)/shard_map/ppermute | solution.py:341
  31.4 6.7 %collective-permute-start.22 = (bf16[24,768]{1,0:T(8,128)(2,1)S(1)}, bf16[24,768]{1,0:T(8,128)(2,1)S(1)}, u32[]{:S(2)}, u32[]{:S(2)}) collective-permute-start(bf16[24,768]{1,0:T(8,128)(2,1)S(1)} %get-tuple-element.20), channel_id=1, source_target_pairs={{0,12},{1,13},{2,14},{3,15},{4,0},{5,1},{6,2},{7,3},{8,4},{9,5},{1... | collective-permute-start | bytes 110600 | tf_op jit(solution)/shard_map/ppermute | solution.py:341
  34.1 6.9 %collective-permute-start.23 = (bf16[24,768]{1,0:T(8,128)(2,1)S(1)}, bf16[24,768]{1,0:T(8,128)(2,1)S(1)}, u32[]{:S(2)}, u32[]{:S(2)}) collective-permute-start(bf16[24,768]{1,0:T(8,128)(2,1)S(1)} %get-tuple-element.20), channel_id=1, source_target_pairs={{0,14},{1,15},{2,0},{3,1},{4,2},{5,3},{6,4},{7,5},{8,6},{9,7},{10,... | collective-permute-start | bytes 110600 | tf_op jit(solution)/shard_map/ppermute | solution.py:341
  36.5 5.8 %collective-permute-start.7 = (bf16[24,768]{1,0:T(8,128)(2,1)S(1)}, bf16[24,768]{1,0:T(8,128)(2,1)S(1)}, u32[]{:S(2)}, u32[]{:S(2)}) collective-permute-start(bf16[24,768]{1,0:T(8,128)(2,1)S(1)} %get-tuple-element.22), channel_id=1, source_target_pairs={{0,16},{1,17},{2,18},{3,19},{4,20},{5,21},{6,22},{7,23},{8,24},{9,... | collective-permute-start | bytes 110600 | tf_op jit(solution)/shard_map/ppermute | solution.py:341
  38.1 5.5 %collective-permute-start.8 = (bf16[24,768]{1,0:T(8,128)(2,1)S(1)}, bf16[24,768]{1,0:T(8,128)(2,1)S(1)}, u32[]{:S(2)}, u32[]{:S(2)}) collective-permute-start(bf16[24,768]{1,0:T(8,128)(2,1)S(1)} %get-tuple-element.22), channel_id=1, source_target_pairs={{0,32},{1,33},{2,34},{3,35},{4,36},{5,37},{6,38},{7,39},{8,40},{9,... | collective-permute-start | bytes 110600 | tf_op jit(solution)/shard_map/ppermute | solution.py:341
  41.0 4.2 %collective-permute-start.9 = (bf16[24,768]{1,0:T(8,128)(2,1)S(1)}, bf16[24,768]{1,0:T(8,128)(2,1)S(1)}, u32[]{:S(2)}, u32[]{:S(2)}) collective-permute-start(bf16[24,768]{1,0:T(8,128)(2,1)S(1)} %get-tuple-element.22), channel_id=1, source_target_pairs={{0,48},{1,49},{2,50},{3,51},{4,52},{5,53},{6,54},{7,55},{8,56},{9,... | collective-permute-start | bytes 110600 | tf_op jit(solution)/shard_map/ppermute | solution.py:341
  42.4 7.0 %collective-permute-start.2 = (bf16[128,768]{1,0:T(8,128)(2,1)S(1)}, bf16[128,768]{1,0:T(8,128)(2,1)S(1)}, u32[]{:S(2)}, u32[]{:S(2)}) collective-permute-start(bf16[128,768]{1,0:T(8,128)(2,1)S(1)} %copy-done), channel_id=1, source_target_pairs={{0,192},{64,128},{128,64},{192,0},{1,193},{65,129},{129,65},{193,1... | collective-permute-start | bytes 589832 | tf_op jit(solution)/shard_map/ppermute | solution.py:377
  43.6 46.5 %collective-permute-start.24 = (bf16[8,24,768]{2,1,0:T(8,128)(2,1)S(1)}, bf16[8,24,768]{2,1,0:T(8,128)(2,1)S(1)}, u32[]{:S(2)}, u32[]{:S(2)}) collective-permute-start(bf16[8,24,768]{2,1,0:T(8,128)(2,1)S(1)} %constant_dynamic-update-slice_fusion.2), channel_id=1, source_target_pairs={{0,16},{1,17},{2,18},{3,19},{4,20},{5,21},{6,22},{7,23},{8,24},{9,... | collective-permute-start | bytes 884744 | tf_op jit(solution)/shard_map/ppermute | solution.py:341
  45.2 7.3 %collective-permute-start.10 = (bf16[96,768]{1,0:T(8,128)(2,1)S(1)}, bf16[96,768]{1,0:T(8,128)(2,1)S(1)}, u32[]{:S(2)}, u32[]{:S(2)}) collective-permute-start(bf16[96,768]{1,0:T(8,128)(2,1)S(1)} %pad_maximum_fusion.1), channel_id=1, source_target_pairs={{0,2},{1,3},{2,4},{3,5},{4,6},{5,7},{6,8},{7,9},{8,10},{9,11},{10,... | collective-permute-start | bytes 442376 | tf_op jit(solution)/shard_map/ppermute | solution.py:341
  45.3 44.8 %collective-permute-start.25 = (bf16[8,24,768]{2,1,0:T(8,128)(2,1)S(1)}, bf16[8,24,768]{2,1,0:T(8,128)(2,1)S(1)}, u32[]{:S(2)}, u32[]{:S(2)}) collective-permute-start(bf16[8,24,768]{2,1,0:T(8,128)(2,1)S(1)} %constant_dynamic-update-slice_fusion.2), channel_id=1, source_target_pairs={{0,32},{1,33},{2,34},{3,35},{4,36},{5,37},{6,38},{7,39},{8,40},{9,... | collective-permute-start | bytes 884744 | tf_op jit(solution)/shard_map/ppermute | solution.py:341
  47.8 42.4 %collective-permute-start.26 = (bf16[8,24,768]{2,1,0:T(8,128)(2,1)S(1)}, bf16[8,24,768]{2,1,0:T(8,128)(2,1)S(1)}, u32[]{:S(2)}, u32[]{:S(2)}) collective-permute-start(bf16[8,24,768]{2,1,0:T(8,128)(2,1)S(1)} %constant_dynamic-update-slice_fusion.2), channel_id=1, source_target_pairs={{0,48},{1,49},{2,50},{3,51},{4,52},{5,53},{6,54},{7,55},{8,56},{9,... | collective-permute-start | bytes 884744 | tf_op jit(solution)/shard_map/ppermute | solution.py:341
  49.4 14.7 %collective-permute-start.11 = (bf16[96,768]{1,0:T(8,128)(2,1)S(1)}, bf16[96,768]{1,0:T(8,128)(2,1)S(1)}, u32[]{:S(2)}, u32[]{:S(2)}) collective-permute-start(bf16[96,768]{1,0:T(8,128)(2,1)S(1)} %pad_maximum_fusion.1), channel_id=1, source_target_pairs={{0,4},{1,5},{2,6},{3,7},{4,8},{5,9},{6,10},{7,11},{8,12},{9,13},{1... | collective-permute-start | bytes 442376 | tf_op jit(solution)/shard_map/ppermute | solution.py:341
  52.5 18.7 %collective-permute-start.12 = (bf16[96,768]{1,0:T(8,128)(2,1)S(1)}, bf16[96,768]{1,0:T(8,128)(2,1)S(1)}, u32[]{:S(2)}, u32[]{:S(2)}) collective-permute-start(bf16[96,768]{1,0:T(8,128)(2,1)S(1)} %pad_maximum_fusion.1), channel_id=1, source_target_pairs={{0,6},{1,7},{2,8},{3,9},{4,10},{5,11},{6,12},{7,13},{8,14},{9,15},... | collective-permute-start | bytes 442376 | tf_op jit(solution)/shard_map/ppermute | solution.py:341
  64.1 11.9 %collective-permute-start.13 = (bf16[96,768]{1,0:T(8,128)(2,1)S(1)}, bf16[96,768]{1,0:T(8,128)(2,1)S(1)}, u32[]{:S(2)}, u32[]{:S(2)}) collective-permute-start(bf16[96,768]{1,0:T(8,128)(2,1)S(1)} %pad_maximum_fusion.1), channel_id=1, source_target_pairs={{0,8},{1,9},{2,10},{3,11},{4,12},{5,13},{6,14},{7,15},{8,0},{9,1},... | collective-permute-start | bytes 442376 | tf_op jit(solution)/shard_map/ppermute | solution.py:341
  71.2 13.7 %collective-permute-start.14 = (bf16[96,768]{1,0:T(8,128)(2,1)S(1)}, bf16[96,768]{1,0:T(8,128)(2,1)S(1)}, u32[]{:S(2)}, u32[]{:S(2)}) collective-permute-start(bf16[96,768]{1,0:T(8,128)(2,1)S(1)} %pad_maximum_fusion.1), channel_id=1, source_target_pairs={{0,10},{1,11},{2,12},{3,13},{4,14},{5,15},{6,0},{7,1},{8,2},{9,3},... | collective-permute-start | bytes 442376 | tf_op jit(solution)/shard_map/ppermute | solution.py:341
  76.0 12.3 %collective-permute-start.15 = (bf16[96,768]{1,0:T(8,128)(2,1)S(1)}, bf16[96,768]{1,0:T(8,128)(2,1)S(1)}, u32[]{:S(2)}, u32[]{:S(2)}) collective-permute-start(bf16[96,768]{1,0:T(8,128)(2,1)S(1)} %pad_maximum_fusion.1), channel_id=1, source_target_pairs={{0,12},{1,13},{2,14},{3,15},{4,0},{5,1},{6,2},{7,3},{8,4},{9,5},{1... | collective-permute-start | bytes 442376 | tf_op jit(solution)/shard_map/ppermute | solution.py:341
  85.0 5.1 %collective-permute-start.16 = (bf16[96,768]{1,0:T(8,128)(2,1)S(1)}, bf16[96,768]{1,0:T(8,128)(2,1)S(1)}, u32[]{:S(2)}, u32[]{:S(2)}) collective-permute-start(bf16[96,768]{1,0:T(8,128)(2,1)S(1)} %pad_maximum_fusion.1), channel_id=1, source_target_pairs={{0,14},{1,15},{2,0},{3,1},{4,2},{5,3},{6,4},{7,5},{8,6},{9,7},{10,... | collective-permute-start | bytes 442376 | tf_op jit(solution)/shard_map/ppermute | solution.py:341
  93.3 1.8 collective-permute-start.27
  95.2 8.1 %collective-permute-start.28 = (bf16[128,768]{1,0:T(8,128)(2,1)S(1)}, bf16[128,768]{1,0:T(8,128)(2,1)S(1)}, u32[]{:S(2)}, u32[]{:S(2)}) collective-permute-start(bf16[128,768]{1,0:T(8,128)(2,1)S(1)} %add_convert_fusion), channel_id=1, source_target_pairs={{0,128},{64,192},{128,0},{192,64},{1,129},{65,193},{129,1},{193,65... | collective-permute-start | bytes 589832 | tf_op jit(solution)/shard_map/ppermute | solution.py:383
  105.0 33.2 %all-to-all-start = ((bf16[64,5,768]{2,1,0:T(8,128)(2,1)}), bf16[64,5,768]{2,1,0:T(8,128)(2,1)S(1)}, u32[]{:S(2)}, u32[]{:S(2)}) async-start(bf16[64,5,768]{2,1,0:T(8,128)(2,1)} %reshape.30), calls=%async_computation | async-start | bytes 1572864 | tf_op jit(solution)/shard_map/all_to_all | solution.py:388
  113.9 43.4 %copy-start.3 = (f32[32,128]{1,0:T(8,128)S(1)}, f32[32,128]{1,0:T(8,128)}, u32[]{:S(2)}) copy-start(f32[32,128]{1,0:T(8,128)} %constant.16.clone.discount_ref) | copy-start | bytes 49156
  (6 other events, 80.0 us)

commit v2 on v1

v2 whole, which is shorter than its diff:
```python
import math

import jax
import jax.numpy as jnp
import numpy as np
from jax import lax
from jax.experimental import pallas as pl
from jax.experimental.pallas import tpu as pltpu
from jax.sharding import PartitionSpec as P

CAP = 2
EPSILON = 1e-05
LOG_TWO = math.log(2.0)
EMPTY = 1024.0

f32 = jnp.float32
bf16 = jnp.bfloat16
LANES = 128


def params():
    return pltpu.CompilerParams(vmem_limit_bytes=48 * 1024 * 1024)


def contract_last(a, b):
    return lax.dot_general(a, b, (((1,), (1,)), ((), ())), preferred_element_type=f32)


def encode_kernel(x_ref, w_ref, own_ref, far_ref, near_ref):
    rows, width = own_ref.shape
    for k in (1, 3, 2, 0):
        inner = contract_last(x_ref[pl.ds(k * rows, rows), :], w_ref[:, :width])
        hidden = 0.5 * inner * (1.0 + lax.erf(inner * math.sqrt(0.5)))
        part = jnp.dot(hidden.astype(bf16), w_ref[:, width:], preferred_element_type=f32)
        if k == 0:
            own_ref[...] = part
        elif k == 2:
            far_ref[...] = part
        else:
            near_ref[pl.ds(k // 2 * rows, rows), :] = part.astype(bf16)


def encode(x4, projections, rows):
    width = x4.shape[1]
    return pl.pallas_call(
        encode_kernel,
        out_shape=(
            jax.ShapeDtypeStruct((rows, width), f32),
            jax.ShapeDtypeStruct((rows, width), f32),
            jax.ShapeDtypeStruct((2 * rows, width), bf16),
        ),
        compiler_params=params(),
        name="encode",
    )(x4, projections)


ROWS = 32


def place_kernel(cls_ref, own_ref, near_ref, far_ref, owner_ref, query_ref, out_ref):
    rows, width = cls_ref.shape
    blocks = owner_ref.shape[1]
    total = out_ref.shape[0]
    shards = total // ROWS
    chunks = width // LANES
    resid = (
        cls_ref[...].astype(f32)
        + own_ref[...]
        + near_ref[:rows, :].astype(f32)
        + far_ref[...].astype(f32)
    )
    centred = resid - jnp.mean(resid, -1, keepdims=True)
    variance = jnp.mean(centred * centred, -1, keepdims=True)
    fresh = (centred * lax.rsqrt(variance + EPSILON)).astype(bf16)

    owner = owner_ref[...]
    shard_of = lax.broadcasted_iota(jnp.int32, (shards, blocks), 0)
    onehot = (shard_of == owner).astype(f32)
    before = lax.broadcasted_iota(jnp.int32, (blocks, blocks), 0) < lax.broadcasted_iota(
        jnp.int32, (blocks, blocks), 1
    )
    earlier = jnp.dot(onehot.astype(bf16), before.astype(bf16), preferred_element_type=f32)
    slot = jnp.sum(earlier * onehot, 0, keepdims=True)
    passage = lax.broadcasted_iota(jnp.int32, (blocks, rows), 1)
    block = lax.broadcasted_iota(jnp.int32, (blocks, rows), 0)
    widen = (passage // 2 == block).astype(bf16)
    both = jnp.concatenate(
        (jnp.broadcast_to(owner.astype(f32), (8, blocks)), jnp.broadcast_to(slot, (8, blocks))), 0
    )
    both = jnp.dot(both.astype(bf16), widen, preferred_element_type=f32)
    parity = lax.broadcasted_iota(jnp.int32, (1, rows), 1) & 1
    target = both[0:1] * ROWS + (both[8:9] * 2.0 + parity.astype(f32)) * chunks

    row = lax.broadcasted_iota(jnp.int32, (total, rows), 0).astype(f32)
    placed = jnp.zeros((total, LANES), f32)
    taken = jnp.zeros((total, rows), f32)
    for j in range(chunks):
        onto = (row == target + float(j)).astype(f32)
        taken = taken + onto
        placed = placed + jnp.dot(
            onto.astype(bf16), fresh[:, j * LANES : (j + 1) * LANES], preferred_element_type=f32
        )
    filled = jnp.dot(taken.astype(bf16), jnp.ones((rows, LANES), bf16), preferred_element_type=f32)
    rest = jnp.broadcast_to(query_ref[...].astype(f32)[None], (shards, ROWS, LANES))
    out_ref[...] = jnp.where(filled > 0.5, placed, rest.reshape(total, LANES)).astype(bf16)


def place(cls_states, own, near, far, owner, query, shards):
    return pl.pallas_call(
        place_kernel,
        out_shape=jax.ShapeDtypeStruct((shards * ROWS, LANES), bf16),
        compiler_params=params(),
        name="place",
    )(cls_states, own, near, far, owner, query)


def score_kernel(recv_ref, stale_ref, idsg_ref, refreshed_ref, packed_ref, recv_s, arrived_s):
    cache_rows, width = stale_ref.shape
    shards = recv_ref.shape[0] // ROWS
    chunks = width // LANES
    per_shard = cache_rows // shards
    recv_s[...] = recv_ref[...].astype(f32)
    queries = []
    for j in range(chunks):
        for c in range(per_shard):
            arrived_s[j, pl.ds(c, shards, stride=per_shard), :] = recv_s[
                pl.ds(c * chunks + j, shards, stride=ROWS), :
            ]
        queries.append(recv_s[pl.ds(per_shard * chunks + j, shards, stride=ROWS), :])
    queries = jnp.concatenate(queries, 1).astype(bf16)
    arrived = jnp.concatenate([arrived_s[j] for j in range(chunks)], 1)
    refreshed = jnp.where(arrived > 0.5 * EMPTY, stale_ref[...].astype(f32), arrived).astype(bf16)
    refreshed_ref[...] = refreshed
    scores = contract_last(queries, refreshed)
    ids = idsg_ref[...]
    lane = lax.broadcasted_iota(jnp.int32, ids.shape, 1)
    low = ids & (LANES - 1)
    picked = jnp.zeros(ids.shape, f32)
    for part in range(cache_rows // LANES):
        here = jnp.take_along_axis(scores[:, part * LANES : (part + 1) * LANES], low, axis=1)
        picked = jnp.where(ids // LANES == part, here, picked)
    packed_ref[...] = jnp.where(lane < LANES // 2, picked, ids.astype(f32))


def score(recv, stale, idsg):
    return pl.pallas_call(
        score_kernel,
        out_shape=(
            jax.ShapeDtypeStruct(stale.shape, bf16),
            jax.ShapeDtypeStruct(idsg.shape, f32),
        ),
        scratch_shapes=[
            pltpu.VMEM(recv.shape, f32),
            pltpu.VMEM((stale.shape[1] // LANES, stale.shape[0], LANES), f32),
        ],
        compiler_params=params(),
        name="score",
    )(recv, stale, idsg)


HALF = LANES // 2


def spread_down(row):
    return jnp.broadcast_to(row, (LANES, LANES)).T


def pair_kernel(
    x_ref, discount_ref, grad_ref, loss_ref, half_s, wide_w, columns, across, near_q, far_q
):
    x = x_ref[...]
    n_blocks = x.shape[0] // 2
    count = n_blocks * LANES
    top, low = x[:n_blocks], x[n_blocks:]
    lane = lax.broadcasted_iota(jnp.int32, (n_blocks, LANES), 1)
    left = lane < HALF
    scores = jnp.where(left, top, pltpu.roll(low, HALF, 1))
    gains = jnp.exp2(jnp.where(left, pltpu.roll(top, HALF, 1), low))
    position = lax.broadcasted_iota(jnp.int32, (n_blocks, LANES), 0) * LANES + lane

    ordered = jnp.ones((n_blocks, LANES), f32)
    for level in range(1, 5):
        above = jnp.sum((gains > float(2**level) - 0.5).astype(f32))
        ordered = jnp.where(position.astype(f32) < above, float(2**level), ordered)
    ideal = jnp.sum(ordered * discount_ref[...])

    span = n_blocks // 2
    groups = LANES // 8

    def sweep(values, load_or_make):
        columns[...] = jnp.zeros_like(columns)
        values[n_blocks:] = values[:n_blocks]

        def met(i, k, kept, first, acc, both):
            v_k = jnp.broadcast_to(values[pl.ds(k, 1), :], (8, LANES))
            column = [jnp.zeros((8, LANES), f32) for _ in range(4)]
            out = []
            for g in range(groups):
                value = load_or_make(first[8 * g : 8 * g + 8], v_k, kept, 8 * g)
                out.append(acc[g] + value)
                column[g % 4] = column[g % 4] + value
            if both:
                columns[k] = columns[k] + ((column[0] + column[1]) + (column[2] + column[3]))
            return out

        def block(i, _):
            first = spread_down(values[pl.ds(i, 1), :])
            acc = [jnp.zeros((8, LANES), f32) for _ in range(groups)]
            for d in range(span):
                acc = met(i, i + d, near_q.at[i, d], first, acc, d > 0)
            across[pl.ds(i, 1), :] = jnp.sum(jnp.concatenate(acc, 0).T, 0, keepdims=True)
            return 0

        lax.fori_loop(0, n_blocks, block, 0)

        def opposite(i, _):
            first = spread_down(values[pl.ds(i, 1), :])
            acc = [jnp.zeros((8, LANES), f32) for _ in range(groups)]
            acc = met(i, i + span, far_q.at[i], first, acc, True)
            here = jnp.sum(jnp.concatenate(acc, 0).T, 0, keepdims=True)
            across[pl.ds(i, 1), :] = across[pl.ds(i, 1), :] + here
            return 0

        lax.fori_loop(0, span, opposite, 0)
        folded = jnp.sum(columns[...], 1)
        wrapped = jnp.concatenate((folded[n_blocks:], jnp.zeros((span, LANES), f32)), 0)
        return across[...] - folded[:n_blocks] - wrapped

    def rank_term(s_i, s_k, kept, at):
        t = jnp.tanh(s_k - s_i)
        kept[pl.ds(at, 8), :] = 1.0 - t * t
        return t

    def cross_term(w_i, w_k, kept, at):
        return (w_k - w_i) * kept[pl.ds(at, 8), :]

    half_s[:n_blocks] = 0.5 * scores
    rank = 0.5 + 0.5 * count + 0.5 * sweep(half_s, rank_term)
    logged = jnp.log2(1.0 + rank)
    weight = gains / (ideal * LOG_TWO * (1.0 + rank) * logged * logged)
    loss_ref[...] = jnp.full((1, LANES), 1.0 - jnp.sum(gains / logged) / ideal, f32)
    wide_w[:n_blocks] = 0.25 * weight
    grad = sweep(wide_w, cross_term).astype(bf16).astype(f32)
    grad_ref[:n_blocks] = grad
    grad_ref[n_blocks:] = pltpu.roll(grad, HALF, 1)


def pair(x, discount):
    n_blocks = x.shape[0] // 2
    span = n_blocks // 2
    return pl.pallas_call(
        pair_kernel,
        out_shape=(
            jax.ShapeDtypeStruct(x.shape, f32),
            jax.ShapeDtypeStruct((1, LANES), f32),
        ),
        scratch_shapes=[
            pltpu.VMEM((2 * n_blocks, LANES), f32),
            pltpu.VMEM((2 * n_blocks, LANES), f32),
            pltpu.VMEM((n_blocks + span, 8, LANES), f32),
            pltpu.VMEM((n_blocks, LANES), f32),
            pltpu.VMEM((n_blocks, span, LANES, LANES), f32),
            pltpu.VMEM((span, LANES, LANES), f32),
        ],
        compiler_params=params(),
        name="pair",
    )(x, discount)


def share_kernel(grad_ref, idsg_ref, refreshed_ref, out_ref, rows_w):
    lists, cache_rows = rows_w.shape
    for g in range(lists // 8):
        part = slice(8 * g, 8 * g + 8)
        grads = grad_ref[part, :]
        ids = idsg_ref[part, :]
        spots = [
            lax.broadcasted_iota(jnp.int32, (8, LANES), 1) + LANES * p
            for p in range(cache_rows // LANES)
        ]
        acc = [jnp.zeros((8, LANES), f32) for _ in spots]
        for j in range(HALF):
            id_j = jnp.broadcast_to(ids[:, j : j + 1], (8, LANES))
            grad_j = jnp.broadcast_to(grads[:, j : j + 1], (8, LANES))
            acc = [a + jnp.where(id_j == spot, grad_j, 0.0) for a, spot in zip(acc, spots)]
        for p, a in enumerate(acc):
            rows_w[part, p * LANES : (p + 1) * LANES] = a
    weights = rows_w[...]
    high = weights.astype(bf16)
    rest = (weights - high.astype(f32)).astype(bf16)
    refreshed = refreshed_ref[...]
    out_ref[...] = jnp.dot(high, refreshed, preferred_element_type=f32) + jnp.dot(
        rest, refreshed, preferred_element_type=f32
    )


def share(grads, idsg, refreshed):
    return pl.pallas_call(
        share_kernel,
        out_shape=jax.ShapeDtypeStruct((grads.shape[0], refreshed.shape[1]), f32),
        scratch_shapes=[pltpu.VMEM((grads.shape[0], refreshed.shape[0]), f32)],
        compiler_params=params(),
        name="share",
    )(grads, idsg, refreshed)


Y, ZZ, ZL, X = 4, 4, 2, 2


def shard_at(y, zz, zl, x):
    return ((y * ZZ + zz) * ZL + zl) * X + x


def everywhere():
    return [
        (y, zz, zl, x) for y in range(Y) for zz in range(ZZ) for zl in range(ZL) for x in range(X)
    ]


def current_projections(trainer_in, trainer_out):
    roles = lax.axis_size("role")
    shards = lax.axis_size("shard")
    axes = ("role", "shard")
    mine = jnp.concatenate((trainer_in[0], trainer_out[0]), 1)
    mine = lax.ppermute(
        mine,
        axes,
        [
            ((roles - 1) * shards + shard_at(y, zz, zl, x), zz * shards + shard_at(y, zz, zl, x))
            for y, zz, zl, x in everywhere()
        ],
    )
    block = mine
    for by in range(1, ZZ):
        block = block + lax.ppermute(
            mine,
            axes,
            [
                (
                    zz * shards + shard_at(y, zz, zl, x),
                    zz * shards + shard_at(y, (zz + by) % ZZ, zl, x),
                )
                for y, zz, zl, x in everywhere()
            ],
        )
    groups = [
        [shard_at(y, zz, zl, x) for zl in range(ZL) for y in range(Y) for x in range(X)]
        for zz in range(ZZ)
    ]
    parts = len(groups[0])
    units, width = block.shape
    gathered = lax.all_to_all(
        jnp.broadcast_to(block[None], (parts, units, width)),
        "shard",
        split_axis=0,
        concat_axis=0,
        tiled=True,
        axis_index_groups=groups,
    )
    return gathered.reshape(parts * units, width)


def per_device(
    cls_states, trainer_in, trainer_out, stale_cache, block_owner, queries, neg_ids, grades
):
    shards = lax.axis_size("shard")
    passages, width = cls_states.shape
    near = [(0, 1), (1, 0), (2, 3), (3, 2)]
    across = [(0, 2), (1, 3), (2, 0), (3, 1)]
    diagonal = [(0, 3), (1, 2), (2, 1), (3, 0)]
    x4 = jnp.concatenate(
        [cls_states] + [lax.ppermute(cls_states, "role", p) for p in (near, across, diagonal)], 0
    )
    projections = current_projections(trainer_in, trainer_out)
    own, far, to_near = encode(x4, projections, passages)
    from_near = lax.ppermute(to_near, "role", near)
    to_far = (far + from_near[passages:].astype(f32)).astype(bf16)
    from_far = lax.ppermute(to_far, "role", across)
    chunks = width // LANES
    rest = jnp.concatenate(
        (
            jnp.full((2 * CAP * chunks, LANES), EMPTY, bf16),
            queries.reshape(chunks, LANES),
            jnp.full((ROWS - (2 * CAP + 1) * chunks, LANES), EMPTY, bf16),
        ),
        0,
    )
    idsg = jnp.concatenate((neg_ids, grades), 1)
    outgoing = place(
        cls_states, own, from_near, from_far, block_owner.reshape(1, -1), rest, shards
    )
    outgoing, idsg = lax.optimization_barrier((outgoing, idsg))
    arrived = lax.all_to_all(
        outgoing.reshape(shards, ROWS, LANES), "shard", split_axis=0, concat_axis=0, tiled=True
    )
    refreshed, packed = score(arrived.reshape(-1, LANES), stale_cache, idsg)
    packed = lax.all_to_all(packed, "shard", split_axis=0, concat_axis=0, tiled=True)
    count = shards * neg_ids.shape[1]
    position = np.arange(1, count + 1, dtype=np.float64)
    discount = (1.0 / np.log2(1.0 + position)).astype(np.float32).reshape(-1, LANES)
    grads, loss = pair(packed, jnp.asarray(discount))
    grads = lax.all_to_all(grads, "shard", split_axis=0, concat_axis=0, tiled=True)
    shares = share(grads, idsg, refreshed)
    shares = lax.all_to_all(shares, "shard", split_axis=0, concat_axis=0, tiled=True)
    return refreshed, jnp.sum(shares, 0, keepdims=True), loss[0, :1]


def solution(mesh):
    return jax.shard_map(
        per_device,
        mesh=mesh,
        in_specs=(
            P(("role", "shard"), None),
            P("role", "shard", None),
            P("role", "shard", None),
            P(("role", "shard"), None),
            P(("role", "shard"), None),
            P(("role", "shard"), None),
            P("role", "shard"),
            P("role", "shard"),
        ),
        out_specs=(P(("role", "shard"), None), P(("role", "shard"), None), P(("role", "shard"))),
        check_vma=False,
    )
```

time: 222 us -> 198 us (0.89)
  starting transfers between devices: 65.7 us -> 13.8 us
  blocking collectives: 49.3 us -> 80 us
  waiting for transfers between devices: 64.6 us -> 57.9 us
    ppermute x24 -> x4, starting transfers between devices: 48.7 us -> 3.3 us  [the longest x3 2.63 us: current_projections(): lax.ppermute(mine, axes, [(zz * shards + shard_at(y, zz, zl, x), zz * sha...]
    ppermute x3, waiting for transfers between devices: 0.01 us -> 36.2 us  [per_device(): lax.ppermute(cls_states, 'role', p)]
    all_to_all x0 -> x1, blocking collectives: none -> 30.6 us  [per_device(): lax.all_to_all(outgoing.reshape(shards, ROWS, LANES), 'shard', split_axis...]
    all_to_all x1, waiting for transfers between devices: 24.3 us -> 0.01 us  [current_projections(): lax.all_to_all(jnp.broadcast_to(block[None], (parts, units, width)), 'sha...]
    ppermute x24 -> x4, waiting for transfers between devices: 33.4 us -> 13.3 us  [the longest x3 13.3 us: current_projections(): lax.ppermute(mine, axes, [(zz * shards + shard_at(y, zz, zl, x), zz * sha...]
    ppermute x1, starting transfers between devices: 2.89 us -> 0.18 us  [per_device(): from_far = lax.ppermute(to_far, 'role', across)]
    all_to_all x1, starting transfers between devices: 8.8 us -> 6.33 us  [current_projections(): lax.all_to_all(jnp.broadcast_to(block[None], (parts, units, width)), 'sha...]
  transfers between devices with their start and end apart: 30 -> 10, of which waited for: 12 -> 5; matrix products, arithmetic and copies ran while one was open for 0% -> 0% of each run, Pallas kernels for 0% -> 0%
where the time goes in v2:
time: 198 us; the launch traced here: 197 us
  blocking collectives  80 us (40%)
  waiting for transfers between devices  57.9 us (29%)
  Pallas kernels  36 us (18%)
  starting transfers between devices  13.8 us (7%)
  local copies, waits for them, and re-layouts  6.04 us (3%)
  other arithmetic  2.38 us (1%)
    ppermute x3, waiting for transfers between devices, per_device(): lax.ppermute(cls_states, 'role', p)  36.2 us
    all_to_all x1, blocking collectives, per_device(): lax.all_to_all(outgoing.reshape(shards, ROWS, LANES), 'shard', split_axis...  30.6 us
    pallas_call x1, Pallas kernels, pair(): pl.pallas_call(pair_kernel, out_shape=(jax.ShapeDtypeStruct(x.shape, f32)...  28 us
    all_to_all x1, blocking collectives, per_device(): lax.all_to_all(packed, 'shard', split_axis=0, concat_axis=0, tiled=True)  17.5 us
    all_to_all x1, blocking collectives, per_device(): lax.all_to_all(shares, 'shard', split_axis=0, concat_axis=0, tiled=True)  16.2 us
    all_to_all x1, blocking collectives, per_device(): lax.all_to_all(grads, 'shard', split_axis=0, concat_axis=0, tiled=True)  15.7 us
    ppermute x3, waiting for transfers between devices, current_projections(): lax.ppermute(mine, axes, [(zz * shards + shard_at(y, zz, zl, x), zz * sha...  13.3 us
    ppermute x1, waiting for transfers between devices, per_device(): from_far = lax.ppermute(to_far, 'role', across)  7 us
  transfers between devices with their start and end apart: 10, of which 5 were waited for; matrix products, arithmetic and copies ran while one was open for 0% of the time, Pallas kernels for 0%

profile of v2, /device:TPU:2, one launch (start us, length us, event | category | flops | bytes accessed | tf_op | source)
XLA Modules:
  0.0 196.8 jit_solution(17247295057167286462)
XLA Ops:
  0.6 0.9 pad_maximum_fusion.1
  1.6 0.7 collective-permute-start.3
  2.3 0.7 collective-permute-start.4
  2.9 1.3 collective-permute-start.5
  4.2 0.7 collective-permute-start.6
  4.9 13.3 %collective-permute-done.5 = bf16[48,1536]{1,0:T(8,128)(2,1)S(1)} collective-permute-done((bf16[48,1536]{1,0:T(8,128)(2,1)S(1)}, bf16[48,1536]{1,0:T(8,128)(2,1)S(1)}, u32[]{:S(2)}, u32[]{:S(2)}) %collective-permute-start.5) | collective-permute-done | bytes 147488 | tf_op jit(solution)/shard_map/ppermute | solution.py:334
  18.2 1.7 broadcast_in_dim.15
  19.9 6.3 %all-to-all-start = ((bf16[16,48,1536]{2,1,0:T(8,128)(2,1)}), bf16[16,48,1536]{2,1,0:T(8,128)(2,1)S(1)}, u32[]{:S(2)}, u32[]{:S(2)}) async-start(bf16[16,48,1536]{2,1,0:T(8,128)(2,1)} %broadcast_in_dim.15), calls=%async_computation | async-start | bytes 4718592 | tf_op jit(solution)/shard_map/all_to_all | solution.py:351
  26.2 0.8 collective-permute-start
  27.0 2.4 %collective-permute-start.1 = (bf16[128,768]{1,0:T(8,128)(2,1)S(1)}, bf16[128,768]{1,0:T(8,128)(2,1)S(1)}, u32[]{:S(2)}, u32[]{:S(2)}) collective-permute-start(bf16[128,768]{1,0:T(8,128)(2,1)S(1)} %copy-done), channel_id=1, source_target_pairs={{0,128},{64,192},{128,0},{192,64},{1,129},{65,193},{129,1},{193,65... | collective-permute-start | bytes 589832 | tf_op jit(solution)/shard_map/ppermute | solution.py:371
  29.5 33.7 %collective-permute-done.1 = bf16[128,768]{1,0:T(8,128)(2,1)S(1)} collective-permute-done((bf16[128,768]{1,0:T(8,128)(2,1)S(1)}, bf16[128,768]{1,0:T(8,128)(2,1)S(1)}, u32[]{:S(2)}, u32[]{:S(2)}) %collective-permute-start.1) | collective-permute-done | bytes 196640 | tf_op jit(solution)/shard_map/ppermute | solution.py:371
  63.2 2.6 %collective-permute-done.2 = bf16[128,768]{1,0:T(8,128)(2,1)S(1)} collective-permute-done((bf16[128,768]{1,0:T(8,128)(2,1)S(1)}, bf16[128,768]{1,0:T(8,128)(2,1)S(1)}, u32[]{:S(2)}, u32[]{:S(2)}) %collective-permute-start.2) | collective-permute-done | bytes 196640 | tf_op jit(solution)/shard_map/ppermute | solution.py:371
  65.9 2.9 %encode.1 = (f32[128,768]{1,0:T(8,128)S(1)}, f32[128,768]{1,0:T(8,128)S(1)}, bf16[256,768]{1,0:T(8,128)(2,1)}) custom-call(bf16[512,768]{1,0:T(8,128)(2,1)S(1)} %pad_maximum_fusion.x_ref, bf16[768,1536]{1,0:T(8,128)(2,1)S(1)} %bitcast.18), custom_call_target="tpu_custom_call" | custom-call | tf_op jit(solution)/shard_map/encode/pallas_call | solution.py:45
  68.8 0.7 copy-done.2
  69.5 0.7 copy-done.4
  70.2 0.7 collective-permute-start.7
  71.1 1.3 collective-permute-done.7.near_ref
  72.5 1.0 add_convert_fusion
  73.5 0.2 collective-permute-start.8
  73.8 7.0 %collective-permute-done.8.far_ref = bf16[128,768]{1,0:T(8,128)(2,1)S(1)} collective-permute-done((bf16[128,768]{1,0:T(8,128)(2,1)S(1)}, bf16[128,768]{1,0:T(8,128)(2,1)S(1)}, u32[]{:S(2)}, u32[]{:S(2)}) %collective-permute-start.8) | collective-permute-done | bytes 196640 | tf_op jit(solution)/shard_map/ppermute | solution.py:377
  80.8 1.0 copy-done.5
  81.8 1.5 place.1
  83.3 30.6 %all_to_all.41 = bf16[64,32,128]{2,1,0:T(8,128)(2,1)S(1)} all-to-all(bf16[64,32,128]{2,1,0:T(8,128)(2,1)S(1)} %bitcast.19), channel_id=1, replica_groups=mesh['role'=4,'shard'=64] {'shard'}, dimensions={0} | all-to-all | bytes 1048576 | tf_op jit(solution)/shard_map/all_to_all | solution.py:392
  114.0 1.6 score.1
  115.5 17.5 %all_to_all.42 = f32[64,1,128]{2,1,0:T(1,128)S(1)} all-to-all(f32[64,1,128]{2,1,0:T(1,128)S(1)} %bitcast.25), channel_id=1, replica_groups=mesh['role'=4,'shard'=64] {'shard'}, dimensions={0} | all-to-all | bytes 65536 | tf_op jit(solution)/shard_map/all_to_all | solution.py:396
  133.1 28.0 %pair.1 = (f32[64,128]{1,0:T(8,128)S(1)}, f32[1,128]{1,0:T(1,128)}) custom-call(f32[64,128]{1,0:T(8,128)S(1)} %bitcast.23, f32[32,128]{1,0:T(8,128)S(1)} %copy-done.6), custom_call_target="tpu_custom_call" | custom-call | tf_op jit(solution)/shard_map/pair/pallas_call | solution.py:251
  161.1 15.7 %all_to_all.43 = f32[64,1,128]{2,1,0:T(1,128)S(1)} all-to-all(f32[64,1,128]{2,1,0:T(1,128)S(1)} %bitcast.24), channel_id=1, replica_groups=mesh['role'=4,'shard'=64] {'shard'}, dimensions={0} | all-to-all | bytes 65536 | tf_op jit(solution)/shard_map/all_to_all | solution.py:401
  176.8 1.0 copy-done.1
  177.8 2.0 %share.1 = f32[64,768]{1,0:T(8,128)S(1)} custom-call(f32[64,128]{1,0:T(8,128)S(1)} %bitcast.22, s32[64,128]{1,0:T(8,128)S(1)} %pad_add_fusion.idsg_ref, bf16[256,768]{1,0:T(8,128)(2,1)S(1)} %copy-done.1), custom_call_target="tpu_custom_call" | custom-call | tf_op jit(solution)/shard_map/share/pallas_call | solution.py:297
  179.7 0.2 copy.14
  180.0 16.2 %all_to_all.44 = f32[64,1,768]{2,1,0:T(1,128)S(1)} all-to-all(f32[64,1,768]{2,1,0:T(1,128)S(1)} %copy.14), channel_id=1, replica_groups=mesh['role'=4,'shard'=64] {'shard'}, dimensions={0} | all-to-all | bytes 393216 | tf_op jit(solution)/shard_map/all_to_all | solution.py:403
  196.3 0.6 broadcast_in_dim.18
  (34 shorter events, 0.6 us)
Async XLA Ops:
  1.6 0.7 collective-permute-start.3
  2.3 2.7 %collective-permute-start.4 = (bf16[48,1536]{1,0:T(8,128)(2,1)S(1)}, bf16[48,1536]{1,0:T(8,128)(2,1)S(1)}, u32[]{:S(2)}, u32[]{:S(2)}) collective-permute-start(bf16[48,1536]{1,0:T(8,128)(2,1)S(1)} %collective-permute-done.3), channel_id=1, source_target_pairs={{0,4},{1,5},{2,6},{3,7},{68,72},{69,73},{70,74},{71,75},{136,140},... | collective-permute-start | bytes 442376 | tf_op jit(solution)/shard_map/ppermute | solution.py:334
  2.9 15.3 %collective-permute-start.5 = (bf16[48,1536]{1,0:T(8,128)(2,1)S(1)}, bf16[48,1536]{1,0:T(8,128)(2,1)S(1)}, u32[]{:S(2)}, u32[]{:S(2)}) collective-permute-start(bf16[48,1536]{1,0:T(8,128)(2,1)S(1)} %collective-permute-done.3), channel_id=1, source_target_pairs={{0,8},{1,9},{2,10},{3,11},{68,76},{69,77},{70,78},{71,79},{136,128... | collective-permute-start | bytes 442376 | tf_op jit(solution)/shard_map/ppermute | solution.py:334
  4.2 14.0 %collective-permute-start.6 = (bf16[48,1536]{1,0:T(8,128)(2,1)S(1)}, bf16[48,1536]{1,0:T(8,128)(2,1)S(1)}, u32[]{:S(2)}, u32[]{:S(2)}) collective-permute-start(bf16[48,1536]{1,0:T(8,128)(2,1)S(1)} %collective-permute-done.3), channel_id=1, source_target_pairs={{0,12},{1,13},{2,14},{3,15},{68,64},{69,65},{70,66},{71,67},{136,1... | collective-permute-start | bytes 442376 | tf_op jit(solution)/shard_map/ppermute | solution.py:334
  19.9 6.3 %copy-start = (bf16[128,768]{1,0:T(8,128)(2,1)S(1)}, bf16[128,768]{1,0:T(8,128)(2,1)}, u32[]{:S(2)}) copy-start(bf16[128,768]{1,0:T(8,128)(2,1)} %cls_ref.1) | copy-start | bytes 589828
  19.9 45.9 %all-to-all-start = ((bf16[16,48,1536]{2,1,0:T(8,128)(2,1)}), bf16[16,48,1536]{2,1,0:T(8,128)(2,1)S(1)}, u32[]{:S(2)}, u32[]{:S(2)}) async-start(bf16[16,48,1536]{2,1,0:T(8,128)(2,1)} %broadcast_in_dim.15), calls=%async_computation | async-start | bytes 4718592 | tf_op jit(solution)/shard_map/all_to_all | solution.py:351
  26.2 3.3 %collective-permute-start = (bf16[128,768]{1,0:T(8,128)(2,1)S(1)}, bf16[128,768]{1,0:T(8,128)(2,1)S(1)}, u32[]{:S(2)}, u32[]{:S(2)}) collective-permute-start(bf16[128,768]{1,0:T(8,128)(2,1)S(1)} %copy-done), channel_id=1, source_target_pairs={{0,64},{64,0},{128,192},{192,128},{1,65},{65,1},{129,193},{193,129... | collective-permute-start | bytes 589832 | tf_op jit(solution)/shard_map/ppermute | solution.py:371
  27.0 36.2 %collective-permute-start.1 = (bf16[128,768]{1,0:T(8,128)(2,1)S(1)}, bf16[128,768]{1,0:T(8,128)(2,1)S(1)}, u32[]{:S(2)}, u32[]{:S(2)}) collective-permute-start(bf16[128,768]{1,0:T(8,128)(2,1)S(1)} %copy-done), channel_id=1, source_target_pairs={{0,128},{64,192},{128,0},{192,64},{1,129},{65,193},{129,1},{193,65... | collective-permute-start | bytes 589832 | tf_op jit(solution)/shard_map/ppermute | solution.py:371
  29.5 36.3 %collective-permute-start.2 = (bf16[128,768]{1,0:T(8,128)(2,1)S(1)}, bf16[128,768]{1,0:T(8,128)(2,1)S(1)}, u32[]{:S(2)}, u32[]{:S(2)}) collective-permute-start(bf16[128,768]{1,0:T(8,128)(2,1)S(1)} %copy-done), channel_id=1, source_target_pairs={{0,192},{64,128},{128,64},{192,0},{1,193},{65,129},{129,65},{193,1... | collective-permute-start | bytes 589832 | tf_op jit(solution)/shard_map/ppermute | solution.py:371
  65.8 5.2 %copy-start.10 = (bf16[1,768]{1,0:T(2,128)(2,1)S(1)}, bf16[1,768]{1,0:T(2,128)(2,1)}, u32[]{:S(2)}) copy-start(bf16[1,768]{1,0:T(2,128)(2,1)} %param.14) | copy-start | bytes 4612
  65.8 5.2 %copy-start.8 = (s32[64,64]{1,0:T(8,128)S(1)}, s32[64,64]{1,0:T(8,128)}, u32[]{:S(2)}) copy-start(s32[64,64]{1,0:T(8,128)} %param.16) | copy-start | bytes 49156
  65.8 5.2 %copy-start.9 = (s32[64,64]{1,0:T(8,128)S(1)}, s32[64,64]{1,0:T(8,128)}, u32[]{:S(2)}) copy-start(s32[64,64]{1,0:T(8,128)} %param.15) | copy-start | bytes 49156
  65.9 14.9 %copy-start.7 = (s32[64,1]{0,1:T(1,128)S(1)}, s32[64,1]{0,1:T(1,128)}, u32[]{:S(2)}) copy-start(s32[64,1]{0,1:T(1,128)} %param.13) | copy-start | bytes 772
  68.8 0.7 copy-start.2
  69.5 0.7 copy-start.4
  70.2 2.2 %collective-permute-start.7 = (bf16[256,768]{1,0:T(8,128)(2,1)}, bf16[256,768]{1,0:T(8,128)(2,1)S(1)}, u32[]{:S(2)}, u32[]{:S(2)}) collective-permute-start(bf16[256,768]{1,0:T(8,128)(2,1)} %get-tuple-element.13), channel_id=1, source_target_pairs={{0,64},{64,0},{128,192},{192,128},{1,65},{65,1},{129,193},{193,129... | collective-permute-start | bytes 1179656 | tf_op jit(solution)/shard_map/ppermute | solution.py:375
  73.5 40.5 %copy-start.3 = (bf16[256,768]{1,0:T(8,128)(2,1)S(1)}, bf16[256,768]{1,0:T(8,128)(2,1)}, u32[]{:S(2)}) copy-start(bf16[256,768]{1,0:T(8,128)(2,1)} %stale_ref.1) | copy-start | bytes 1179652
  73.5 7.3 %collective-permute-start.8 = (bf16[128,768]{1,0:T(8,128)(2,1)S(1)}, bf16[128,768]{1,0:T(8,128)(2,1)S(1)}, u32[]{:S(2)}, u32[]{:S(2)}) collective-permute-start(bf16[128,768]{1,0:T(8,128)(2,1)S(1)} %add_convert_fusion), channel_id=1, source_target_pairs={{0,128},{64,192},{128,0},{192,64},{1,129},{65,193},{129,1},{193,65... | collective-permute-start | bytes 589832 | tf_op jit(solution)/shard_map/ppermute | solution.py:377
  80.8 1.0 copy-start.5
  81.8 51.3 %copy-start.6 = (f32[32,128]{1,0:T(8,128)S(1)}, f32[32,128]{1,0:T(8,128)}, u32[]{:S(2)}) copy-start(f32[32,128]{1,0:T(8,128)} %constant.2.clone.discount_ref) | copy-start | bytes 49156
  176.8 1.0 copy-start.1

commit v3 on v2

--- a/solution.py
+++ b/solution.py
@@ -26,32 +26,25 @@
     return lax.dot_general(a, b, (((1,), (1,)), ((), ())), preferred_element_type=f32)
 
 
-def encode_kernel(x_ref, w_ref, own_ref, far_ref, near_ref):
-    rows, width = own_ref.shape
-    for k in (1, 3, 2, 0):
-        inner = contract_last(x_ref[pl.ds(k * rows, rows), :], w_ref[:, :width])
+def encode_kernel(kept_x_ref, sent_x_ref, w_ref, kept_ref, sent_ref):
+    width = kept_ref.shape[1]
+    for x_ref, out_ref in ((sent_x_ref, sent_ref), (kept_x_ref, kept_ref)):
+        inner = contract_last(x_ref[...], w_ref[:, :width])
         hidden = 0.5 * inner * (1.0 + lax.erf(inner * math.sqrt(0.5)))
         part = jnp.dot(hidden.astype(bf16), w_ref[:, width:], preferred_element_type=f32)
-        if k == 0:
-            own_ref[...] = part
-        elif k == 2:
-            far_ref[...] = part
-        else:
-            near_ref[pl.ds(k // 2 * rows, rows), :] = part.astype(bf16)
-
-
-def encode(x4, projections, rows):
-    width = x4.shape[1]
+        out_ref[...] = part.astype(out_ref.dtype)
+
+
+def encode(kept_x, sent_x, projections):
     return pl.pallas_call(
         encode_kernel,
         out_shape=(
-            jax.ShapeDtypeStruct((rows, width), f32),
-            jax.ShapeDtypeStruct((rows, width), f32),
-            jax.ShapeDtypeStruct((2 * rows, width), bf16),
+            jax.ShapeDtypeStruct(kept_x.shape, f32),
+            jax.ShapeDtypeStruct(sent_x.shape, bf16),
         ),
         compiler_params=params(),
         name="encode",
-    )(x4, projections)
+    )(kept_x, sent_x, projections)
 
 
 ROWS = 32
@@ -66,7 +59,7 @@
     resid = (
         cls_ref[...].astype(f32)
         + own_ref[...]
-        + near_ref[:rows, :].astype(f32)
+        + near_ref[...].astype(f32)
         + far_ref[...].astype(f32)
     )
     centred = resid - jnp.mean(resid, -1, keepdims=True)
@@ -161,12 +154,8 @@
 HALF = LANES // 2
 
 
-def spread_down(row):
-    return jnp.broadcast_to(row, (LANES, LANES)).T
-
-
 def pair_kernel(
-    x_ref, discount_ref, grad_ref, loss_ref, half_s, wide_w, columns, across, near_q, far_q
+    x_ref, discount_ref, grad_ref, loss_ref, half_s, wide_w, columns, across, rows_s, near_q, far_q
 ):
     x = x_ref[...]
     n_blocks = x.shape[0] // 2
@@ -191,37 +180,38 @@
         columns[...] = jnp.zeros_like(columns)
         values[n_blocks:] = values[:n_blocks]
 
-        def met(i, k, kept, first, acc, both):
-            v_k = jnp.broadcast_to(values[pl.ds(k, 1), :], (8, LANES))
-            column = [jnp.zeros((8, LANES), f32) for _ in range(4)]
-            out = []
+        def spread(i, _):
+            rows_s[i] = jnp.broadcast_to(values[pl.ds(i, 1), :], (LANES, LANES)).T
+            return 0
+
+        lax.fori_loop(0, n_blocks, spread, 0, unroll=8)
+
+        def block(i, last):
+            first = [rows_s[i, pl.ds(8 * g, 8), :] for g in range(groups)]
+            acc = [jnp.zeros((8, LANES), f32) for _ in range(groups)]
+            for d in range(last + 1):
+                k = i + d
+                kept = near_q.at[i, d] if d < span else far_q.at[i]
+                v_k = jnp.broadcast_to(values[pl.ds(k, 1), :], (8, LANES))
+                column = [jnp.zeros((8, LANES), f32) for _ in range(4)]
+                for g in range(groups):
+                    value = load_or_make(first[g], v_k, kept, 8 * g)
+                    acc[g] = acc[g] + value
+                    column[g % 4] = column[g % 4] + value
+                if d > 0:
+                    columns[k] = columns[k] + ((column[0] + column[1]) + (column[2] + column[3]))
             for g in range(groups):
-                value = load_or_make(first[8 * g : 8 * g + 8], v_k, kept, 8 * g)
-                out.append(acc[g] + value)
-                column[g % 4] = column[g % 4] + value
-            if both:
-                columns[k] = columns[k] + ((column[0] + column[1]) + (column[2] + column[3]))
-            return out
-
-        def block(i, _):
-            first = spread_down(values[pl.ds(i, 1), :])
-            acc = [jnp.zeros((8, LANES), f32) for _ in range(groups)]
-            for d in range(span):
-                acc = met(i, i + d, near_q.at[i, d], first, acc, d > 0)
-            across[pl.ds(i, 1), :] = jnp.sum(jnp.concatenate(acc, 0).T, 0, keepdims=True)
+                rows_s[i, pl.ds(8 * g, 8), :] = acc[g]
             return 0
 
-        lax.fori_loop(0, n_blocks, block, 0)
-
-        def opposite(i, _):
-            first = spread_down(values[pl.ds(i, 1), :])
-            acc = [jnp.zeros((8, LANES), f32) for _ in range(groups)]
-            acc = met(i, i + span, far_q.at[i], first, acc, True)
-            here = jnp.sum(jnp.concatenate(acc, 0).T, 0, keepdims=True)
-            across[pl.ds(i, 1), :] = across[pl.ds(i, 1), :] + here
+        lax.fori_loop(0, span, lambda i, _: block(i, span), 0)
+        lax.fori_loop(span, n_blocks, lambda i, _: block(i, span - 1), 0)
+
+        def collect(i, _):
+            across[pl.ds(i, 1), :] = jnp.sum(rows_s[i].T, 0, keepdims=True)
             return 0
 
-        lax.fori_loop(0, span, opposite, 0)
+        lax.fori_loop(0, n_blocks, collect, 0, unroll=8)
         folded = jnp.sum(columns[...], 1)
         wrapped = jnp.concatenate((folded[n_blocks:], jnp.zeros((span, LANES), f32)), 0)
         return across[...] - folded[:n_blocks] - wrapped
@@ -259,6 +249,7 @@
             pltpu.VMEM((2 * n_blocks, LANES), f32),
             pltpu.VMEM((n_blocks + span, 8, LANES), f32),
             pltpu.VMEM((n_blocks, LANES), f32),
+            pltpu.VMEM((n_blocks, LANES, LANES), f32),
             pltpu.VMEM((n_blocks, span, LANES, LANES), f32),
             pltpu.VMEM((span, LANES, LANES), f32),
         ],
@@ -342,6 +333,10 @@
                 for y, zz, zl, x in everywhere()
             ],
         )
+    return block
+
+
+def gather_units(block):
     groups = [
         [shard_at(y, zz, zl, x) for zl in range(ZL) for y in range(Y) for x in range(X)]
         for zz in range(ZZ)
@@ -366,15 +361,16 @@
     passages, width = cls_states.shape
     near = [(0, 1), (1, 0), (2, 3), (3, 2)]
     across = [(0, 2), (1, 3), (2, 0), (3, 1)]
-    diagonal = [(0, 3), (1, 2), (2, 1), (3, 0)]
-    x4 = jnp.concatenate(
-        [cls_states] + [lax.ppermute(cls_states, "role", p) for p in (near, across, diagonal)], 0
-    )
-    projections = current_projections(trainer_in, trainer_out)
-    own, far, to_near = encode(x4, projections, passages)
-    from_near = lax.ppermute(to_near, "role", near)
-    to_far = (far + from_near[passages:].astype(f32)).astype(bf16)
+    x_across = lax.ppermute(cls_states, "role", across)
+    x_others = lax.ppermute(jnp.concatenate((cls_states, x_across), 0), "role", near)
+    block = current_projections(trainer_in, trainer_out)
+    block, x_across, x_others = lax.optimization_barrier((block, x_across, x_others))
+    projections = gather_units(block)
+    far, for_far = encode(x_across, x_others[passages:], projections)
+    to_far = (far + lax.ppermute(for_far, "role", near).astype(f32)).astype(bf16)
     from_far = lax.ppermute(to_far, "role", across)
+    own, for_near = encode(cls_states, x_others[:passages], projections)
+    from_near = lax.ppermute(for_near, "role", near)
     chunks = width // LANES
     rest = jnp.concatenate(
         (

time: 198 us -> 178 us (0.90)
  Pallas kernels: 36 us -> 24.3 us
  waiting for transfers between devices: 57.9 us -> 48.2 us
  starting transfers between devices: 13.8 us -> 17.8 us
  local copies, waits for them, and re-layouts: 6.04 us -> 3.6 us
    ppermute x4, waiting for transfers between devices: 37.6 us -> 0.31 us  [the longest x1 0.3 us: per_device(): x_across = lax.ppermute(cls_states, 'role', across)]
    all_to_all x1, waiting for transfers between devices: 0.01 us -> 35.8 us  [gather_units(): lax.all_to_all(jnp.broadcast_to(block[None], (parts, units, width)), 'sha...]
    pallas_call x1, Pallas kernels: 28 us -> 16.1 us  [pair(): pl.pallas_call(pair_kernel, out_shape=(jax.ShapeDtypeStruct(x.shape, f32)...]
    ppermute x3, waiting for transfers between devices: 13.3 us -> 7.03 us  [current_projections(): lax.ppermute(mine, axes, [(zz * shards + shard_at(y, zz, zl, x), zz * sha...]
    unnamed x22 -> x12, local copies, waits for them, and re-layouts: 3.51 us -> 1.03 us
    ppermute x4, starting transfers between devices: 3.95 us -> 6.27 us  [the longest x1 3.26 us: per_device(): lax.ppermute(jnp.concatenate((cls_states, x_across), 0), 'role', near)]
  transfers between devices with their start and end apart: 10 -> 10, of which waited for: 5 -> 4; matrix products, arithmetic and copies ran while one was open for 0% -> 2% of each run, Pallas kernels for 0% -> 1%
where the time goes in v3:
time: 178 us; the launch traced here: 177 us
  blocking collectives  79.3 us (45%)
  waiting for transfers between devices  48.2 us (27%)
  Pallas kernels  24.3 us (14%)
  starting transfers between devices  17.8 us (10%)
  local copies, waits for them, and re-layouts  3.6 us (2%)
  other arithmetic  3.05 us (2%)
    all_to_all x1, waiting for transfers between devices, gather_units(): lax.all_to_all(jnp.broadcast_to(block[None], (parts, units, width)), 'sha...  35.8 us
    all_to_all x1, blocking collectives, per_device(): lax.all_to_all(outgoing.reshape(shards, ROWS, LANES), 'shard', split_axis...  29.7 us
    all_to_all x1, blocking collectives, per_device(): lax.all_to_all(packed, 'shard', split_axis=0, concat_axis=0, tiled=True)  17.6 us
    all_to_all x1, blocking collectives, per_device(): lax.all_to_all(shares, 'shard', split_axis=0, concat_axis=0, tiled=True)  16.2 us
    pallas_call x1, Pallas kernels, pair(): pl.pallas_call(pair_kernel, out_shape=(jax.ShapeDtypeStruct(x.shape, f32)...  16.1 us
    all_to_all x1, blocking collectives, per_device(): lax.all_to_all(grads, 'shard', split_axis=0, concat_axis=0, tiled=True)  15.8 us
    ppermute x3, waiting for transfers between devices, current_projections(): lax.ppermute(mine, axes, [(zz * shards + shard_at(y, zz, zl, x), zz * sha...  7.03 us
    all_to_all x1, starting transfers between devices, gather_units(): lax.all_to_all(jnp.broadcast_to(block[None], (parts, units, width)), 'sha...  6.48 us
  transfers between devices with their start and end apart: 10, of which 4 were waited for; matrix products, arithmetic and copies ran while one was open for 2% of the time, Pallas kernels for 1%

profile of v3, /device:TPU:2, one launch (start us, length us, event | category | flops | bytes accessed | tf_op | source)
XLA Modules:
  0.0 177.1 jit_solution(12649130133767183419)
XLA Ops:
  0.6 2.4 %collective-permute-start.4 = (bf16[128,768]{1,0:T(8,128)(2,1)}, bf16[128,768]{1,0:T(8,128)(2,1)S(1)}, u32[]{:S(2)}, u32[]{:S(2)}) collective-permute-start(bf16[128,768]{1,0:T(8,128)(2,1)} %cls_ref.1), channel_id=1, source_target_pairs={{0,128},{64,192},{128,0},{192,64},{1,129},{65,193},{129,1},{193,65... | collective-permute-start | bytes 589832 | tf_op jit(solution)/shard_map/ppermute | solution.py:364
  3.0 0.9 pad_maximum_fusion.1
  3.9 0.7 collective-permute-start
  4.6 0.7 collective-permute-start.1
  5.3 1.3 collective-permute-start.2
  6.6 0.7 collective-permute-start.3
  7.3 0.3 collective-permute-done.4.kept_x_ref
  7.6 1.0 pad_maximum_fusion
  8.5 3.3 %collective-permute-start.5 = (bf16[256,768]{1,0:T(8,128)(2,1)S(1)}, bf16[256,768]{1,0:T(8,128)(2,1)S(1)}, u32[]{:S(2)}, u32[]{:S(2)}) collective-permute-start(bf16[256,768]{1,0:T(8,128)(2,1)S(1)} %pad_maximum_fusion), channel_id=1, source_target_pairs={{0,64},{64,0},{128,192},{192,128},{1,65},{65,1},{129,193},{193,129... | collective-permute-start | bytes 1179656 | tf_op jit(solution)/shard_map/ppermute | solution.py:365
  11.8 7.0 %collective-permute-done.2 = bf16[48,1536]{1,0:T(8,128)(2,1)S(1)} collective-permute-done((bf16[48,1536]{1,0:T(8,128)(2,1)S(1)}, bf16[48,1536]{1,0:T(8,128)(2,1)S(1)}, u32[]{:S(2)}, u32[]{:S(2)}) %collective-permute-start.2) | collective-permute-done | bytes 147488 | tf_op jit(solution)/shard_map/ppermute | solution.py:325
  18.9 1.7 broadcast_in_dim.15
  20.5 6.5 %all-to-all-start = ((bf16[16,48,1536]{2,1,0:T(8,128)(2,1)}), bf16[16,48,1536]{2,1,0:T(8,128)(2,1)S(1)}, u32[]{:S(2)}, u32[]{:S(2)}) async-start(bf16[16,48,1536]{2,1,0:T(8,128)(2,1)} %broadcast_in_dim.15), calls=%async_computation | async-start | bytes 4718592 | tf_op jit(solution)/shard_map/all_to_all | solution.py:346
  27.1 35.8 %all-to-all-done = bf16[16,48,1536]{2,1,0:T(8,128)(2,1)S(1)} async-done(((bf16[16,48,1536]{2,1,0:T(8,128)(2,1)}), bf16[16,48,1536]{2,1,0:T(8,128)(2,1)S(1)}, u32[]{:S(2)}, u32[]{:S(2)}) %all-to-all-start) | async-done | bytes 2359328 | tf_op jit(solution)/shard_map/all_to_all | solution.py:346
  62.9 1.5 encode.3
  64.4 0.1 collective-permute-start.7
  64.7 0.9 pad_add_fusion.idsg_ref
  65.5 1.5 encode.2
  67.1 0.6 collective-permute-start.6
  67.7 1.8 %collective-permute-start.8 = (bf16[128,768]{1,0:T(8,128)(2,1)S(1)}, bf16[128,768]{1,0:T(8,128)(2,1)S(1)}, u32[]{:S(2)}, u32[]{:S(2)}) collective-permute-start(bf16[128,768]{1,0:T(8,128)(2,1)S(1)} %add_convert_fusion), channel_id=1, source_target_pairs={{0,128},{64,192},{128,0},{192,64},{1,129},{65,193},{129,1},{193,65... | collective-permute-start | bytes 589832 | tf_op jit(solution)/shard_map/ppermute | solution.py:371
  69.6 5.1 %collective-permute-done.8.far_ref = bf16[128,768]{1,0:T(8,128)(2,1)S(1)} collective-permute-done((bf16[128,768]{1,0:T(8,128)(2,1)S(1)}, bf16[128,768]{1,0:T(8,128)(2,1)S(1)}, u32[]{:S(2)}, u32[]{:S(2)}) %collective-permute-start.8) | collective-permute-done | bytes 196640 | tf_op jit(solution)/shard_map/ppermute | solution.py:371
  74.6 1.5 place.1
  76.2 29.7 %all_to_all.41 = bf16[64,32,128]{2,1,0:T(8,128)(2,1)S(1)} all-to-all(bf16[64,32,128]{2,1,0:T(8,128)(2,1)S(1)} %bitcast.20), channel_id=1, replica_groups=mesh['role'=4,'shard'=64] {'shard'}, dimensions={0} | all-to-all | bytes 1048576 | tf_op jit(solution)/shard_map/all_to_all | solution.py:388
  105.9 1.6 score.1
  107.5 17.6 %all_to_all.42 = f32[64,1,128]{2,1,0:T(1,128)S(1)} all-to-all(f32[64,1,128]{2,1,0:T(1,128)S(1)} %bitcast.26), channel_id=1, replica_groups=mesh['role'=4,'shard'=64] {'shard'}, dimensions={0} | all-to-all | bytes 65536 | tf_op jit(solution)/shard_map/all_to_all | solution.py:392
  125.1 16.1 %pair.1 = (f32[64,128]{1,0:T(8,128)S(1)}, f32[1,128]{1,0:T(1,128)}) custom-call(f32[64,128]{1,0:T(8,128)S(1)} %bitcast.24, f32[32,128]{1,0:T(8,128)S(1)} %copy-done.3), custom_call_target="tpu_custom_call" | custom-call | tf_op jit(solution)/shard_map/pair/pallas_call | solution.py:241
  141.2 15.8 %all_to_all.43 = f32[64,1,128]{2,1,0:T(1,128)S(1)} all-to-all(f32[64,1,128]{2,1,0:T(1,128)S(1)} %bitcast.25), channel_id=1, replica_groups=mesh['role'=4,'shard'=64] {'shard'}, dimensions={0} | all-to-all | bytes 65536 | tf_op jit(solution)/shard_map/all_to_all | solution.py:397
  157.0 1.0 copy-done.1
  158.0 2.0 %share.1 = f32[64,768]{1,0:T(8,128)S(1)} custom-call(f32[64,128]{1,0:T(8,128)S(1)} %bitcast.23, s32[64,128]{1,0:T(8,128)S(1)} %pad_add_fusion.idsg_ref, bf16[256,768]{1,0:T(8,128)(2,1)S(1)} %copy-done.1), custom_call_target="tpu_custom_call" | custom-call | tf_op jit(solution)/shard_map/share/pallas_call | solution.py:288
  160.0 0.2 copy.14
  160.2 16.2 %all_to_all.44 = f32[64,1,768]{2,1,0:T(1,128)S(1)} all-to-all(f32[64,1,768]{2,1,0:T(1,128)S(1)} %copy.14), channel_id=1, replica_groups=mesh['role'=4,'shard'=64] {'shard'}, dimensions={0} | all-to-all | bytes 393216 | tf_op jit(solution)/shard_map/all_to_all | solution.py:399
  176.4 0.1 reduce_sum.9
  176.5 0.6 broadcast_in_dim.18
  (26 shorter events, 0.3 us)
Async XLA Ops:
  0.6 6.9 %collective-permute-start.4 = (bf16[128,768]{1,0:T(8,128)(2,1)}, bf16[128,768]{1,0:T(8,128)(2,1)S(1)}, u32[]{:S(2)}, u32[]{:S(2)}) collective-permute-start(bf16[128,768]{1,0:T(8,128)(2,1)} %cls_ref.1), channel_id=1, source_target_pairs={{0,128},{64,192},{128,0},{192,64},{1,129},{65,193},{129,1},{193,65... | collective-permute-start | bytes 589832 | tf_op jit(solution)/shard_map/ppermute | solution.py:364
  3.9 0.7 collective-permute-start
  4.6 7.2 %collective-permute-start.1 = (bf16[48,1536]{1,0:T(8,128)(2,1)S(1)}, bf16[48,1536]{1,0:T(8,128)(2,1)S(1)}, u32[]{:S(2)}, u32[]{:S(2)}) collective-permute-start(bf16[48,1536]{1,0:T(8,128)(2,1)S(1)} %collective-permute-done), channel_id=1, source_target_pairs={{0,4},{1,5},{2,6},{3,7},{68,72},{69,73},{70,74},{71,75},{136,140},... | collective-permute-start | bytes 442376 | tf_op jit(solution)/shard_map/ppermute | solution.py:325
  5.3 13.5 %collective-permute-start.2 = (bf16[48,1536]{1,0:T(8,128)(2,1)S(1)}, bf16[48,1536]{1,0:T(8,128)(2,1)S(1)}, u32[]{:S(2)}, u32[]{:S(2)}) collective-permute-start(bf16[48,1536]{1,0:T(8,128)(2,1)S(1)} %collective-permute-done), channel_id=1, source_target_pairs={{0,8},{1,9},{2,10},{3,11},{68,76},{69,77},{70,78},{71,79},{136,128... | collective-permute-start | bytes 442376 | tf_op jit(solution)/shard_map/ppermute | solution.py:325
  6.6 12.2 %collective-permute-start.3 = (bf16[48,1536]{1,0:T(8,128)(2,1)S(1)}, bf16[48,1536]{1,0:T(8,128)(2,1)S(1)}, u32[]{:S(2)}, u32[]{:S(2)}) collective-permute-start(bf16[48,1536]{1,0:T(8,128)(2,1)S(1)} %collective-permute-done), channel_id=1, source_target_pairs={{0,12},{1,13},{2,14},{3,15},{68,64},{69,65},{70,66},{71,67},{136,1... | collective-permute-start | bytes 442376 | tf_op jit(solution)/shard_map/ppermute | solution.py:325
  8.5 10.3 %collective-permute-start.5 = (bf16[256,768]{1,0:T(8,128)(2,1)S(1)}, bf16[256,768]{1,0:T(8,128)(2,1)S(1)}, u32[]{:S(2)}, u32[]{:S(2)}) collective-permute-start(bf16[256,768]{1,0:T(8,128)(2,1)S(1)} %pad_maximum_fusion), channel_id=1, source_target_pairs={{0,64},{64,0},{128,192},{192,128},{1,65},{65,1},{129,193},{193,129... | collective-permute-start | bytes 1179656 | tf_op jit(solution)/shard_map/ppermute | solution.py:365
  20.5 42.4 %all-to-all-start = ((bf16[16,48,1536]{2,1,0:T(8,128)(2,1)}), bf16[16,48,1536]{2,1,0:T(8,128)(2,1)S(1)}, u32[]{:S(2)}, u32[]{:S(2)}) async-start(bf16[16,48,1536]{2,1,0:T(8,128)(2,1)} %broadcast_in_dim.15), calls=%async_computation | async-start | bytes 4718592 | tf_op jit(solution)/shard_map/all_to_all | solution.py:346
  27.0 37.6 %copy-start.5 = (bf16[1,768]{1,0:T(2,128)(2,1)S(1)}, bf16[1,768]{1,0:T(2,128)(2,1)}, u32[]{:S(2)}) copy-start(bf16[1,768]{1,0:T(2,128)(2,1)} %param.14) | copy-start | bytes 4612
  27.0 38.5 %copy-start = (bf16[128,768]{1,0:T(8,128)(2,1)S(1)}, bf16[128,768]{1,0:T(8,128)(2,1)}, u32[]{:S(2)}) copy-start(bf16[128,768]{1,0:T(8,128)(2,1)} %cls_ref.1) | copy-start | bytes 589828
  64.4 10.2 %copy-start.4 = (s32[64,1]{0,1:T(1,128)S(1)}, s32[64,1]{0,1:T(1,128)}, u32[]{:S(2)}) copy-start(s32[64,1]{0,1:T(1,128)} %param.13) | copy-start | bytes 772
  64.4 3.2 %collective-permute-start.7 = (bf16[128,768]{1,0:T(8,128)(2,1)}, bf16[128,768]{1,0:T(8,128)(2,1)S(1)}, u32[]{:S(2)}, u32[]{:S(2)}) collective-permute-start(bf16[128,768]{1,0:T(8,128)(2,1)} %get-tuple-element.22), channel_id=1, source_target_pairs={{0,64},{64,0},{128,192},{192,128},{1,65},{65,1},{129,193},{193,129... | collective-permute-start | bytes 589832 | tf_op jit(solution)/shard_map/ppermute | solution.py:370
  67.1 38.8 %copy-start.2 = (bf16[256,768]{1,0:T(8,128)(2,1)S(1)}, bf16[256,768]{1,0:T(8,128)(2,1)}, u32[]{:S(2)}) copy-start(bf16[256,768]{1,0:T(8,128)(2,1)} %stale_ref.1) | copy-start | bytes 1179652
  67.1 58.0 %copy-start.3 = (f32[32,128]{1,0:T(8,128)S(1)}, f32[32,128]{1,0:T(8,128)}, u32[]{:S(2)}) copy-start(f32[32,128]{1,0:T(8,128)} %constant.2.clone.discount_ref) | copy-start | bytes 49156
  67.1 2.5 %collective-permute-start.6 = (bf16[128,768]{1,0:T(8,128)(2,1)S(1)}, bf16[128,768]{1,0:T(8,128)(2,1)S(1)}, u32[]{:S(2)}, u32[]{:S(2)}) collective-permute-start(bf16[128,768]{1,0:T(8,128)(2,1)S(1)} %get-tuple-element.19), channel_id=1, source_target_pairs={{0,64},{64,0},{128,192},{192,128},{1,65},{65,1},{129,193},{193,129... | collective-permute-start | bytes 589832 | tf_op jit(solution)/shard_map/ppermute | solution.py:373
  67.7 6.9 %collective-permute-start.8 = (bf16[128,768]{1,0:T(8,128)(2,1)S(1)}, bf16[128,768]{1,0:T(8,128)(2,1)S(1)}, u32[]{:S(2)}, u32[]{:S(2)}) collective-permute-start(bf16[128,768]{1,0:T(8,128)(2,1)S(1)} %add_convert_fusion), channel_id=1, source_target_pairs={{0,128},{64,192},{128,0},{192,64},{1,129},{65,193},{129,1},{193,65... | collective-permute-start | bytes 589832 | tf_op jit(solution)/shard_map/ppermute | solution.py:371
  157.0 1.0 copy-start.1

commit v4 on v3

--- a/solution.py
+++ b/solution.py
@@ -26,42 +26,77 @@
     return lax.dot_general(a, b, (((1,), (1,)), ((), ())), preferred_element_type=f32)
 
 
-def encode_kernel(kept_x_ref, sent_x_ref, w_ref, kept_ref, sent_ref):
-    width = kept_ref.shape[1]
-    for x_ref, out_ref in ((sent_x_ref, sent_ref), (kept_x_ref, kept_ref)):
-        inner = contract_last(x_ref[...], w_ref[:, :width])
-        hidden = 0.5 * inner * (1.0 + lax.erf(inner * math.sqrt(0.5)))
-        part = jnp.dot(hidden.astype(bf16), w_ref[:, width:], preferred_element_type=f32)
-        out_ref[...] = part.astype(out_ref.dtype)
-
-
-def encode(kept_x, sent_x, projections):
-    return pl.pallas_call(
-        encode_kernel,
-        out_shape=(
-            jax.ShapeDtypeStruct(kept_x.shape, f32),
-            jax.ShapeDtypeStruct(sent_x.shape, bf16),
-        ),
+def partial_sums(x, w_ref):
+    width = x.shape[1]
+    inner = contract_last(x, w_ref[:, :width])
+    hidden = 0.5 * inner * (1.0 + lax.erf(inner * math.sqrt(0.5)))
+    return jnp.dot(hidden.astype(bf16), w_ref[:, width:], preferred_element_type=f32)
+
+
+def first_kernel(own_ref, across_ref, along_ref, diagonal_ref, w_ref, out_ref):
+    for n, x_ref in enumerate((own_ref, across_ref, along_ref, diagonal_ref)):
+        out_ref[n] = partial_sums(x_ref[...], w_ref)
+
+
+def first_half(xs, units):
+    return pl.pallas_call(
+        first_kernel,
+        out_shape=jax.ShapeDtypeStruct((len(xs),) + xs[0].shape, f32),
         compiler_params=params(),
         name="encode",
-    )(kept_x, sent_x, projections)
+    )(*xs, units)
+
+
+def second_kernel(
+    own_ref,
+    across_ref,
+    along_ref,
+    diagonal_ref,
+    w_ref,
+    so_far_ref,
+    kept_ref,
+    later_ref,
+    send_across_ref,
+    send_along_ref,
+):
+    half = own_ref.shape[0] // 2
+    diagonal = so_far_ref[3] + partial_sums(diagonal_ref[...], w_ref)
+    across = so_far_ref[1] + partial_sums(across_ref[...], w_ref)
+    send_across_ref[:half] = across[:half].astype(bf16)
+    send_across_ref[half:] = diagonal[:half].astype(bf16)
+    along = so_far_ref[2] + partial_sums(along_ref[...], w_ref)
+    send_along_ref[:half] = along[half:].astype(bf16)
+    send_along_ref[half:] = diagonal[half:].astype(bf16)
+    later_ref[:half] = along[:half]
+    later_ref[half:] = across[half:]
+    kept_ref[...] = so_far_ref[0] + partial_sums(own_ref[...], w_ref)
+
+
+def second_half(xs, units, so_far):
+    kept = jax.ShapeDtypeStruct(xs[0].shape, f32)
+    sent = jax.ShapeDtypeStruct(xs[0].shape, bf16)
+    return pl.pallas_call(
+        second_kernel,
+        out_shape=(kept, kept, sent, sent),
+        compiler_params=params(),
+        name="encode_rest",
+    )(*xs, units, so_far)
 
 
 ROWS = 32
 
 
-def place_kernel(cls_ref, own_ref, near_ref, far_ref, owner_ref, query_ref, out_ref):
+def place_kernel(
+    cls_ref, kept_ref, across_ref, along_ref, last_ref, owner_ref, query_ref, out_ref
+):
     rows, width = cls_ref.shape
+    half = rows // 2
     blocks = owner_ref.shape[1]
     total = out_ref.shape[0]
     shards = total // ROWS
     chunks = width // LANES
-    resid = (
-        cls_ref[...].astype(f32)
-        + own_ref[...]
-        + near_ref[...].astype(f32)
-        + far_ref[...].astype(f32)
-    )
+    early = jnp.concatenate((across_ref[:half], along_ref[:half]), 0).astype(f32)
+    resid = cls_ref[...].astype(f32) + kept_ref[...] + early + last_ref[...].astype(f32)
     centred = resid - jnp.mean(resid, -1, keepdims=True)
     variance = jnp.mean(centred * centred, -1, keepdims=True)
     fresh = (centred * lax.rsqrt(variance + EPSILON)).astype(bf16)
@@ -98,13 +133,13 @@
     out_ref[...] = jnp.where(filled > 0.5, placed, rest.reshape(total, LANES)).astype(bf16)
 
 
-def place(cls_states, own, near, far, owner, query, shards):
+def place(cls_states, kept, across, along, last, owner, query, shards):
     return pl.pallas_call(
         place_kernel,
         out_shape=jax.ShapeDtypeStruct((shards * ROWS, LANES), bf16),
         compiler_params=params(),
         name="place",
-    )(cls_states, own, near, far, owner, query)
+    )(cls_states, kept, across, along, last, owner, query)
 
 
 def score_kernel(recv_ref, stale_ref, idsg_ref, refreshed_ref, packed_ref, recv_s, arrived_s):
@@ -307,9 +342,50 @@
     ]
 
 
-def current_projections(trainer_in, trainer_out):
+def gather_units(block):
+    groups = [
+        [shard_at(y, zz, zl, x) for y in range(Y) for x in range(X)]
+        for zz in range(ZZ)
+        for zl in range(ZL)
+    ]
+    parts = len(groups[0])
+    units, width = block.shape
+    gathered = lax.all_to_all(
+        jnp.broadcast_to(block[None], (parts, units, width)),
+        "shard",
+        split_axis=0,
+        concat_axis=0,
+        tiled=True,
+        axis_index_groups=groups,
+    )
+    return gathered.reshape(parts * units, width)
+
+
+def per_device(
+    cls_states, trainer_in, trainer_out, stale_cache, block_owner, queries, neg_ids, grades
+):
+    shards = lax.axis_size("shard")
     roles = lax.axis_size("role")
-    shards = lax.axis_size("shard")
+    passages, width = cls_states.shape
+    half = passages // 2
+    barrier = lax.optimization_barrier
+
+    def to_core(v):
+        return lax.ppermute(v, "role", [(0, 1), (1, 0), (2, 3), (3, 2)])
+
+    def to_across(v):
+        return lax.ppermute(v, "role", [(0, 2), (1, 3), (2, 0), (3, 1)])
+
+    def to_along(v):
+        return lax.ppermute(
+            v,
+            "shard",
+            [
+                (shard_at(y, zz, zl, x), shard_at(y, zz, 1 - zl, x))
+                for y, zz, zl, x in everywhere()
+            ],
+        )
+
     axes = ("role", "shard")
     mine = jnp.concatenate((trainer_in[0], trainer_out[0]), 1)
     mine = lax.ppermute(
@@ -320,6 +396,7 @@
             for y, zz, zl, x in everywhere()
         ],
     )
+    mine, cls_after = barrier((mine, cls_states))
     block = mine
     for by in range(1, ZZ):
         block = block + lax.ppermute(
@@ -333,44 +410,19 @@
                 for y, zz, zl, x in everywhere()
             ],
         )
-    return block
-
-
-def gather_units(block):
-    groups = [
-        [shard_at(y, zz, zl, x) for zl in range(ZL) for y in range(Y) for x in range(X)]
-        for zz in range(ZZ)
-    ]
-    parts = len(groups[0])
-    units, width = block.shape
-    gathered = lax.all_to_all(
-        jnp.broadcast_to(block[None], (parts, units, width)),
-        "shard",
-        split_axis=0,
-        concat_axis=0,
-        tiled=True,
-        axis_index_groups=groups,
-    )
-    return gathered.reshape(parts * units, width)
-
-
-def per_device(
-    cls_states, trainer_in, trainer_out, stale_cache, block_owner, queries, neg_ids, grades
-):
-    shards = lax.axis_size("shard")
-    passages, width = cls_states.shape
-    near = [(0, 1), (1, 0), (2, 3), (3, 2)]
-    across = [(0, 2), (1, 3), (2, 0), (3, 1)]
-    x_across = lax.ppermute(cls_states, "role", across)
-    x_others = lax.ppermute(jnp.concatenate((cls_states, x_across), 0), "role", near)
-    block = current_projections(trainer_in, trainer_out)
-    block, x_across, x_others = lax.optimization_barrier((block, x_across, x_others))
-    projections = gather_units(block)
-    far, for_far = encode(x_across, x_others[passages:], projections)
-    to_far = (far + lax.ppermute(for_far, "role", near).astype(f32)).astype(bf16)
-    from_far = lax.ppermute(to_far, "role", across)
-    own, for_near = encode(cls_states, x_others[:passages], projections)
-    from_near = lax.ppermute(for_near, "role", near)
+    x_across = to_across(cls_after)
+    block, x_across, cls_after = barrier((block, x_across, cls_after))
+    units = gather_units(block)
+    xs = (cls_states, x_across, to_along(cls_after), to_along(x_across))
+    units, xs = barrier((units, xs))
+    other_units = to_core(units)
+    so_far = first_half(xs, units)
+    kept, later, for_across, for_along = second_half(xs, other_units, so_far)
+    from_across = to_across(for_across)
+    from_along = to_along(for_along)
+    then_along = (later[:half] + from_across[half:].astype(f32)).astype(bf16)
+    then_across = (later[half:] + from_along[half:].astype(f32)).astype(bf16)
+    last = jnp.concatenate((to_along(then_along), to_across(then_across)), 0)
     chunks = width // LANES
     rest = jnp.concatenate(
         (
@@ -382,7 +434,7 @@
     )
     idsg = jnp.concatenate((neg_ids, grades), 1)
     outgoing = place(
-        cls_states, own, from_near, from_far, block_owner.reshape(1, -1), rest, shards
+        cls_states, kept, from_across, from_along, last, block_owner.reshape(1, -1), rest, shards
     )
     outgoing, idsg = lax.optimization_barrier((outgoing, idsg))
     arrived = lax.all_to_all(

time: 178 us -> 162 us (0.910)
  waiting for transfers between devices: 48.2 us -> 27.6 us
  starting transfers between devices: 17.8 us -> 28.8 us
  blocking collectives: 79.3 us -> 73.6 us
    all_to_all x1, waiting for transfers between devices: 35.8 us -> 7.7 us  [gather_units(): lax.all_to_all(jnp.broadcast_to(block[None], (parts, units, width)), 'sha...]
    ppermute x9 -> x12, starting transfers between devices: 11.4 us -> 22.7 us  [the longest x3 11.2 us: to_across(): return lax.ppermute(v, 'role', [(0, 2), (1, 3), (2, 0), (3, 1)])]
    ppermute x9 -> x12, waiting for transfers between devices: 12.4 us -> 19.9 us  [the longest x4 8.93 us: to_along(): lax.ppermute(v, 'shard', [(shard_at(y, zz, zl, x), shard_at(y, zz, 1 - zl...]
    all_to_all x1, blocking collectives: 29.7 us -> 24.2 us  [per_device(): lax.all_to_all(outgoing.reshape(shards, ROWS, LANES), 'shard', split_axis...]
  transfers between devices with their start and end apart: 10 -> 13, of which waited for: 4 -> 10; matrix products, arithmetic and copies ran while one was open for 2% -> 0% of each run, Pallas kernels for 1% -> 1%
where the time goes in v4:
time: 162 us; the launch traced here: 160 us
  blocking collectives  73.6 us (45%)
  starting transfers between devices  28.8 us (18%)
  waiting for transfers between devices  27.6 us (17%)
  Pallas kernels  25.2 us (16%)
  local copies, waits for them, and re-layouts  3.06 us (2%)
    all_to_all x1, blocking collectives, per_device(): lax.all_to_all(outgoing.reshape(shards, ROWS, LANES), 'shard', split_axis...  24.2 us
    all_to_all x1, blocking collectives, per_device(): lax.all_to_all(packed, 'shard', split_axis=0, concat_axis=0, tiled=True)  17.6 us
    all_to_all x1, blocking collectives, per_device(): lax.all_to_all(shares, 'shard', split_axis=0, concat_axis=0, tiled=True)  16.2 us
    pallas_call x1, Pallas kernels, pair(): pl.pallas_call(pair_kernel, out_shape=(jax.ShapeDtypeStruct(x.shape, f32)...  16.1 us
    all_to_all x1, blocking collectives, per_device(): lax.all_to_all(grads, 'shard', split_axis=0, concat_axis=0, tiled=True)  15.6 us
    ppermute x3, starting transfers between devices, to_across(): return lax.ppermute(v, 'role', [(0, 2), (1, 3), (2, 0), (3, 1)])  11.2 us
    ppermute x4, waiting for transfers between devices, to_along(): lax.ppermute(v, 'shard', [(shard_at(y, zz, zl, x), shard_at(y, zz, 1 - zl...  8.93 us
    all_to_all x1, waiting for transfers between devices, gather_units(): lax.all_to_all(jnp.broadcast_to(block[None], (parts, units, width)), 'sha...  7.7 us
  transfers between devices with their start and end apart: 13, of which 10 were waited for; matrix products, arithmetic and copies ran while one was open for 0% of the time, Pallas kernels for 1%

profile of v4, /device:TPU:2, one launch (start us, length us, event | category | flops | bytes accessed | tf_op | source)
XLA Modules:
  0.0 160.4 jit_solution(8730529651678193559)
XLA Ops:
  0.6 0.9 pad_maximum_fusion.1
  1.6 0.7 collective-permute-start
  2.3 0.7 collective-permute-start.3
  2.9 1.3 collective-permute-start.2
  4.2 0.7 collective-permute-start.1
  4.9 9.4 %collective-permute-start.4 = (bf16[128,768]{1,0:T(8,128)(2,1)}, bf16[128,768]{1,0:T(8,128)(2,1)S(1)}, u32[]{:S(2)}, u32[]{:S(2)}) collective-permute-start(bf16[128,768]{1,0:T(8,128)(2,1)} %cls_ref.1), channel_id=1, source_target_pairs={{0,128},{64,192},{128,0},{192,64},{1,129},{65,193},{129,1},{193,65... | collective-permute-start | bytes 589832 | tf_op jit(solution)/shard_map/ppermute | solution.py:377
  14.3 3.6 %collective-permute-done.2 = bf16[48,1536]{1,0:T(8,128)(2,1)S(1)} collective-permute-done((bf16[48,1536]{1,0:T(8,128)(2,1)S(1)}, bf16[48,1536]{1,0:T(8,128)(2,1)S(1)}, u32[]{:S(2)}, u32[]{:S(2)}) %collective-permute-start.2) | collective-permute-done | bytes 147488 | tf_op jit(solution)/shard_map/ppermute | solution.py:402
  18.2 1.1 broadcast_in_dim.15
  19.3 6.1 %all-to-all-start = ((bf16[8,48,1536]{2,1,0:T(8,128)(2,1)}), bf16[8,48,1536]{2,1,0:T(8,128)(2,1)S(1)}, u32[]{:S(2)}, u32[]{:S(2)}) async-start(bf16[8,48,1536]{2,1,0:T(8,128)(2,1)} %broadcast_in_dim.15), calls=%async_computation | async-start | bytes 2359296 | tf_op jit(solution)/shard_map/all_to_all | solution.py:353
  25.4 1.6 %collective-permute-start.5 = (bf16[128,768]{1,0:T(8,128)(2,1)S(1)}, bf16[128,768]{1,0:T(8,128)(2,1)S(1)}, u32[]{:S(2)}, u32[]{:S(2)}) collective-permute-start(bf16[128,768]{1,0:T(8,128)(2,1)S(1)} %copy-done), channel_id=1, source_target_pairs={{0,2},{1,3},{2,0},{3,1},{4,6},{5,7},{6,4},{7,5},{8,10},{9,11},{10,... | collective-permute-start | bytes 589832 | tf_op jit(solution)/shard_map/ppermute | solution.py:380
  27.6 3.6 %collective-permute-done.5.along_ref = bf16[128,768]{1,0:T(8,128)(2,1)S(1)} collective-permute-done((bf16[128,768]{1,0:T(8,128)(2,1)S(1)}, bf16[128,768]{1,0:T(8,128)(2,1)S(1)}, u32[]{:S(2)}, u32[]{:S(2)}) %collective-permute-start.5) | collective-permute-done | bytes 196640 | tf_op jit(solution)/shard_map/ppermute | solution.py:380
  31.2 3.5 %collective-permute-done.6.diagonal_ref = bf16[128,768]{1,0:T(8,128)(2,1)S(1)} collective-permute-done((bf16[128,768]{1,0:T(8,128)(2,1)S(1)}, bf16[128,768]{1,0:T(8,128)(2,1)S(1)}, u32[]{:S(2)}, u32[]{:S(2)}) %collective-permute-start.6) | collective-permute-done | bytes 196640 | tf_op jit(solution)/shard_map/ppermute | solution.py:380
  34.7 7.7 %all-to-all-done = bf16[8,48,1536]{2,1,0:T(8,128)(2,1)S(1)} async-done(((bf16[8,48,1536]{2,1,0:T(8,128)(2,1)}), bf16[8,48,1536]{2,1,0:T(8,128)(2,1)S(1)}, u32[]{:S(2)}, u32[]{:S(2)}) %all-to-all-start) | async-done | bytes 1179680 | tf_op jit(solution)/shard_map/all_to_all | solution.py:353
  42.4 2.9 %collective-permute-start.7 = (bf16[384,1536]{1,0:T(8,128)(2,1)S(1)}, bf16[384,1536]{1,0:T(8,128)(2,1)S(1)}, u32[]{:S(2)}, u32[]{:S(2)}) collective-permute-start(bf16[384,1536]{1,0:T(8,128)(2,1)S(1)} %bitcast.18), channel_id=1, source_target_pairs={{0,64},{64,0},{128,192},{192,128},{1,65},{65,1},{129,193},{193,129... | collective-permute-start | bytes 3538952 | tf_op jit(solution)/shard_map/ppermute | solution.py:374
  45.4 2.0 %encode.1.so_far_ref = f32[4,128,768]{2,1,0:T(8,128)S(1)} custom-call(bf16[128,768]{1,0:T(8,128)(2,1)S(1)} %copy-done, bf16[128,768]{1,0:T(8,128)(2,1)S(1)} %collective-permute-done.4.across_ref, bf16[128,768]{1,0:T(8,128)(2,1)S(1)} %collective-permute-done.5.along_ref, bf16[128,768]{1,0:T(8,128)(2,1)S(1)} %collective-permute-done.6.diagonal_ref, ...), custom_call_target="tpu_custom_call" | custom-call | tf_op jit(solution)/shard_map/encode/pallas_call | solution.py:42
  47.8 2.0 %encode_rest.1 = (f32[128,768]{1,0:T(8,128)S(1)}, f32[128,768]{1,0:T(8,128)S(1)}, bf16[128,768]{1,0:T(8,128)(2,1)S(1)}, bf16[128,768]{1,0:T(8,128)(2,1)S(1)}) custom-call(bf16[128,768]{1,0:T(8,128)(2,1)S(1)} %copy-done, bf16[128,768]{1,0:T(8,128)(2,1)S(1)} %collective-permute-done.4.across_ref, bf16[128,768]{1,0:T(8,128)(2,1)S(1)} %collective-permute-done.5.along_ref, ...), custom_call_target="tpu_custom_call" | custom-call | tf_op jit(solution)/shard_map/encode_rest/pallas_call | solution.py:78
  49.9 1.6 %collective-permute-start.9 = (bf16[128,768]{1,0:T(8,128)(2,1)S(1)}, bf16[128,768]{1,0:T(8,128)(2,1)S(1)}, u32[]{:S(2)}, u32[]{:S(2)}) collective-permute-start(bf16[128,768]{1,0:T(8,128)(2,1)S(1)} %get-tuple-element.35), channel_id=1, source_target_pairs={{0,2},{1,3},{2,0},{3,1},{4,6},{5,7},{6,4},{7,5},{8,10},{9,11},{10,... | collective-permute-start | bytes 589832 | tf_op jit(solution)/shard_map/ppermute | solution.py:380
  51.6 5.5 %collective-permute-done.8.across_ref = bf16[128,768]{1,0:T(8,128)(2,1)S(1)} collective-permute-done((bf16[128,768]{1,0:T(8,128)(2,1)S(1)}, bf16[128,768]{1,0:T(8,128)(2,1)S(1)}, u32[]{:S(2)}, u32[]{:S(2)}) %collective-permute-start.8) | collective-permute-done | bytes 196640 | tf_op jit(solution)/shard_map/ppermute | solution.py:377
  57.2 1.7 %collective-permute-start.11 = (bf16[64,768]{1,0:T(8,128)(2,1)S(1)}, bf16[64,768]{1,0:T(8,128)(2,1)S(1)}, u32[]{:S(2)}, u32[]{:S(2)}) collective-permute-start(bf16[64,768]{1,0:T(8,128)(2,1)S(1)} %get-tuple-element.44), channel_id=1, source_target_pairs={{0,128},{64,192},{128,0},{192,64},{1,129},{65,193},{129,1},{193,65... | collective-permute-start | bytes 294920 | tf_op jit(solution)/shard_map/ppermute | solution.py:377
  59.0 1.5 collective-permute-start.10
  60.6 1.4 collective-permute-done.11
  61.9 1.6 %collective-permute-done.10 = bf16[64,768]{1,0:T(8,128)(2,1)S(1)} collective-permute-done((bf16[64,768]{1,0:T(8,128)(2,1)S(1)}, bf16[64,768]{1,0:T(8,128)(2,1)S(1)}, u32[]{:S(2)}, u32[]{:S(2)}) %collective-permute-start.10) | collective-permute-done | bytes 98336 | tf_op jit(solution)/shard_map/ppermute | solution.py:380
  63.6 1.5 place.1
  65.2 24.2 %all_to_all.41 = bf16[64,32,128]{2,1,0:T(8,128)(2,1)S(1)} all-to-all(bf16[64,32,128]{2,1,0:T(8,128)(2,1)S(1)} %bitcast.20), channel_id=1, replica_groups=mesh['role'=4,'shard'=64] {'shard'}, dimensions={0} | all-to-all | bytes 1048576 | tf_op jit(solution)/shard_map/all_to_all | solution.py:440
  89.4 1.6 score.1
  91.0 17.6 %all_to_all.42 = f32[64,1,128]{2,1,0:T(1,128)S(1)} all-to-all(f32[64,1,128]{2,1,0:T(1,128)S(1)} %bitcast.26), channel_id=1, replica_groups=mesh['role'=4,'shard'=64] {'shard'}, dimensions={0} | all-to-all | bytes 65536 | tf_op jit(solution)/shard_map/all_to_all | solution.py:444
  108.5 16.1 %pair.1 = (f32[64,128]{1,0:T(8,128)S(1)}, f32[1,128]{1,0:T(1,128)}) custom-call(f32[64,128]{1,0:T(8,128)S(1)} %bitcast.24, f32[32,128]{1,0:T(8,128)S(1)} %copy-done.3), custom_call_target="tpu_custom_call" | custom-call | tf_op jit(solution)/shard_map/pair/pallas_call | solution.py:276
  124.6 15.6 %all_to_all.43 = f32[64,1,128]{2,1,0:T(1,128)S(1)} all-to-all(f32[64,1,128]{2,1,0:T(1,128)S(1)} %bitcast.25), channel_id=1, replica_groups=mesh['role'=4,'shard'=64] {'shard'}, dimensions={0} | all-to-all | bytes 65536 | tf_op jit(solution)/shard_map/all_to_all | solution.py:449
  140.3 1.0 copy-done.1
  141.3 2.0 %share.1 = f32[64,768]{1,0:T(8,128)S(1)} custom-call(f32[64,128]{1,0:T(8,128)S(1)} %bitcast.23, s32[64,128]{1,0:T(8,128)S(1)} %pad_add_fusion.idsg_ref, bf16[256,768]{1,0:T(8,128)(2,1)S(1)} %copy-done.1), custom_call_target="tpu_custom_call" | custom-call | tf_op jit(solution)/shard_map/share/pallas_call | solution.py:323
  143.5 16.2 %all_to_all.44 = f32[64,1,768]{2,1,0:T(1,128)S(1)} all-to-all(f32[64,1,768]{2,1,0:T(1,128)S(1)} %copy.14), channel_id=1, replica_groups=mesh['role'=4,'shard'=64] {'shard'}, dimensions={0} | all-to-all | bytes 393216 | tf_op jit(solution)/shard_map/all_to_all | solution.py:451
  159.8 0.6 broadcast_in_dim.18
  (35 shorter events, 2.0 us)
Async XLA Ops:
  1.6 0.7 collective-permute-start
  2.3 12.0 %collective-permute-start.3 = (bf16[48,1536]{1,0:T(8,128)(2,1)S(1)}, bf16[48,1536]{1,0:T(8,128)(2,1)S(1)}, u32[]{:S(2)}, u32[]{:S(2)}) collective-permute-start(bf16[48,1536]{1,0:T(8,128)(2,1)S(1)} %collective-permute-done), channel_id=1, source_target_pairs={{0,12},{1,13},{2,14},{3,15},{68,64},{69,65},{70,66},{71,67},{136,1... | collective-permute-start | bytes 442376 | tf_op jit(solution)/shard_map/ppermute | solution.py:402
  2.9 15.0 %collective-permute-start.2 = (bf16[48,1536]{1,0:T(8,128)(2,1)S(1)}, bf16[48,1536]{1,0:T(8,128)(2,1)S(1)}, u32[]{:S(2)}, u32[]{:S(2)}) collective-permute-start(bf16[48,1536]{1,0:T(8,128)(2,1)S(1)} %collective-permute-done), channel_id=1, source_target_pairs={{0,8},{1,9},{2,10},{3,11},{68,76},{69,77},{70,78},{71,79},{136,128... | collective-permute-start | bytes 442376 | tf_op jit(solution)/shard_map/ppermute | solution.py:402
  4.2 13.7 %collective-permute-start.1 = (bf16[48,1536]{1,0:T(8,128)(2,1)S(1)}, bf16[48,1536]{1,0:T(8,128)(2,1)S(1)}, u32[]{:S(2)}, u32[]{:S(2)}) collective-permute-start(bf16[48,1536]{1,0:T(8,128)(2,1)S(1)} %collective-permute-done), channel_id=1, source_target_pairs={{0,4},{1,5},{2,6},{3,7},{68,72},{69,73},{70,74},{71,75},{136,140},... | collective-permute-start | bytes 442376 | tf_op jit(solution)/shard_map/ppermute | solution.py:402
  4.9 13.2 %collective-permute-start.4 = (bf16[128,768]{1,0:T(8,128)(2,1)}, bf16[128,768]{1,0:T(8,128)(2,1)S(1)}, u32[]{:S(2)}, u32[]{:S(2)}) collective-permute-start(bf16[128,768]{1,0:T(8,128)(2,1)} %cls_ref.1), channel_id=1, source_target_pairs={{0,128},{64,192},{128,0},{192,64},{1,129},{65,193},{129,1},{193,65... | collective-permute-start | bytes 589832 | tf_op jit(solution)/shard_map/ppermute | solution.py:377
  19.3 6.1 %copy-start = (bf16[128,768]{1,0:T(8,128)(2,1)S(1)}, bf16[128,768]{1,0:T(8,128)(2,1)}, u32[]{:S(2)}) copy-start(bf16[128,768]{1,0:T(8,128)(2,1)} %cls_ref.1) | copy-start | bytes 589828
  19.3 26.1 %copy-start.7 = (bf16[1,768]{1,0:T(2,128)(2,1)S(1)}, bf16[1,768]{1,0:T(2,128)(2,1)}, u32[]{:S(2)}) copy-start(bf16[1,768]{1,0:T(2,128)(2,1)} %param.14) | copy-start | bytes 4612
  19.3 23.1 %all-to-all-start = ((bf16[8,48,1536]{2,1,0:T(8,128)(2,1)}), bf16[8,48,1536]{2,1,0:T(8,128)(2,1)S(1)}, u32[]{:S(2)}, u32[]{:S(2)}) async-start(bf16[8,48,1536]{2,1,0:T(8,128)(2,1)} %broadcast_in_dim.15), calls=%async_computation | async-start | bytes 2359296 | tf_op jit(solution)/shard_map/all_to_all | solution.py:353
  25.4 5.8 %collective-permute-start.5 = (bf16[128,768]{1,0:T(8,128)(2,1)S(1)}, bf16[128,768]{1,0:T(8,128)(2,1)S(1)}, u32[]{:S(2)}, u32[]{:S(2)}) collective-permute-start(bf16[128,768]{1,0:T(8,128)(2,1)S(1)} %copy-done), channel_id=1, source_target_pairs={{0,2},{1,3},{2,0},{3,1},{4,6},{5,7},{6,4},{7,5},{8,10},{9,11},{10,... | collective-permute-start | bytes 589832 | tf_op jit(solution)/shard_map/ppermute | solution.py:380
  27.1 7.7 %collective-permute-start.6 = (bf16[128,768]{1,0:T(8,128)(2,1)S(1)}, bf16[128,768]{1,0:T(8,128)(2,1)S(1)}, u32[]{:S(2)}, u32[]{:S(2)}) collective-permute-start(bf16[128,768]{1,0:T(8,128)(2,1)S(1)} %collective-permute-done.4.across_ref), channel_id=1, source_target_pairs={{0,2},{1,3},{2,0},{3,1},{4,6},{5,7},{6,4},{7,5},{8,10},{9,11},{10,... | collective-permute-start | bytes 589832 | tf_op jit(solution)/shard_map/ppermute | solution.py:380
  42.4 5.4 %collective-permute-start.7 = (bf16[384,1536]{1,0:T(8,128)(2,1)S(1)}, bf16[384,1536]{1,0:T(8,128)(2,1)S(1)}, u32[]{:S(2)}, u32[]{:S(2)}) collective-permute-start(bf16[384,1536]{1,0:T(8,128)(2,1)S(1)} %bitcast.18), channel_id=1, source_target_pairs={{0,64},{64,0},{128,192},{192,128},{1,65},{65,1},{129,193},{193,129... | collective-permute-start | bytes 3538952 | tf_op jit(solution)/shard_map/ppermute | solution.py:374
  47.4 13.0 %copy-start.5 = (s32[64,64]{1,0:T(8,128)S(1)}, s32[64,64]{1,0:T(8,128)}, u32[]{:S(2)}) copy-start(s32[64,64]{1,0:T(8,128)} %param.16) | copy-start | bytes 49156
  47.5 13.0 %copy-start.6 = (s32[64,64]{1,0:T(8,128)S(1)}, s32[64,64]{1,0:T(8,128)}, u32[]{:S(2)}) copy-start(s32[64,64]{1,0:T(8,128)} %param.15) | copy-start | bytes 49156
  49.8 13.8 %copy-start.4 = (s32[64,1]{0,1:T(1,128)S(1)}, s32[64,1]{0,1:T(1,128)}, u32[]{:S(2)}) copy-start(s32[64,1]{0,1:T(1,128)} %param.13) | copy-start | bytes 772
  49.8 7.3 %collective-permute-start.8 = (bf16[128,768]{1,0:T(8,128)(2,1)S(1)}, bf16[128,768]{1,0:T(8,128)(2,1)S(1)}, u32[]{:S(2)}, u32[]{:S(2)}) collective-permute-start(bf16[128,768]{1,0:T(8,128)(2,1)S(1)} %get-tuple-element.34), channel_id=1, source_target_pairs={{0,128},{64,192},{128,0},{192,64},{1,129},{65,193},{129,1},{193,65... | collective-permute-start | bytes 589832 | tf_op jit(solution)/shard_map/ppermute | solution.py:377
  49.9 7.3 %collective-permute-start.9 = (bf16[128,768]{1,0:T(8,128)(2,1)S(1)}, bf16[128,768]{1,0:T(8,128)(2,1)S(1)}, u32[]{:S(2)}, u32[]{:S(2)}) collective-permute-start(bf16[128,768]{1,0:T(8,128)(2,1)S(1)} %get-tuple-element.35), channel_id=1, source_target_pairs={{0,2},{1,3},{2,0},{3,1},{4,6},{5,7},{6,4},{7,5},{8,10},{9,11},{10,... | collective-permute-start | bytes 589832 | tf_op jit(solution)/shard_map/ppermute | solution.py:380
  57.2 4.7 %collective-permute-start.11 = (bf16[64,768]{1,0:T(8,128)(2,1)S(1)}, bf16[64,768]{1,0:T(8,128)(2,1)S(1)}, u32[]{:S(2)}, u32[]{:S(2)}) collective-permute-start(bf16[64,768]{1,0:T(8,128)(2,1)S(1)} %get-tuple-element.44), channel_id=1, source_target_pairs={{0,128},{64,192},{128,0},{192,64},{1,129},{65,193},{129,1},{193,65... | collective-permute-start | bytes 294920 | tf_op jit(solution)/shard_map/ppermute | solution.py:377
  59.0 4.6 %collective-permute-start.10 = (bf16[64,768]{1,0:T(8,128)(2,1)S(1)}, bf16[64,768]{1,0:T(8,128)(2,1)S(1)}, u32[]{:S(2)}, u32[]{:S(2)}) collective-permute-start(bf16[64,768]{1,0:T(8,128)(2,1)S(1)} %get-tuple-element.43), channel_id=1, source_target_pairs={{0,2},{1,3},{2,0},{3,1},{4,6},{5,7},{6,4},{7,5},{8,10},{9,11},{10,... | collective-permute-start | bytes 294920 | tf_op jit(solution)/shard_map/ppermute | solution.py:380
  63.6 25.8 %copy-start.2 = (bf16[256,768]{1,0:T(8,128)(2,1)S(1)}, bf16[256,768]{1,0:T(8,128)(2,1)}, u32[]{:S(2)}) copy-start(bf16[256,768]{1,0:T(8,128)(2,1)} %stale_ref.1) | copy-start | bytes 1179652
  65.2 43.4 %copy-start.3 = (f32[32,128]{1,0:T(8,128)S(1)}, f32[32,128]{1,0:T(8,128)}, u32[]{:S(2)}) copy-start(f32[32,128]{1,0:T(8,128)} %constant.2.clone.discount_ref) | copy-start | bytes 49156
  140.3 1.0 copy-start.1

commit v5 on v4

--- a/solution.py
+++ b/solution.py
@@ -142,7 +142,9 @@
     )(cls_states, kept, across, along, last, owner, query)
 
 
-def score_kernel(recv_ref, stale_ref, idsg_ref, refreshed_ref, packed_ref, recv_s, arrived_s):
+def score_kernel(
+    recv_ref, stale_ref, idsg_ref, refreshed_ref, again_ref, packed_ref, recv_s, arrived_s
+):
     cache_rows, width = stale_ref.shape
     shards = recv_ref.shape[0] // ROWS
     chunks = width // LANES
@@ -159,6 +161,7 @@
     arrived = jnp.concatenate([arrived_s[j] for j in range(chunks)], 1)
     refreshed = jnp.where(arrived > 0.5 * EMPTY, stale_ref[...].astype(f32), arrived).astype(bf16)
     refreshed_ref[...] = refreshed
+    again_ref[...] = refreshed
     scores = contract_last(queries, refreshed)
     ids = idsg_ref[...]
     lane = lax.broadcasted_iota(jnp.int32, ids.shape, 1)
@@ -174,6 +177,7 @@
     return pl.pallas_call(
         score_kernel,
         out_shape=(
+            jax.ShapeDtypeStruct(stale.shape, bf16),
             jax.ShapeDtypeStruct(stale.shape, bf16),
             jax.ShapeDtypeStruct(idsg.shape, f32),
         ),
@@ -386,32 +390,25 @@
             ],
         )
 
-    axes = ("role", "shard")
+    x_across = to_across(cls_states)
     mine = jnp.concatenate((trainer_in[0], trainer_out[0]), 1)
-    mine = lax.ppermute(
-        mine,
-        axes,
-        [
-            ((roles - 1) * shards + shard_at(y, zz, zl, x), zz * shards + shard_at(y, zz, zl, x))
-            for y, zz, zl, x in everywhere()
+    mine = lax.all_to_all(
+        mine.reshape(roles, -1, 2 * width), "role", split_axis=0, concat_axis=0, tiled=True
+    )[roles - 1]
+    block = lax.all_to_all(
+        jnp.broadcast_to(mine[None], (ZZ,) + mine.shape),
+        "shard",
+        split_axis=0,
+        concat_axis=0,
+        tiled=True,
+        axis_index_groups=[
+            [shard_at(y, zz, zl, x) for zz in range(ZZ)]
+            for y in range(Y)
+            for zl in range(ZL)
+            for x in range(X)
         ],
-    )
-    mine, cls_after = barrier((mine, cls_states))
-    block = mine
-    for by in range(1, ZZ):
-        block = block + lax.ppermute(
-            mine,
-            axes,
-            [
-                (
-                    zz * shards + shard_at(y, zz, zl, x),
-                    zz * shards + shard_at(y, (zz + by) % ZZ, zl, x),
-                )
-                for y, zz, zl, x in everywhere()
-            ],
-        )
-    x_across = to_across(cls_after)
-    block, x_across, cls_after = barrier((block, x_across, cls_after))
+    ).reshape(-1, 2 * width)
+    block, x_across, cls_after = barrier((block, x_across, cls_states))
     units = gather_units(block)
     xs = (cls_states, x_across, to_along(cls_after), to_along(x_across))
     units, xs = barrier((units, xs))
@@ -440,14 +437,14 @@
     arrived = lax.all_to_all(
         outgoing.reshape(shards, ROWS, LANES), "shard", split_axis=0, concat_axis=0, tiled=True
     )
-    refreshed, packed = score(arrived.reshape(-1, LANES), stale_cache, idsg)
+    refreshed, again, packed = score(arrived.reshape(-1, LANES), stale_cache, idsg)
     packed = lax.all_to_all(packed, "shard", split_axis=0, concat_axis=0, tiled=True)
     count = shards * neg_ids.shape[1]
     position = np.arange(1, count + 1, dtype=np.float64)
     discount = (1.0 / np.log2(1.0 + position)).astype(np.float32).reshape(-1, LANES)
     grads, loss = pair(packed, jnp.asarray(discount))
     grads = lax.all_to_all(grads, "shard", split_axis=0, concat_axis=0, tiled=True)
-    shares = share(grads, idsg, refreshed)
+    shares = share(grads, idsg, again)
     shares = lax.all_to_all(shares, "shard", split_axis=0, concat_axis=0, tiled=True)
     return refreshed, jnp.sum(shares, 0, keepdims=True), loss[0, :1]
 

time: 162 us -> 167 us (1.031)
  starting transfers between devices: 28.8 us -> 21.7 us
  blocking collectives: 73.6 us -> 80.3 us
  waiting for transfers between devices: 27.6 us -> 32.2 us
    all_to_all x0 -> x1, blocking collectives: none -> 8.3 us  [per_device(): lax.all_to_all(mine.reshape(roles, -1, 2 * width), 'role', split_axis=0,...]
    all_to_all x0 -> x1, waiting for transfers between devices: none -> 8.3 us  [per_device(): lax.all_to_all(jnp.broadcast_to(mine[None], (ZZ,) + mine.shape), 'shard',...]
    all_to_all x0 -> x1, starting transfers between devices: none -> 6.92 us  [per_device(): lax.all_to_all(jnp.broadcast_to(mine[None], (ZZ,) + mine.shape), 'shard',...]
    ppermute x3, starting transfers between devices: 11.2 us -> 4.58 us  [to_across(): return lax.ppermute(v, 'role', [(0, 2), (1, 3), (2, 0), (3, 1)])]
    ppermute x4 -> x0, waiting for transfers between devices: 3.6 us -> none  [the longest x3 3.6 us: per_device(): lax.ppermute(mine, axes, [(zz * shards + shard_at(y, zz, zl, x), zz * sha...]
    ppermute x4 -> x0, starting transfers between devices: 3.3 us -> none  [the longest x3 2.63 us: per_device(): lax.ppermute(mine, axes, [(zz * shards + shard_at(y, zz, zl, x), zz * sha...]
    ppermute x1, starting transfers between devices: 2.89 us -> 0.01 us  [to_core(): return lax.ppermute(v, 'role', [(0, 1), (1, 0), (2, 3), (3, 2)])]
    concatenate x0 -> x2, local copies, waits for them, and re-layouts: none -> 1.85 us  [per_device(): mine = jnp.concatenate((trainer_in[0], trainer_out[0]), 1)]
  transfers between devices with their start and end apart: 13 -> 10, of which waited for: 10 -> 9; matrix products, arithmetic and copies ran while one was open for 0% -> 0% of each run, Pallas kernels for 1% -> 1%
where the time goes in v5:
time: 167 us; the launch traced here: 165 us
  blocking collectives  80.3 us (48%)
  waiting for transfers between devices  32.2 us (19%)
  Pallas kernels  25.2 us (15%)
  starting transfers between devices  21.7 us (13%)
  local copies, waits for them, and re-layouts  4.64 us (3%)
    all_to_all x1, blocking collectives, per_device(): lax.all_to_all(outgoing.reshape(shards, ROWS, LANES), 'shard', split_axis...  22.6 us
    all_to_all x1, blocking collectives, per_device(): lax.all_to_all(packed, 'shard', split_axis=0, concat_axis=0, tiled=True)  17.6 us
    all_to_all x1, blocking collectives, per_device(): lax.all_to_all(shares, 'shard', split_axis=0, concat_axis=0, tiled=True)  16.2 us
    pallas_call x1, Pallas kernels, pair(): pl.pallas_call(pair_kernel, out_shape=(jax.ShapeDtypeStruct(x.shape, f32)...  16.1 us
    all_to_all x1, blocking collectives, per_device(): lax.all_to_all(grads, 'shard', split_axis=0, concat_axis=0, tiled=True)  15.6 us
    all_to_all x1, blocking collectives, per_device(): lax.all_to_all(mine.reshape(roles, -1, 2 * width), 'role', split_axis=0,...  8.3 us
    all_to_all x1, waiting for transfers between devices, per_device(): lax.all_to_all(jnp.broadcast_to(mine[None], (ZZ,) + mine.shape), 'shard',...  8.3 us
    all_to_all x1, waiting for transfers between devices, gather_units(): lax.all_to_all(jnp.broadcast_to(block[None], (parts, units, width)), 'sha...  8.07 us
  transfers between devices with their start and end apart: 10, of which 9 were waited for; matrix products, arithmetic and copies ran while one was open for 0% of the time, Pallas kernels for 1%

profile of v5, /device:TPU:2, one launch (start us, length us, event | category | flops | bytes accessed | tf_op | source)
XLA Modules:
  0.0 165.1 jit_solution(9885322949363663913)
XLA Ops:
  0.6 0.9 concatenate.18
  1.6 0.9 concatenate.17
  2.5 8.3 %all_to_all.51 = bf16[4,12,1536]{2,1,0:T(8,128)(2,1)S(1)} all-to-all(bf16[4,12,1536]{2,1,0:T(8,128)(2,1)S(1)} %pad_maximum_fusion), channel_id=1, replica_groups=mesh['role'=4,'shard'=64] {'role'}, dimensions={0} | all-to-all | bytes 294912 | tf_op jit(solution)/shard_map/all_to_all | solution.py:395
  10.8 0.7 broadcast_in_dim.23
  11.5 6.9 %all-to-all-start.1 = ((bf16[4,12,1536]{2,1,0:T(8,128)(2,1)}), bf16[4,12,1536]{2,1,0:T(8,128)(2,1)S(1)}, u32[]{:S(2)}, u32[]{:S(2)}) async-start(bf16[4,12,1536]{2,1,0:T(8,128)(2,1)} %broadcast_in_dim.23), calls=%async_computation.1 | async-start | bytes 393216 | tf_op jit(solution)/shard_map/all_to_all | solution.py:398
  18.4 1.7 %collective-permute-start = (bf16[128,768]{1,0:T(8,128)(2,1)S(1)}, bf16[128,768]{1,0:T(8,128)(2,1)S(1)}, u32[]{:S(2)}, u32[]{:S(2)}) collective-permute-start(bf16[128,768]{1,0:T(8,128)(2,1)S(1)} %copy-done), channel_id=1, source_target_pairs={{0,128},{64,192},{128,0},{192,64},{1,129},{65,193},{129,1},{193,65... | collective-permute-start | bytes 589832 | tf_op jit(solution)/shard_map/ppermute | solution.py:381
  20.1 8.3 %all-to-all-done.1 = bf16[4,12,1536]{2,1,0:T(8,128)(2,1)S(1)} async-done(((bf16[4,12,1536]{2,1,0:T(8,128)(2,1)}), bf16[4,12,1536]{2,1,0:T(8,128)(2,1)S(1)}, u32[]{:S(2)}, u32[]{:S(2)}) %all-to-all-start.1) | async-done | bytes 147488 | tf_op jit(solution)/shard_map/all_to_all | solution.py:398
  28.5 1.1 broadcast_in_dim.24
  29.6 6.3 %all-to-all-start.2 = ((bf16[8,48,1536]{2,1,0:T(8,128)(2,1)}), bf16[8,48,1536]{2,1,0:T(8,128)(2,1)S(1)}, u32[]{:S(2)}, u32[]{:S(2)}) async-start(bf16[8,48,1536]{2,1,0:T(8,128)(2,1)} %broadcast_in_dim.24), calls=%async_computation.2 | async-start | bytes 2359296 | tf_op jit(solution)/shard_map/all_to_all | solution.py:357
  35.9 0.8 collective-permute-start.1
  36.7 1.2 collective-permute-start.2
  37.9 3.8 %collective-permute-done.1.along_ref = bf16[128,768]{1,0:T(8,128)(2,1)S(1)} collective-permute-done((bf16[128,768]{1,0:T(8,128)(2,1)S(1)}, bf16[128,768]{1,0:T(8,128)(2,1)S(1)}, u32[]{:S(2)}, u32[]{:S(2)}) %collective-permute-start.1) | collective-permute-done | bytes 196640 | tf_op jit(solution)/shard_map/ppermute | solution.py:384
  41.7 2.1 %collective-permute-done.2.diagonal_ref = bf16[128,768]{1,0:T(8,128)(2,1)S(1)} collective-permute-done((bf16[128,768]{1,0:T(8,128)(2,1)S(1)}, bf16[128,768]{1,0:T(8,128)(2,1)S(1)}, u32[]{:S(2)}, u32[]{:S(2)}) %collective-permute-start.2) | collective-permute-done | bytes 196640 | tf_op jit(solution)/shard_map/ppermute | solution.py:384
  43.8 8.1 %all-to-all-done.2 = bf16[8,48,1536]{2,1,0:T(8,128)(2,1)S(1)} async-done(((bf16[8,48,1536]{2,1,0:T(8,128)(2,1)}), bf16[8,48,1536]{2,1,0:T(8,128)(2,1)S(1)}, u32[]{:S(2)}, u32[]{:S(2)}) %all-to-all-start.2) | async-done | bytes 1179680 | tf_op jit(solution)/shard_map/all_to_all | solution.py:357
  52.0 2.0 %encode.1.so_far_ref = f32[4,128,768]{2,1,0:T(8,128)S(1)} custom-call(bf16[128,768]{1,0:T(8,128)(2,1)S(1)} %copy-done, bf16[128,768]{1,0:T(8,128)(2,1)S(1)} %collective-permute-done.across_ref, bf16[128,768]{1,0:T(8,128)(2,1)S(1)} %collective-permute-done.1.along_ref, bf16[128,768]{1,0:T(8,128)(2,1)S(1)} %collective-permute-done.2.diagonal_ref, ...), custom_call_target="tpu_custom_call" | custom-call | tf_op jit(solution)/shard_map/encode/pallas_call | solution.py:42
  54.0 0.7 collective-permute-done.3.w_ref
  54.7 2.0 %encode_rest.1 = (f32[128,768]{1,0:T(8,128)S(1)}, f32[128,768]{1,0:T(8,128)S(1)}, bf16[128,768]{1,0:T(8,128)(2,1)S(1)}, bf16[128,768]{1,0:T(8,128)(2,1)S(1)}) custom-call(bf16[128,768]{1,0:T(8,128)(2,1)S(1)} %copy-done, bf16[128,768]{1,0:T(8,128)(2,1)S(1)} %collective-permute-done.across_ref, bf16[128,768]{1,0:T(8,128)(2,1)S(1)} %collective-permute-done.1.along_ref, ...), custom_call_target="tpu_custom_call" | custom-call | tf_op jit(solution)/shard_map/encode_rest/pallas_call | solution.py:78
  56.7 2.4 %collective-permute-start.4 = (bf16[128,768]{1,0:T(8,128)(2,1)S(1)}, bf16[128,768]{1,0:T(8,128)(2,1)S(1)}, u32[]{:S(2)}, u32[]{:S(2)}) collective-permute-start(bf16[128,768]{1,0:T(8,128)(2,1)S(1)} %get-tuple-element.31), channel_id=1, source_target_pairs={{0,128},{64,192},{128,0},{192,64},{1,129},{65,193},{129,1},{193,65... | collective-permute-start | bytes 589832 | tf_op jit(solution)/shard_map/ppermute | solution.py:381
  59.2 1.0 collective-permute-start.5
  60.2 4.2 %collective-permute-done.4.across_ref = bf16[128,768]{1,0:T(8,128)(2,1)S(1)} collective-permute-done((bf16[128,768]{1,0:T(8,128)(2,1)S(1)}, bf16[128,768]{1,0:T(8,128)(2,1)S(1)}, u32[]{:S(2)}, u32[]{:S(2)}) %collective-permute-start.4) | collective-permute-done | bytes 196640 | tf_op jit(solution)/shard_map/ppermute | solution.py:381
  64.4 1.5 collective-permute-done.5.along_ref
  66.3 1.0 collective-permute-start.6
  67.4 3.2 %collective-permute-done.7 = bf16[64,768]{1,0:T(8,128)(2,1)S(1)} collective-permute-done((bf16[64,768]{1,0:T(8,128)(2,1)S(1)}, bf16[64,768]{1,0:T(8,128)(2,1)S(1)}, u32[]{:S(2)}, u32[]{:S(2)}) %collective-permute-start.7) | collective-permute-done | bytes 98336 | tf_op jit(solution)/shard_map/ppermute | solution.py:381
  71.0 1.5 place.1
  72.5 22.6 %all_to_all.52 = bf16[64,32,128]{2,1,0:T(8,128)(2,1)S(1)} all-to-all(bf16[64,32,128]{2,1,0:T(8,128)(2,1)S(1)} %bitcast.20), channel_id=1, replica_groups=mesh['role'=4,'shard'=64] {'shard'}, dimensions={0} | all-to-all | bytes 1048576 | tf_op jit(solution)/shard_map/all_to_all | solution.py:437
  95.2 1.6 score.1
  96.8 17.6 %all_to_all.53 = f32[64,1,128]{2,1,0:T(1,128)S(1)} all-to-all(f32[64,1,128]{2,1,0:T(1,128)S(1)} %bitcast.25), channel_id=1, replica_groups=mesh['role'=4,'shard'=64] {'shard'}, dimensions={0} | all-to-all | bytes 65536 | tf_op jit(solution)/shard_map/all_to_all | solution.py:441
  114.3 16.1 %pair.1 = (f32[64,128]{1,0:T(8,128)S(1)}, f32[1,128]{1,0:T(1,128)}) custom-call(f32[64,128]{1,0:T(8,128)S(1)} %bitcast.24, f32[32,128]{1,0:T(8,128)S(1)} %copy-done.2), custom_call_target="tpu_custom_call" | custom-call | tf_op jit(solution)/shard_map/pair/pallas_call | solution.py:280
  130.4 15.6 %all_to_all.54 = f32[64,1,128]{2,1,0:T(1,128)S(1)} all-to-all(f32[64,1,128]{2,1,0:T(1,128)S(1)} %bitcast.26), channel_id=1, replica_groups=mesh['role'=4,'shard'=64] {'shard'}, dimensions={0} | all-to-all | bytes 65536 | tf_op jit(solution)/shard_map/all_to_all | solution.py:446
  146.1 2.0 %share.1 = f32[64,768]{1,0:T(8,128)S(1)} custom-call(f32[64,128]{1,0:T(8,128)S(1)} %bitcast.23, s32[64,128]{1,0:T(8,128)S(1)} %pad_add_fusion.idsg_ref, bf16[256,768]{1,0:T(8,128)(2,1)S(1)} %get-tuple-element.39.refreshed_ref), custom_call_target="tpu_custom_call" | custom-call | tf_op jit(solution)/shard_map/share/pallas_call | solution.py:327
  148.3 16.2 %all_to_all.55 = f32[64,1,768]{2,1,0:T(1,128)S(1)} all-to-all(f32[64,1,768]{2,1,0:T(1,128)S(1)} %copy.14), channel_id=1, replica_groups=mesh['role'=4,'shard'=64] {'shard'}, dimensions={0} | all-to-all | bytes 393216 | tf_op jit(solution)/shard_map/all_to_all | solution.py:448
  164.6 0.6 broadcast_in_dim.27
  (32 shorter events, 1.6 us)
Async XLA Ops:
  0.6 17.8 %copy-start = (bf16[128,768]{1,0:T(8,128)(2,1)S(1)}, bf16[128,768]{1,0:T(8,128)(2,1)}, u32[]{:S(2)}) copy-start(bf16[128,768]{1,0:T(8,128)(2,1)} %cls_ref.1) | copy-start | bytes 589828
  11.5 16.9 %all-to-all-start.1 = ((bf16[4,12,1536]{2,1,0:T(8,128)(2,1)}), bf16[4,12,1536]{2,1,0:T(8,128)(2,1)S(1)}, u32[]{:S(2)}, u32[]{:S(2)}) async-start(bf16[4,12,1536]{2,1,0:T(8,128)(2,1)} %broadcast_in_dim.23), calls=%async_computation.1 | async-start | bytes 393216 | tf_op jit(solution)/shard_map/all_to_all | solution.py:398
  18.4 10.0 %collective-permute-start = (bf16[128,768]{1,0:T(8,128)(2,1)S(1)}, bf16[128,768]{1,0:T(8,128)(2,1)S(1)}, u32[]{:S(2)}, u32[]{:S(2)}) collective-permute-start(bf16[128,768]{1,0:T(8,128)(2,1)S(1)} %copy-done), channel_id=1, source_target_pairs={{0,128},{64,192},{128,0},{192,64},{1,129},{65,193},{129,1},{193,65... | collective-permute-start | bytes 589832 | tf_op jit(solution)/shard_map/ppermute | solution.py:381
  29.6 22.3 %copy-start.6 = (bf16[1,768]{1,0:T(2,128)(2,1)S(1)}, bf16[1,768]{1,0:T(2,128)(2,1)}, u32[]{:S(2)}) copy-start(bf16[1,768]{1,0:T(2,128)(2,1)} %param.14) | copy-start | bytes 4612
  29.6 22.2 %all-to-all-start.2 = ((bf16[8,48,1536]{2,1,0:T(8,128)(2,1)}), bf16[8,48,1536]{2,1,0:T(8,128)(2,1)S(1)}, u32[]{:S(2)}, u32[]{:S(2)}) async-start(bf16[8,48,1536]{2,1,0:T(8,128)(2,1)} %broadcast_in_dim.24), calls=%async_computation.2 | async-start | bytes 2359296 | tf_op jit(solution)/shard_map/all_to_all | solution.py:357
  35.9 5.8 %collective-permute-start.1 = (bf16[128,768]{1,0:T(8,128)(2,1)S(1)}, bf16[128,768]{1,0:T(8,128)(2,1)S(1)}, u32[]{:S(2)}, u32[]{:S(2)}) collective-permute-start(bf16[128,768]{1,0:T(8,128)(2,1)S(1)} %copy-done), channel_id=1, source_target_pairs={{0,2},{1,3},{2,0},{3,1},{4,6},{5,7},{6,4},{7,5},{8,10},{9,11},{10,... | collective-permute-start | bytes 589832 | tf_op jit(solution)/shard_map/ppermute | solution.py:384
  36.7 7.1 %collective-permute-start.2 = (bf16[128,768]{1,0:T(8,128)(2,1)S(1)}, bf16[128,768]{1,0:T(8,128)(2,1)S(1)}, u32[]{:S(2)}, u32[]{:S(2)}) collective-permute-start(bf16[128,768]{1,0:T(8,128)(2,1)S(1)} %collective-permute-done.across_ref), channel_id=1, source_target_pairs={{0,2},{1,3},{2,0},{3,1},{4,6},{5,7},{6,4},{7,5},{8,10},{9,11},{10,... | collective-permute-start | bytes 589832 | tf_op jit(solution)/shard_map/ppermute | solution.py:384
  51.8 2.8 %collective-permute-start.3 = (bf16[384,1536]{1,0:T(8,128)(2,1)S(1)}, bf16[384,1536]{1,0:T(8,128)(2,1)S(1)}, u32[]{:S(2)}, u32[]{:S(2)}) collective-permute-start(bf16[384,1536]{1,0:T(8,128)(2,1)S(1)} %bitcast.18), channel_id=1, source_target_pairs={{0,64},{64,0},{128,192},{192,128},{1,65},{65,1},{129,193},{193,129... | collective-permute-start | bytes 3538952 | tf_op jit(solution)/shard_map/ppermute | solution.py:378
  54.0 13.3 %copy-start.4 = (s32[64,64]{1,0:T(8,128)S(1)}, s32[64,64]{1,0:T(8,128)}, u32[]{:S(2)}) copy-start(s32[64,64]{1,0:T(8,128)} %param.16) | copy-start | bytes 49156
  54.0 13.3 %copy-start.5 = (s32[64,64]{1,0:T(8,128)S(1)}, s32[64,64]{1,0:T(8,128)}, u32[]{:S(2)}) copy-start(s32[64,64]{1,0:T(8,128)} %param.15) | copy-start | bytes 49156
  56.7 14.3 %copy-start.3 = (s32[64,1]{0,1:T(1,128)S(1)}, s32[64,1]{0,1:T(1,128)}, u32[]{:S(2)}) copy-start(s32[64,1]{0,1:T(1,128)} %param.13) | copy-start | bytes 772
  56.7 7.6 %collective-permute-start.4 = (bf16[128,768]{1,0:T(8,128)(2,1)S(1)}, bf16[128,768]{1,0:T(8,128)(2,1)S(1)}, u32[]{:S(2)}, u32[]{:S(2)}) collective-permute-start(bf16[128,768]{1,0:T(8,128)(2,1)S(1)} %get-tuple-element.31), channel_id=1, source_target_pairs={{0,128},{64,192},{128,0},{192,64},{1,129},{65,193},{129,1},{193,65... | collective-permute-start | bytes 589832 | tf_op jit(solution)/shard_map/ppermute | solution.py:381
  59.2 6.7 %collective-permute-start.5 = (bf16[128,768]{1,0:T(8,128)(2,1)S(1)}, bf16[128,768]{1,0:T(8,128)(2,1)S(1)}, u32[]{:S(2)}, u32[]{:S(2)}) collective-permute-start(bf16[128,768]{1,0:T(8,128)(2,1)S(1)} %get-tuple-element.32), channel_id=1, source_target_pairs={{0,2},{1,3},{2,0},{3,1},{4,6},{5,7},{6,4},{7,5},{8,10},{9,11},{10,... | collective-permute-start | bytes 589832 | tf_op jit(solution)/shard_map/ppermute | solution.py:384
  65.9 4.7 %collective-permute-start.7 = (bf16[64,768]{1,0:T(8,128)(2,1)S(1)}, bf16[64,768]{1,0:T(8,128)(2,1)S(1)}, u32[]{:S(2)}, u32[]{:S(2)}) collective-permute-start(bf16[64,768]{1,0:T(8,128)(2,1)S(1)} %get-tuple-element.42), channel_id=1, source_target_pairs={{0,128},{64,192},{128,0},{192,64},{1,129},{65,193},{129,1},{193,65... | collective-permute-start | bytes 294920 | tf_op jit(solution)/shard_map/ppermute | solution.py:381
  66.3 4.6 %collective-permute-start.6 = (bf16[64,768]{1,0:T(8,128)(2,1)S(1)}, bf16[64,768]{1,0:T(8,128)(2,1)S(1)}, u32[]{:S(2)}, u32[]{:S(2)}) collective-permute-start(bf16[64,768]{1,0:T(8,128)(2,1)S(1)} %get-tuple-element.41), channel_id=1, source_target_pairs={{0,2},{1,3},{2,0},{3,1},{4,6},{5,7},{6,4},{7,5},{8,10},{9,11},{10,... | collective-permute-start | bytes 294920 | tf_op jit(solution)/shard_map/ppermute | solution.py:384
  71.0 24.2 %copy-start.1 = (bf16[256,768]{1,0:T(8,128)(2,1)S(1)}, bf16[256,768]{1,0:T(8,128)(2,1)}, u32[]{:S(2)}) copy-start(bf16[256,768]{1,0:T(8,128)(2,1)} %stale_ref.1) | copy-start | bytes 1179652
  72.5 41.8 %copy-start.2 = (f32[32,128]{1,0:T(8,128)S(1)}, f32[32,128]{1,0:T(8,128)}, u32[]{:S(2)}) copy-start(f32[32,128]{1,0:T(8,128)} %constant.2.clone.discount_ref) | copy-start | bytes 49156

commit v6 on v5

--- a/solution.py
+++ b/solution.py
@@ -1,3 +1,4 @@
+import functools
 import math
 
 import jax
@@ -47,56 +48,36 @@
     )(*xs, units)
 
 
-def second_kernel(
-    own_ref,
-    across_ref,
-    along_ref,
-    diagonal_ref,
-    w_ref,
-    so_far_ref,
-    kept_ref,
-    later_ref,
-    send_across_ref,
-    send_along_ref,
-):
-    half = own_ref.shape[0] // 2
-    diagonal = so_far_ref[3] + partial_sums(diagonal_ref[...], w_ref)
-    across = so_far_ref[1] + partial_sums(across_ref[...], w_ref)
-    send_across_ref[:half] = across[:half].astype(bf16)
-    send_across_ref[half:] = diagonal[:half].astype(bf16)
-    along = so_far_ref[2] + partial_sums(along_ref[...], w_ref)
-    send_along_ref[:half] = along[half:].astype(bf16)
-    send_along_ref[half:] = diagonal[half:].astype(bf16)
-    later_ref[:half] = along[:half]
-    later_ref[half:] = across[half:]
-    kept_ref[...] = so_far_ref[0] + partial_sums(own_ref[...], w_ref)
-
-
-def second_half(xs, units, so_far):
-    kept = jax.ShapeDtypeStruct(xs[0].shape, f32)
-    sent = jax.ShapeDtypeStruct(xs[0].shape, bf16)
-    return pl.pallas_call(
-        second_kernel,
-        out_shape=(kept, kept, sent, sent),
+def second_kernel(at, *refs):
+    x_refs, (w_ref, so_far_ref), out_refs = refs[: len(at)], refs[len(at) :][:2], refs[-len(at) :]
+    for n, x_ref, out_ref in zip(at, x_refs, out_refs):
+        part = so_far_ref[n] + partial_sums(x_ref[...], w_ref)
+        out_ref[...] = part.astype(out_ref.dtype)
+
+
+def second_half(xs, units, so_far, at, dtype):
+    return pl.pallas_call(
+        functools.partial(second_kernel, at),
+        out_shape=tuple(jax.ShapeDtypeStruct(xs[n].shape, dtype) for n in at),
         compiler_params=params(),
         name="encode_rest",
-    )(*xs, units, so_far)
+    )(*(xs[n] for n in at), units, so_far)
 
 
 ROWS = 32
 
 
 def place_kernel(
-    cls_ref, kept_ref, across_ref, along_ref, last_ref, owner_ref, query_ref, out_ref
+    cls_ref, own_ref, across_ref, along_ref, diagonal_ref, owner_ref, query_ref, out_ref
 ):
     rows, width = cls_ref.shape
-    half = rows // 2
     blocks = owner_ref.shape[1]
     total = out_ref.shape[0]
     shards = total // ROWS
     chunks = width // LANES
-    early = jnp.concatenate((across_ref[:half], along_ref[:half]), 0).astype(f32)
-    resid = cls_ref[...].astype(f32) + kept_ref[...] + early + last_ref[...].astype(f32)
+    resid = cls_ref[...].astype(f32) + own_ref[...]
+    for part_ref in (across_ref, along_ref, diagonal_ref):
+        resid = resid + part_ref[...].astype(f32)
     centred = resid - jnp.mean(resid, -1, keepdims=True)
     variance = jnp.mean(centred * centred, -1, keepdims=True)
     fresh = (centred * lax.rsqrt(variance + EPSILON)).astype(bf16)
@@ -133,13 +114,13 @@
     out_ref[...] = jnp.where(filled > 0.5, placed, rest.reshape(total, LANES)).astype(bf16)
 
 
-def place(cls_states, kept, across, along, last, owner, query, shards):
+def place(cls_states, own, across, along, diagonal, owner, query, shards):
     return pl.pallas_call(
         place_kernel,
         out_shape=jax.ShapeDtypeStruct((shards * ROWS, LANES), bf16),
         compiler_params=params(),
         name="place",
-    )(cls_states, kept, across, along, last, owner, query)
+    )(cls_states, own, across, along, diagonal, owner, query)
 
 
 def score_kernel(
@@ -370,8 +351,7 @@
 ):
     shards = lax.axis_size("shard")
     roles = lax.axis_size("role")
-    passages, width = cls_states.shape
-    half = passages // 2
+    width = cls_states.shape[1]
     barrier = lax.optimization_barrier
 
     def to_core(v):
@@ -390,36 +370,45 @@
             ],
         )
 
-    x_across = to_across(cls_states)
-    mine = jnp.concatenate((trainer_in[0], trainer_out[0]), 1)
-    mine = lax.all_to_all(
-        mine.reshape(roles, -1, 2 * width), "role", split_axis=0, concat_axis=0, tiled=True
-    )[roles - 1]
-    block = lax.all_to_all(
-        jnp.broadcast_to(mine[None], (ZZ,) + mine.shape),
-        "shard",
-        split_axis=0,
-        concat_axis=0,
-        tiled=True,
-        axis_index_groups=[
-            [shard_at(y, zz, zl, x) for zz in range(ZZ)]
-            for y in range(Y)
-            for zl in range(ZL)
-            for x in range(X)
-        ],
-    ).reshape(-1, 2 * width)
-    block, x_across, cls_after = barrier((block, x_across, cls_states))
+    def to_diagonal(v):
+        return lax.ppermute(
+            v,
+            ("role", "shard"),
+            [
+                (r * shards + shard_at(y, zz, zl, x), (r ^ 2) * shards + shard_at(y, zz, 1 - zl, x))
+                for r in range(roles)
+                for y, zz, zl, x in everywhere()
+            ],
+        )
+
+    pieces = jnp.concatenate((trainer_in[0], trainer_out[0]), 1).reshape(roles, -1, 2 * width)
+    role = lax.axis_index("role")
+    arrived = [lax.ppermute(pieces[k], "role", [(roles - 1, k)]) for k in range(roles - 1)]
+    mine = pieces[roles - 1]
+    for k in range(roles - 1):
+        mine = jnp.where(role == k, arrived[k], mine)
+    mine, cls_after = barrier((mine, cls_states))
+    block = [mine]
+    for by in range(1, ZZ):
+        turn = [
+            (shard_at(y, zz, zl, x), shard_at(y, (zz + by) % ZZ, zl, x))
+            for y, zz, zl, x in everywhere()
+        ]
+        block.append(lax.ppermute(mine, "shard", turn))
+    block = jnp.concatenate(block, 0)
+    x_across = to_across(cls_after)
+    block, x_across, cls_after = barrier((block, x_across, cls_after))
     units = gather_units(block)
     xs = (cls_states, x_across, to_along(cls_after), to_along(x_across))
     units, xs = barrier((units, xs))
     other_units = to_core(units)
     so_far = first_half(xs, units)
-    kept, later, for_across, for_along = second_half(xs, other_units, so_far)
-    from_across = to_across(for_across)
-    from_along = to_along(for_along)
-    then_along = (later[:half] + from_across[half:].astype(f32)).astype(bf16)
-    then_across = (later[half:] + from_along[half:].astype(f32)).astype(bf16)
-    last = jnp.concatenate((to_along(then_along), to_across(then_across)), 0)
+    (diagonal,) = second_half(xs, other_units, so_far, (3,), bf16)
+    from_diagonal = to_diagonal(diagonal)
+    across, along = second_half(xs, other_units, so_far, (1, 2), bf16)
+    from_across = to_across(across)
+    from_along = to_along(along)
+    (own,) = second_half(xs, other_units, so_far, (0,), f32)
     chunks = width // LANES
     rest = jnp.concatenate(
         (
@@ -431,7 +420,14 @@
     )
     idsg = jnp.concatenate((neg_ids, grades), 1)
     outgoing = place(
-        cls_states, kept, from_across, from_along, last, block_owner.reshape(1, -1), rest, shards
+        cls_states,
+        own,
+        from_across,
+        from_along,
+        from_diagonal,
+        block_owner.reshape(1, -1),
+        rest,
+        shards,
     )
     outgoing, idsg = lax.optimization_barrier((outgoing, idsg))
     arrived = lax.all_to_all(

time: 167 us -> 162 us (0.970)
  starting transfers between devices: 21.7 us -> 30 us
  blocking collectives: 80.3 us -> 73.8 us
  waiting for transfers between devices: 32.2 us -> 27.1 us
  local copies, waits for them, and re-layouts: 4.64 us -> 2.05 us
    ppermute x0 -> x7, starting transfers between devices: none -> 14.1 us  [the longest x3 10.2 us: per_device(): block.append(lax.ppermute(mine, 'shard', turn))]
    all_to_all x1 -> x0, blocking collectives: 8.3 us -> none  [per_device(): lax.all_to_all(mine.reshape(roles, -1, 2 * width), 'role', split_axis=0,...]
    all_to_all x1 -> x0, waiting for transfers between devices: 8.3 us -> none  [per_device(): lax.all_to_all(jnp.broadcast_to(mine[None], (ZZ,) + mine.shape), 'shard',...]
    all_to_all x1 -> x0, starting transfers between devices: 6.92 us -> none  [per_device(): lax.all_to_all(jnp.broadcast_to(mine[None], (ZZ,) + mine.shape), 'shard',...]
    ppermute x0 -> x7, waiting for transfers between devices: none -> 4.05 us  [the longest x1 3.56 us: to_diagonal(): lax.ppermute(v, ('role', 'shard'), [(r * shards + shard_at(y, zz, zl, x),...]
    all_to_all x1, blocking collectives: 22.6 us -> 24.5 us  [per_device(): lax.all_to_all(outgoing.reshape(shards, ROWS, LANES), 'shard', split_axis...]
    concatenate x2 -> x0, local copies, waits for them, and re-layouts: 1.85 us -> none  [per_device(): mine = jnp.concatenate((trainer_in[0], trainer_out[0]), 1)]
    ppermute x3 -> x2, starting transfers between devices: 4.58 us -> 6.34 us  [to_across(): return lax.ppermute(v, 'role', [(0, 2), (1, 3), (2, 0), (3, 1)])]
  transfers between devices with their start and end apart: 10 -> 14, of which waited for: 9 -> 9; matrix products, arithmetic and copies ran while one was open for 0% -> 0% of each run, Pallas kernels for 1% -> 2%
where the time goes in v6:
time: 162 us; the launch traced here: 161 us
  blocking collectives  73.8 us (46%)
  starting transfers between devices  30 us (19%)
  waiting for transfers between devices  27.1 us (17%)
  Pallas kernels  25.6 us (16%)
  local copies, waits for them, and re-layouts  2.05 us (1%)
  other arithmetic  2.04 us (1%)
    all_to_all x1, blocking collectives, per_device(): lax.all_to_all(outgoing.reshape(shards, ROWS, LANES), 'shard', split_axis...  24.5 us
    all_to_all x1, blocking collectives, per_device(): lax.all_to_all(packed, 'shard', split_axis=0, concat_axis=0, tiled=True)  17.5 us
    all_to_all x1, blocking collectives, per_device(): lax.all_to_all(shares, 'shard', split_axis=0, concat_axis=0, tiled=True)  16.2 us
    pallas_call x1, Pallas kernels, pair(): pl.pallas_call(pair_kernel, out_shape=(jax.ShapeDtypeStruct(x.shape, f32)...  16.1 us
    all_to_all x1, blocking collectives, per_device(): lax.all_to_all(grads, 'shard', split_axis=0, concat_axis=0, tiled=True)  15.6 us
    ppermute x3, starting transfers between devices, per_device(): block.append(lax.ppermute(mine, 'shard', turn))  10.2 us
    ppermute x3, waiting for transfers between devices, to_along(): lax.ppermute(v, 'shard', [(shard_at(y, zz, zl, x), shard_at(y, zz, 1 - zl...  8.58 us
    all_to_all x1, waiting for transfers between devices, gather_units(): lax.all_to_all(jnp.broadcast_to(block[None], (parts, units, width)), 'sha...  7.99 us
  transfers between devices with their start and end apart: 14, of which 9 were waited for; matrix products, arithmetic and copies ran while one was open for 0% of the time, Pallas kernels for 2%

profile of v6, /device:TPU:2, one launch (start us, length us, event | category | flops | bytes accessed | tf_op | source)
XLA Modules:
  0.0 161.4 jit_solution(6692319361797315428)
XLA Ops:
  0.6 0.9 fusion
  1.5 1.3 collective-permute-start
  2.8 0.7 collective-permute-start.1
  4.6 0.8 fusion.5
  5.4 6.4 %collective-permute-start.5 = (bf16[12,1536]{1,0:T(8,128)(2,1)S(1)}, bf16[12,1536]{1,0:T(8,128)(2,1)S(1)}, u32[]{:S(2)}, u32[]{:S(2)}) collective-permute-start(bf16[12,1536]{1,0:T(8,128)(2,1)S(1)} %fusion.5), channel_id=1, source_target_pairs={{0,12},{1,13},{2,14},{3,15},{4,0},{5,1},{6,2},{7,3},{8,4},{9,5},{1... | collective-permute-start | bytes 110600 | tf_op jit(solution)/shard_map/ppermute | solution.py:397
  11.8 1.0 collective-permute-start.4
  12.8 2.8 %collective-permute-start.3 = (bf16[12,1536]{1,0:T(8,128)(2,1)S(1)}, bf16[12,1536]{1,0:T(8,128)(2,1)S(1)}, u32[]{:S(2)}, u32[]{:S(2)}) collective-permute-start(bf16[12,1536]{1,0:T(8,128)(2,1)S(1)} %fusion.5), channel_id=1, source_target_pairs={{0,4},{1,5},{2,6},{3,7},{4,8},{5,9},{6,10},{7,11},{8,12},{9,13},{1... | collective-permute-start | bytes 110600 | tf_op jit(solution)/shard_map/ppermute | solution.py:397
  15.6 5.3 %collective-permute-start.6 = (bf16[128,768]{1,0:T(8,128)(2,1)}, bf16[128,768]{1,0:T(8,128)(2,1)S(1)}, u32[]{:S(2)}, u32[]{:S(2)}) collective-permute-start(bf16[128,768]{1,0:T(8,128)(2,1)} %cls_ref.1), channel_id=1, source_target_pairs={{0,128},{64,192},{128,0},{192,64},{1,129},{65,193},{129,1},{193,65... | collective-permute-start | bytes 589832 | tf_op jit(solution)/shard_map/ppermute | solution.py:361
  21.0 3.9 %collective-permute-done.6.across_ref.refs_0_ = bf16[128,768]{1,0:T(8,128)(2,1)S(1)} collective-permute-done((bf16[128,768]{1,0:T(8,128)(2,1)}, bf16[128,768]{1,0:T(8,128)(2,1)S(1)}, u32[]{:S(2)}, u32[]{:S(2)}) %collective-permute-start.6) | collective-permute-done | bytes 196640 | tf_op jit(solution)/shard_map/ppermute | solution.py:361
  24.9 1.1 broadcast_in_dim.15
  26.0 6.2 %all-to-all-start = ((bf16[8,48,1536]{2,1,0:T(8,128)(2,1)}), bf16[8,48,1536]{2,1,0:T(8,128)(2,1)S(1)}, u32[]{:S(2)}, u32[]{:S(2)}) async-start(bf16[8,48,1536]{2,1,0:T(8,128)(2,1)} %broadcast_in_dim.15), calls=%async_computation | async-start | bytes 2359296 | tf_op jit(solution)/shard_map/all_to_all | solution.py:338
  32.2 1.1 collective-permute-start.7
  33.3 1.0 collective-permute-start.8
  34.3 4.6 %collective-permute-done.7.along_ref.refs_1_ = bf16[128,768]{1,0:T(8,128)(2,1)S(1)} collective-permute-done((bf16[128,768]{1,0:T(8,128)(2,1)S(1)}, bf16[128,768]{1,0:T(8,128)(2,1)S(1)}, u32[]{:S(2)}, u32[]{:S(2)}) %collective-permute-start.7) | collective-permute-done | bytes 196640 | tf_op jit(solution)/shard_map/ppermute | solution.py:364
  38.9 2.1 %collective-permute-done.8.diagonal_ref.refs_0_ = bf16[128,768]{1,0:T(8,128)(2,1)S(1)} collective-permute-done((bf16[128,768]{1,0:T(8,128)(2,1)S(1)}, bf16[128,768]{1,0:T(8,128)(2,1)S(1)}, u32[]{:S(2)}, u32[]{:S(2)}) %collective-permute-start.8) | collective-permute-done | bytes 196640 | tf_op jit(solution)/shard_map/ppermute | solution.py:364
  41.1 8.0 %all-to-all-done = bf16[8,48,1536]{2,1,0:T(8,128)(2,1)S(1)} async-done(((bf16[8,48,1536]{2,1,0:T(8,128)(2,1)}), bf16[8,48,1536]{2,1,0:T(8,128)(2,1)S(1)}, u32[]{:S(2)}, u32[]{:S(2)}) %all-to-all-start) | async-done | bytes 1179680 | tf_op jit(solution)/shard_map/all_to_all | solution.py:338
  49.3 2.0 %encode.1.refs_2_.refs_3_ = f32[4,128,768]{2,1,0:T(8,128)S(1)} custom-call(bf16[128,768]{1,0:T(8,128)(2,1)S(1)} %copy-done, bf16[128,768]{1,0:T(8,128)(2,1)S(1)} %collective-permute-done.6.across_ref.refs_0_, bf16[128,768]{1,0:T(8,128)(2,1)S(1)} %collective-permute-done.7.along_ref.refs_1_, bf16[128,768]{1,0:T(8,128)(2,1)S(1)} %collective-permute-done.8.diagonal_ref.refs_0_, ...), custom_call_target="tpu_custom_call" | custom-call | tf_op jit(solution)/shard_map/encode/pallas_call | solution.py:43
  51.9 1.1 encode_rest.4
  53.0 1.1 collective-permute-start.10
  54.0 1.3 collective-permute-start.11
  56.0 1.3 collective-permute-start.12
  58.0 2.0 %collective-permute-done.10.across_ref = bf16[128,768]{1,0:T(8,128)(2,1)S(1)} collective-permute-done((bf16[128,768]{1,0:T(8,128)(2,1)S(1)}, bf16[128,768]{1,0:T(8,128)(2,1)S(1)}, u32[]{:S(2)}, u32[]{:S(2)}) %collective-permute-start.10) | collective-permute-done | bytes 196640 | tf_op jit(solution)/shard_map/ppermute | solution.py:361
  60.0 1.8 %collective-permute-done.11.along_ref = bf16[128,768]{1,0:T(8,128)(2,1)S(1)} collective-permute-done((bf16[128,768]{1,0:T(8,128)(2,1)S(1)}, bf16[128,768]{1,0:T(8,128)(2,1)S(1)}, u32[]{:S(2)}, u32[]{:S(2)}) %collective-permute-start.11) | collective-permute-done | bytes 196640 | tf_op jit(solution)/shard_map/ppermute | solution.py:364
  61.8 3.6 %collective-permute-done.12.diagonal_ref = bf16[128,768]{1,0:T(8,128)(2,1)S(1)} collective-permute-done((bf16[128,768]{1,0:T(8,128)(2,1)S(1)}, bf16[128,768]{1,0:T(8,128)(2,1)S(1)}, u32[]{:S(2)}, u32[]{:S(2)}) %collective-permute-start.12) | collective-permute-done | bytes 196640 | tf_op jit(solution)/shard_map/ppermute | solution.py:374
  65.4 1.6 place.1
  67.0 24.5 %all_to_all.41 = bf16[64,32,128]{2,1,0:T(8,128)(2,1)S(1)} all-to-all(bf16[64,32,128]{2,1,0:T(8,128)(2,1)S(1)} %bitcast.20), channel_id=1, replica_groups=mesh['role'=4,'shard'=64] {'shard'}, dimensions={0} | all-to-all | bytes 1048576 | tf_op jit(solution)/shard_map/all_to_all | solution.py:433
  91.5 1.6 score.1
  93.1 17.5 %all_to_all.42 = f32[64,1,128]{2,1,0:T(1,128)S(1)} all-to-all(f32[64,1,128]{2,1,0:T(1,128)S(1)} %bitcast.25), channel_id=1, replica_groups=mesh['role'=4,'shard'=64] {'shard'}, dimensions={0} | all-to-all | bytes 65536 | tf_op jit(solution)/shard_map/all_to_all | solution.py:437
  110.6 16.1 %pair.1 = (f32[64,128]{1,0:T(8,128)S(1)}, f32[1,128]{1,0:T(1,128)}) custom-call(f32[64,128]{1,0:T(8,128)S(1)} %bitcast.24, f32[32,128]{1,0:T(8,128)S(1)} %copy-done.2), custom_call_target="tpu_custom_call" | custom-call | tf_op jit(solution)/shard_map/pair/pallas_call | solution.py:261
  126.7 15.6 %all_to_all.43 = f32[64,1,128]{2,1,0:T(1,128)S(1)} all-to-all(f32[64,1,128]{2,1,0:T(1,128)S(1)} %bitcast.26), channel_id=1, replica_groups=mesh['role'=4,'shard'=64] {'shard'}, dimensions={0} | all-to-all | bytes 65536 | tf_op jit(solution)/shard_map/all_to_all | solution.py:442
  142.3 2.0 %share.1 = f32[64,768]{1,0:T(8,128)S(1)} custom-call(f32[64,128]{1,0:T(8,128)S(1)} %bitcast.23, s32[64,128]{1,0:T(8,128)S(1)} %pad_add_fusion.idsg_ref, bf16[256,768]{1,0:T(8,128)(2,1)S(1)} %get-tuple-element.39.refreshed_ref), custom_call_target="tpu_custom_call" | custom-call | tf_op jit(solution)/shard_map/share/pallas_call | solution.py:308
  144.5 16.2 %all_to_all.44 = f32[64,1,768]{2,1,0:T(1,128)S(1)} all-to-all(f32[64,1,768]{2,1,0:T(1,128)S(1)} %copy.14), channel_id=1, replica_groups=mesh['role'=4,'shard'=64] {'shard'}, dimensions={0} | all-to-all | bytes 393216 | tf_op jit(solution)/shard_map/all_to_all | solution.py:444
  (36 shorter events, 4.3 us)
Async XLA Ops:
  1.5 3.1 %collective-permute-start = (bf16[12,1536]{1,0:T(8,128)(2,1)S(1)}, bf16[12,1536]{1,0:T(8,128)(2,1)S(1)}, u32[]{:S(2)}, u32[]{:S(2)}) collective-permute-start(bf16[12,1536]{1,0:T(8,128)(2,1)S(1)} %get-tuple-element.42), channel_id=1, source_target_pairs={{192,128},{193,129},{194,130},{195,131},{196,132},{197,133},{198,1... | collective-permute-start | bytes 110600 | tf_op jit(solution)/shard_map/ppermute | solution.py:386
  2.8 1.8 %collective-permute-start.1 = (bf16[12,1536]{1,0:T(8,128)(2,1)S(1)}, bf16[12,1536]{1,0:T(8,128)(2,1)S(1)}, u32[]{:S(2)}, u32[]{:S(2)}) collective-permute-start(bf16[12,1536]{1,0:T(8,128)(2,1)S(1)} %get-tuple-element.43), channel_id=1, source_target_pairs={{192,64},{193,65},{194,66},{195,67},{196,68},{197,69},{198,70},{19... | collective-permute-start | bytes 110600 | tf_op jit(solution)/shard_map/ppermute | solution.py:386
  3.5 1.2 collective-permute-start.2
  5.4 15.5 %collective-permute-start.5 = (bf16[12,1536]{1,0:T(8,128)(2,1)S(1)}, bf16[12,1536]{1,0:T(8,128)(2,1)S(1)}, u32[]{:S(2)}, u32[]{:S(2)}) collective-permute-start(bf16[12,1536]{1,0:T(8,128)(2,1)S(1)} %fusion.5), channel_id=1, source_target_pairs={{0,12},{1,13},{2,14},{3,15},{4,0},{5,1},{6,2},{7,3},{8,4},{9,5},{1... | collective-permute-start | bytes 110600 | tf_op jit(solution)/shard_map/ppermute | solution.py:397
  11.8 9.1 %collective-permute-start.4 = (bf16[12,1536]{1,0:T(8,128)(2,1)S(1)}, bf16[12,1536]{1,0:T(8,128)(2,1)S(1)}, u32[]{:S(2)}, u32[]{:S(2)}) collective-permute-start(bf16[12,1536]{1,0:T(8,128)(2,1)S(1)} %fusion.5), channel_id=1, source_target_pairs={{0,8},{1,9},{2,10},{3,11},{4,12},{5,13},{6,14},{7,15},{8,0},{9,1},... | collective-permute-start | bytes 110600 | tf_op jit(solution)/shard_map/ppermute | solution.py:397
  12.8 8.1 %collective-permute-start.3 = (bf16[12,1536]{1,0:T(8,128)(2,1)S(1)}, bf16[12,1536]{1,0:T(8,128)(2,1)S(1)}, u32[]{:S(2)}, u32[]{:S(2)}) collective-permute-start(bf16[12,1536]{1,0:T(8,128)(2,1)S(1)} %fusion.5), channel_id=1, source_target_pairs={{0,4},{1,5},{2,6},{3,7},{4,8},{5,9},{6,10},{7,11},{8,12},{9,13},{1... | collective-permute-start | bytes 110600 | tf_op jit(solution)/shard_map/ppermute | solution.py:397
  15.6 9.2 %collective-permute-start.6 = (bf16[128,768]{1,0:T(8,128)(2,1)}, bf16[128,768]{1,0:T(8,128)(2,1)S(1)}, u32[]{:S(2)}, u32[]{:S(2)}) collective-permute-start(bf16[128,768]{1,0:T(8,128)(2,1)} %cls_ref.1), channel_id=1, source_target_pairs={{0,128},{64,192},{128,0},{192,64},{1,129},{65,193},{129,1},{193,65... | collective-permute-start | bytes 589832 | tf_op jit(solution)/shard_map/ppermute | solution.py:361
  26.0 6.2 %copy-start = (bf16[128,768]{1,0:T(8,128)(2,1)S(1)}, bf16[128,768]{1,0:T(8,128)(2,1)}, u32[]{:S(2)}) copy-start(bf16[128,768]{1,0:T(8,128)(2,1)} %cls_ref.1) | copy-start | bytes 589828
  26.0 23.1 %copy-start.6 = (bf16[1,768]{1,0:T(2,128)(2,1)S(1)}, bf16[1,768]{1,0:T(2,128)(2,1)}, u32[]{:S(2)}) copy-start(bf16[1,768]{1,0:T(2,128)(2,1)} %param.14) | copy-start | bytes 4612
  26.0 23.2 %copy-start.4 = (s32[64,64]{1,0:T(8,128)S(1)}, s32[64,64]{1,0:T(8,128)}, u32[]{:S(2)}) copy-start(s32[64,64]{1,0:T(8,128)} %param.16) | copy-start | bytes 49156
  26.0 23.2 %copy-start.5 = (s32[64,64]{1,0:T(8,128)S(1)}, s32[64,64]{1,0:T(8,128)}, u32[]{:S(2)}) copy-start(s32[64,64]{1,0:T(8,128)} %param.15) | copy-start | bytes 49156
  26.0 23.0 %all-to-all-start = ((bf16[8,48,1536]{2,1,0:T(8,128)(2,1)}), bf16[8,48,1536]{2,1,0:T(8,128)(2,1)S(1)}, u32[]{:S(2)}, u32[]{:S(2)}) async-start(bf16[8,48,1536]{2,1,0:T(8,128)(2,1)} %broadcast_in_dim.15), calls=%async_computation | async-start | bytes 2359296 | tf_op jit(solution)/shard_map/all_to_all | solution.py:338
  32.2 6.8 %collective-permute-start.7 = (bf16[128,768]{1,0:T(8,128)(2,1)S(1)}, bf16[128,768]{1,0:T(8,128)(2,1)S(1)}, u32[]{:S(2)}, u32[]{:S(2)}) collective-permute-start(bf16[128,768]{1,0:T(8,128)(2,1)S(1)} %copy-done), channel_id=1, source_target_pairs={{0,2},{1,3},{2,0},{3,1},{4,6},{5,7},{6,4},{7,5},{8,10},{9,11},{10,... | collective-permute-start | bytes 589832 | tf_op jit(solution)/shard_map/ppermute | solution.py:364
  33.3 7.8 %collective-permute-start.8 = (bf16[128,768]{1,0:T(8,128)(2,1)S(1)}, bf16[128,768]{1,0:T(8,128)(2,1)S(1)}, u32[]{:S(2)}, u32[]{:S(2)}) collective-permute-start(bf16[128,768]{1,0:T(8,128)(2,1)S(1)} %collective-permute-done.6.across_ref.refs_0_), channel_id=1, source_target_pairs={{0,2},{1,3},{2,0},{3,1},{4,6},{5,7},{6,4},{7,5},{8,10},{9,11},{10,... | collective-permute-start | bytes 589832 | tf_op jit(solution)/shard_map/ppermute | solution.py:364
  49.0 2.8 %collective-permute-start.9 = (bf16[384,1536]{1,0:T(8,128)(2,1)S(1)}, bf16[384,1536]{1,0:T(8,128)(2,1)S(1)}, u32[]{:S(2)}, u32[]{:S(2)}) collective-permute-start(bf16[384,1536]{1,0:T(8,128)(2,1)S(1)} %bitcast.18), channel_id=1, source_target_pairs={{0,64},{64,0},{128,192},{192,128},{1,65},{65,1},{129,193},{193,129... | collective-permute-start | bytes 3538952 | tf_op jit(solution)/shard_map/ppermute | solution.py:358
  53.0 7.0 %collective-permute-start.10 = (bf16[128,768]{1,0:T(8,128)(2,1)S(1)}, bf16[128,768]{1,0:T(8,128)(2,1)S(1)}, u32[]{:S(2)}, u32[]{:S(2)}) collective-permute-start(bf16[128,768]{1,0:T(8,128)(2,1)S(1)} %get-tuple-element.32), channel_id=1, source_target_pairs={{0,128},{64,192},{128,0},{192,64},{1,129},{65,193},{129,1},{193,65... | collective-permute-start | bytes 589832 | tf_op jit(solution)/shard_map/ppermute | solution.py:361
  54.0 7.8 %collective-permute-start.11 = (bf16[128,768]{1,0:T(8,128)(2,1)S(1)}, bf16[128,768]{1,0:T(8,128)(2,1)S(1)}, u32[]{:S(2)}, u32[]{:S(2)}) collective-permute-start(bf16[128,768]{1,0:T(8,128)(2,1)S(1)} %get-tuple-element.33), channel_id=1, source_target_pairs={{0,2},{1,3},{2,0},{3,1},{4,6},{5,7},{6,4},{7,5},{8,10},{9,11},{10,... | collective-permute-start | bytes 589832 | tf_op jit(solution)/shard_map/ppermute | solution.py:364
  56.0 9.4 %collective-permute-start.12 = (bf16[128,768]{1,0:T(8,128)(2,1)S(1)}, bf16[128,768]{1,0:T(8,128)(2,1)S(1)}, u32[]{:S(2)}, u32[]{:S(2)}) collective-permute-start(bf16[128,768]{1,0:T(8,128)(2,1)S(1)} %encode_rest.5), channel_id=1, source_target_pairs={{0,130},{1,131},{2,128},{3,129},{4,134},{5,135},{6,132},{7,133},{8... | collective-permute-start | bytes 589832 | tf_op jit(solution)/shard_map/ppermute | solution.py:374
  57.3 8.0 %copy-start.3 = (s32[64,1]{0,1:T(1,128)S(1)}, s32[64,1]{0,1:T(1,128)}, u32[]{:S(2)}) copy-start(s32[64,1]{0,1:T(1,128)} %param.13) | copy-start | bytes 772
  65.4 26.1 %copy-start.1 = (bf16[256,768]{1,0:T(8,128)(2,1)S(1)}, bf16[256,768]{1,0:T(8,128)(2,1)}, u32[]{:S(2)}) copy-start(bf16[256,768]{1,0:T(8,128)(2,1)} %stale_ref.1) | copy-start | bytes 1179652
  67.0 43.6 %copy-start.2 = (f32[32,128]{1,0:T(8,128)S(1)}, f32[32,128]{1,0:T(8,128)}, u32[]{:S(2)}) copy-start(f32[32,128]{1,0:T(8,128)} %constant.19.clone.discount_ref) | copy-start | bytes 49156

commit v7 on v6

--- a/solution.py
+++ b/solution.py
@@ -175,7 +175,7 @@
 
 
 def pair_kernel(
-    x_ref, discount_ref, grad_ref, loss_ref, half_s, wide_w, columns, across, rows_s, near_q, far_q
+    x_ref, discount_ref, grad_ref, loss_ref, half_s, wide_w, columns, across, spread_s, rows_s, near_q, far_q
 ):
     x = x_ref[...]
     n_blocks = x.shape[0] // 2
@@ -200,14 +200,16 @@
         columns[...] = jnp.zeros_like(columns)
         values[n_blocks:] = values[:n_blocks]
 
-        def spread(i, _):
-            rows_s[i] = jnp.broadcast_to(values[pl.ds(i, 1), :], (LANES, LANES)).T
-            return 0
-
-        lax.fori_loop(0, n_blocks, spread, 0, unroll=8)
+        def spread(i):
+            spread_s[i] = jnp.broadcast_to(values[pl.ds(i, 1), :], (LANES, LANES)).T
+
+        def collect(i):
+            across[pl.ds(i, 1), :] = jnp.sum(rows_s[i].T, 0, keepdims=True)
 
         def block(i, last):
-            first = [rows_s[i, pl.ds(8 * g, 8), :] for g in range(groups)]
+            first = [spread_s[i, pl.ds(8 * g, 8), :] for g in range(groups)]
+            collect(i)
+            spread(i + 1)
             acc = [jnp.zeros((8, LANES), f32) for _ in range(groups)]
             for d in range(last + 1):
                 k = i + d
@@ -221,20 +223,17 @@
                 if d > 0:
                     columns[k] = columns[k] + ((column[0] + column[1]) + (column[2] + column[3]))
             for g in range(groups):
-                rows_s[i, pl.ds(8 * g, 8), :] = acc[g]
+                rows_s[i + 1, pl.ds(8 * g, 8), :] = acc[g]
             return 0
 
+        rows_s[0] = jnp.zeros((LANES, LANES), f32)
+        spread(0)
         lax.fori_loop(0, span, lambda i, _: block(i, span), 0)
         lax.fori_loop(span, n_blocks, lambda i, _: block(i, span - 1), 0)
-
-        def collect(i, _):
-            across[pl.ds(i, 1), :] = jnp.sum(rows_s[i].T, 0, keepdims=True)
-            return 0
-
-        lax.fori_loop(0, n_blocks, collect, 0, unroll=8)
+        collect(n_blocks)
         folded = jnp.sum(columns[...], 1)
         wrapped = jnp.concatenate((folded[n_blocks:], jnp.zeros((span, LANES), f32)), 0)
-        return across[...] - folded[:n_blocks] - wrapped
+        return across[1:] - folded[:n_blocks] - wrapped
 
     def rank_term(s_i, s_k, kept, at):
         t = jnp.tanh(s_k - s_i)
@@ -268,8 +267,9 @@
             pltpu.VMEM((2 * n_blocks, LANES), f32),
             pltpu.VMEM((2 * n_blocks, LANES), f32),
             pltpu.VMEM((n_blocks + span, 8, LANES), f32),
-            pltpu.VMEM((n_blocks, LANES), f32),
-            pltpu.VMEM((n_blocks, LANES, LANES), f32),
+            pltpu.VMEM((n_blocks + 1, LANES), f32),
+            pltpu.VMEM((n_blocks + 1, LANES, LANES), f32),
+            pltpu.VMEM((n_blocks + 1, LANES, LANES), f32),
             pltpu.VMEM((n_blocks, span, LANES, LANES), f32),
             pltpu.VMEM((span, LANES, LANES), f32),
         ],
@@ -381,21 +381,24 @@
             ],
         )
 
-    pieces = jnp.concatenate((trainer_in[0], trainer_out[0]), 1).reshape(roles, -1, 2 * width)
-    role = lax.axis_index("role")
-    arrived = [lax.ppermute(pieces[k], "role", [(roles - 1, k)]) for k in range(roles - 1)]
-    mine = pieces[roles - 1]
-    for k in range(roles - 1):
-        mine = jnp.where(role == k, arrived[k], mine)
+    axes = ("role", "shard")
+    mine = jnp.concatenate((trainer_in[0], trainer_out[0]), 1)
+    mine = lax.ppermute(
+        mine,
+        axes,
+        [
+            ((roles - 1) * shards + shard_at(y, zz, zl, x), zz * shards + shard_at(y, zz, zl, x))
+            for y, zz, zl, x in everywhere()
+        ],
+    )
     mine, cls_after = barrier((mine, cls_states))
-    block = [mine]
+    block = mine
     for by in range(1, ZZ):
         turn = [
-            (shard_at(y, zz, zl, x), shard_at(y, (zz + by) % ZZ, zl, x))
+            (zz * shards + shard_at(y, zz, zl, x), zz * shards + shard_at(y, (zz + by) % ZZ, zl, x))
             for y, zz, zl, x in everywhere()
         ]
-        block.append(lax.ppermute(mine, "shard", turn))
-    block = jnp.concatenate(block, 0)
+        block = block + lax.ppermute(mine, axes, turn)
     x_across = to_across(cls_after)
     block, x_across, cls_after = barrier((block, x_across, cls_after))
     units = gather_units(block)
@@ -405,6 +408,7 @@
     so_far = first_half(xs, units)
     (diagonal,) = second_half(xs, other_units, so_far, (3,), bf16)
     from_diagonal = to_diagonal(diagonal)
+    other_units, diagonal = barrier((other_units, diagonal))
     across, along = second_half(xs, other_units, so_far, (1, 2), bf16)
     from_across = to_across(across)
     from_along = to_along(along)

time: 162 us -> 159 us (0.981)
  starting transfers between devices: 30 us -> 27.5 us
  blocking collectives: 73.8 us -> 75.5 us
    ppermute x6 -> x4, starting transfers between devices: 12.8 us -> 3.3 us  [the longest x3 2.63 us: per_device(): block = block + lax.ppermute(mine, axes, turn)]
    ppermute x2, starting transfers between devices: 6.34 us -> 12.5 us  [to_across(): return lax.ppermute(v, 'role', [(0, 2), (1, 3), (2, 0), (3, 1)])]
    ppermute x1, waiting for transfers between devices: 3.56 us -> 0.01 us  [to_diagonal(): lax.ppermute(v, ('role', 'shard'), [(r * shards + shard_at(y, zz, zl, x),...]
    ppermute x6 -> x4, waiting for transfers between devices: 0.49 us -> 3.6 us  [the longest x3 3.6 us: per_device(): block = block + lax.ppermute(mine, axes, turn)]
    ppermute x1, starting transfers between devices: 0.01 us -> 2.89 us  [to_core(): return lax.ppermute(v, 'role', [(0, 1), (1, 0), (2, 3), (3, 2)])]
  transfers between devices with their start and end apart: 14 -> 12, of which waited for: 9 -> 7; matrix products, arithmetic and copies ran while one was open for 0% -> 0% of each run, Pallas kernels for 2% -> 2%
where the time goes in v7:
time: 159 us; the launch traced here: 158 us
  blocking collectives  75.5 us (47%)
  starting transfers between devices  27.5 us (17%)
  waiting for transfers between devices  25.9 us (16%)
  Pallas kernels  24.8 us (16%)
  local copies, waits for them, and re-layouts  2.05 us (1%)
    all_to_all x1, blocking collectives, per_device(): lax.all_to_all(outgoing.reshape(shards, ROWS, LANES), 'shard', split_axis...  26.1 us
    all_to_all x1, blocking collectives, per_device(): lax.all_to_all(packed, 'shard', split_axis=0, concat_axis=0, tiled=True)  17.6 us
    all_to_all x1, blocking collectives, per_device(): lax.all_to_all(shares, 'shard', split_axis=0, concat_axis=0, tiled=True)  16.2 us
    all_to_all x1, blocking collectives, per_device(): lax.all_to_all(grads, 'shard', split_axis=0, concat_axis=0, tiled=True)  15.7 us
    pallas_call x1, Pallas kernels, pair(): pl.pallas_call(pair_kernel, out_shape=(jax.ShapeDtypeStruct(x.shape, f32)...  15.4 us
    ppermute x2, starting transfers between devices, to_across(): return lax.ppermute(v, 'role', [(0, 2), (1, 3), (2, 0), (3, 1)])  12.5 us
    all_to_all x1, waiting for transfers between devices, gather_units(): lax.all_to_all(jnp.broadcast_to(block[None], (parts, units, width)), 'sha...  7.7 us
    ppermute x3, waiting for transfers between devices, to_along(): lax.ppermute(v, 'shard', [(shard_at(y, zz, zl, x), shard_at(y, zz, 1 - zl...  7.18 us
  transfers between devices with their start and end apart: 12, of which 7 were waited for; matrix products, arithmetic and copies ran while one was open for 0% of the time, Pallas kernels for 2%

profile of v7, /device:TPU:2, one launch (start us, length us, event | category | flops | bytes accessed | tf_op | source)
XLA Modules:
  0.0 157.9 jit_solution(12414915944375943121)
XLA Ops:
  0.6 0.9 pad_maximum_fusion
  1.6 0.7 collective-permute-start
  2.3 0.7 collective-permute-start.3
  2.9 1.3 collective-permute-start.2
  4.2 0.7 collective-permute-start.1
  4.9 9.4 %collective-permute-start.4 = (bf16[128,768]{1,0:T(8,128)(2,1)}, bf16[128,768]{1,0:T(8,128)(2,1)S(1)}, u32[]{:S(2)}, u32[]{:S(2)}) collective-permute-start(bf16[128,768]{1,0:T(8,128)(2,1)} %cls_ref.1), channel_id=1, source_target_pairs={{0,128},{64,192},{128,0},{192,64},{1,129},{65,193},{129,1},{193,65... | collective-permute-start | bytes 589832 | tf_op jit(solution)/shard_map/ppermute | solution.py:361
  14.3 3.6 %collective-permute-done.2 = bf16[48,1536]{1,0:T(8,128)(2,1)S(1)} collective-permute-done((bf16[48,1536]{1,0:T(8,128)(2,1)S(1)}, bf16[48,1536]{1,0:T(8,128)(2,1)S(1)}, u32[]{:S(2)}, u32[]{:S(2)}) %collective-permute-start.2) | collective-permute-done | bytes 147488 | tf_op jit(solution)/shard_map/ppermute | solution.py:401
  18.2 1.1 broadcast_in_dim.15
  19.3 6.1 %all-to-all-start = ((bf16[8,48,1536]{2,1,0:T(8,128)(2,1)}), bf16[8,48,1536]{2,1,0:T(8,128)(2,1)S(1)}, u32[]{:S(2)}, u32[]{:S(2)}) async-start(bf16[8,48,1536]{2,1,0:T(8,128)(2,1)} %broadcast_in_dim.15), calls=%async_computation | async-start | bytes 2359296 | tf_op jit(solution)/shard_map/all_to_all | solution.py:338
  25.5 1.6 %collective-permute-start.5 = (bf16[128,768]{1,0:T(8,128)(2,1)S(1)}, bf16[128,768]{1,0:T(8,128)(2,1)S(1)}, u32[]{:S(2)}, u32[]{:S(2)}) collective-permute-start(bf16[128,768]{1,0:T(8,128)(2,1)S(1)} %copy-done), channel_id=1, source_target_pairs={{0,2},{1,3},{2,0},{3,1},{4,6},{5,7},{6,4},{7,5},{8,10},{9,11},{10,... | collective-permute-start | bytes 589832 | tf_op jit(solution)/shard_map/ppermute | solution.py:364
  27.1 0.5 collective-permute-start.6
  27.6 3.6 %collective-permute-done.5.along_ref.refs_1_ = bf16[128,768]{1,0:T(8,128)(2,1)S(1)} collective-permute-done((bf16[128,768]{1,0:T(8,128)(2,1)S(1)}, bf16[128,768]{1,0:T(8,128)(2,1)S(1)}, u32[]{:S(2)}, u32[]{:S(2)}) %collective-permute-start.5) | collective-permute-done | bytes 196640 | tf_op jit(solution)/shard_map/ppermute | solution.py:364
  31.2 3.5 %collective-permute-done.6.diagonal_ref.refs_0_ = bf16[128,768]{1,0:T(8,128)(2,1)S(1)} collective-permute-done((bf16[128,768]{1,0:T(8,128)(2,1)S(1)}, bf16[128,768]{1,0:T(8,128)(2,1)S(1)}, u32[]{:S(2)}, u32[]{:S(2)}) %collective-permute-start.6) | collective-permute-done | bytes 196640 | tf_op jit(solution)/shard_map/ppermute | solution.py:364
  34.8 7.7 %all-to-all-done = bf16[8,48,1536]{2,1,0:T(8,128)(2,1)S(1)} async-done(((bf16[8,48,1536]{2,1,0:T(8,128)(2,1)}), bf16[8,48,1536]{2,1,0:T(8,128)(2,1)S(1)}, u32[]{:S(2)}, u32[]{:S(2)}) %all-to-all-start) | async-done | bytes 1179680 | tf_op jit(solution)/shard_map/all_to_all | solution.py:338
  42.5 2.9 %collective-permute-start.7 = (bf16[384,1536]{1,0:T(8,128)(2,1)S(1)}, bf16[384,1536]{1,0:T(8,128)(2,1)S(1)}, u32[]{:S(2)}, u32[]{:S(2)}) collective-permute-start(bf16[384,1536]{1,0:T(8,128)(2,1)S(1)} %bitcast.18), channel_id=1, source_target_pairs={{0,64},{64,0},{128,192},{192,128},{1,65},{65,1},{129,193},{193,129... | collective-permute-start | bytes 3538952 | tf_op jit(solution)/shard_map/ppermute | solution.py:358
  45.6 2.0 %encode.1.refs_2_.refs_3_ = f32[4,128,768]{2,1,0:T(8,128)S(1)} custom-call(bf16[128,768]{1,0:T(8,128)(2,1)S(1)} %copy-done, bf16[128,768]{1,0:T(8,128)(2,1)S(1)} %collective-permute-done.4.across_ref.refs_0_, bf16[128,768]{1,0:T(8,128)(2,1)S(1)} %collective-permute-done.5.along_ref.refs_1_, bf16[128,768]{1,0:T(8,128)(2,1)S(1)} %collective-permute-done.6.diagonal_ref.refs_0_, ...), custom_call_target="tpu_custom_call" | custom-call | tf_op jit(solution)/shard_map/encode/pallas_call | solution.py:43
  47.6 0.3 collective-permute-done.7.refs_1_.refs_2_
  47.8 0.6 encode_rest.3
  48.6 1.1 encode_rest.5
  49.6 3.1 %collective-permute-start.8 = (bf16[128,768]{1,0:T(8,128)(2,1)S(1)}, bf16[128,768]{1,0:T(8,128)(2,1)S(1)}, u32[]{:S(2)}, u32[]{:S(2)}) collective-permute-start(bf16[128,768]{1,0:T(8,128)(2,1)S(1)} %get-tuple-element.34), channel_id=1, source_target_pairs={{0,128},{64,192},{128,0},{192,64},{1,129},{65,193},{129,1},{193,65... | collective-permute-start | bytes 589832 | tf_op jit(solution)/shard_map/ppermute | solution.py:361
  52.7 0.5 collective-permute-start.9
  53.3 0.6 encode_rest.4.own_ref
  53.9 6.9 %collective-permute-done.8.across_ref = bf16[128,768]{1,0:T(8,128)(2,1)S(1)} collective-permute-done((bf16[128,768]{1,0:T(8,128)(2,1)S(1)}, bf16[128,768]{1,0:T(8,128)(2,1)S(1)}, u32[]{:S(2)}, u32[]{:S(2)}) %collective-permute-start.8) | collective-permute-done | bytes 196640 | tf_op jit(solution)/shard_map/ppermute | solution.py:361
  60.9 1.6 place.1
  62.4 26.1 %all_to_all.41 = bf16[64,32,128]{2,1,0:T(8,128)(2,1)S(1)} all-to-all(bf16[64,32,128]{2,1,0:T(8,128)(2,1)S(1)} %bitcast.20), channel_id=1, replica_groups=mesh['role'=4,'shard'=64] {'shard'}, dimensions={0} | all-to-all | bytes 1048576 | tf_op jit(solution)/shard_map/all_to_all | solution.py:437
  88.5 1.6 %score.1 = (bf16[256,768]{1,0:T(8,128)(2,1)}, bf16[256,768]{1,0:T(8,128)(2,1)S(1)}, f32[64,128]{1,0:T(8,128)S(1)}) custom-call(bf16[2048,128]{1,0:T(8,128)(2,1)S(1)} %bitcast.21, bf16[256,768]{1,0:T(8,128)(2,1)S(1)} %copy-done.1, s32[64,128]{1,0:T(8,128)S(1)} %pad_add_fusion.idsg_ref), custom_call_target="tpu_custom_call" | custom-call | tf_op jit(solution)/shard_map/score/pallas_call | solution.py:158
  90.1 17.6 %all_to_all.42 = f32[64,1,128]{2,1,0:T(1,128)S(1)} all-to-all(f32[64,1,128]{2,1,0:T(1,128)S(1)} %bitcast.25), channel_id=1, replica_groups=mesh['role'=4,'shard'=64] {'shard'}, dimensions={0} | all-to-all | bytes 65536 | tf_op jit(solution)/shard_map/all_to_all | solution.py:441
  107.8 15.4 %pair.1 = (f32[64,128]{1,0:T(8,128)S(1)}, f32[1,128]{1,0:T(1,128)}) custom-call(f32[64,128]{1,0:T(8,128)S(1)} %bitcast.24, f32[32,128]{1,0:T(8,128)S(1)} %copy-done.2), custom_call_target="tpu_custom_call" | custom-call | tf_op jit(solution)/shard_map/pair/pallas_call | solution.py:260
  123.1 15.7 %all_to_all.43 = f32[64,1,128]{2,1,0:T(1,128)S(1)} all-to-all(f32[64,1,128]{2,1,0:T(1,128)S(1)} %bitcast.26), channel_id=1, replica_groups=mesh['role'=4,'shard'=64] {'shard'}, dimensions={0} | all-to-all | bytes 65536 | tf_op jit(solution)/shard_map/all_to_all | solution.py:446
  138.8 2.0 %share.1 = f32[64,768]{1,0:T(8,128)S(1)} custom-call(f32[64,128]{1,0:T(8,128)S(1)} %bitcast.23, s32[64,128]{1,0:T(8,128)S(1)} %pad_add_fusion.idsg_ref, bf16[256,768]{1,0:T(8,128)(2,1)S(1)} %get-tuple-element.41.refreshed_ref), custom_call_target="tpu_custom_call" | custom-call | tf_op jit(solution)/shard_map/share/pallas_call | solution.py:308
  141.0 16.2 %all_to_all.44 = f32[64,1,768]{2,1,0:T(1,128)S(1)} all-to-all(f32[64,1,768]{2,1,0:T(1,128)S(1)} %copy.14), channel_id=1, replica_groups=mesh['role'=4,'shard'=64] {'shard'}, dimensions={0} | all-to-all | bytes 393216 | tf_op jit(solution)/shard_map/all_to_all | solution.py:448
  157.3 0.6 broadcast_in_dim.18
  (31 shorter events, 1.0 us)
Async XLA Ops:
  1.6 0.7 collective-permute-start
  2.3 12.0 %collective-permute-start.3 = (bf16[48,1536]{1,0:T(8,128)(2,1)S(1)}, bf16[48,1536]{1,0:T(8,128)(2,1)S(1)}, u32[]{:S(2)}, u32[]{:S(2)}) collective-permute-start(bf16[48,1536]{1,0:T(8,128)(2,1)S(1)} %collective-permute-done), channel_id=1, source_target_pairs={{0,12},{1,13},{2,14},{3,15},{68,64},{69,65},{70,66},{71,67},{136,1... | collective-permute-start | bytes 442376 | tf_op jit(solution)/shard_map/ppermute | solution.py:401
  2.9 15.0 %collective-permute-start.2 = (bf16[48,1536]{1,0:T(8,128)(2,1)S(1)}, bf16[48,1536]{1,0:T(8,128)(2,1)S(1)}, u32[]{:S(2)}, u32[]{:S(2)}) collective-permute-start(bf16[48,1536]{1,0:T(8,128)(2,1)S(1)} %collective-permute-done), channel_id=1, source_target_pairs={{0,8},{1,9},{2,10},{3,11},{68,76},{69,77},{70,78},{71,79},{136,128... | collective-permute-start | bytes 442376 | tf_op jit(solution)/shard_map/ppermute | solution.py:401
  4.2 13.7 %collective-permute-start.1 = (bf16[48,1536]{1,0:T(8,128)(2,1)S(1)}, bf16[48,1536]{1,0:T(8,128)(2,1)S(1)}, u32[]{:S(2)}, u32[]{:S(2)}) collective-permute-start(bf16[48,1536]{1,0:T(8,128)(2,1)S(1)} %collective-permute-done), channel_id=1, source_target_pairs={{0,4},{1,5},{2,6},{3,7},{68,72},{69,73},{70,74},{71,75},{136,140},... | collective-permute-start | bytes 442376 | tf_op jit(solution)/shard_map/ppermute | solution.py:401
  4.9 13.2 %collective-permute-start.4 = (bf16[128,768]{1,0:T(8,128)(2,1)}, bf16[128,768]{1,0:T(8,128)(2,1)S(1)}, u32[]{:S(2)}, u32[]{:S(2)}) collective-permute-start(bf16[128,768]{1,0:T(8,128)(2,1)} %cls_ref.1), channel_id=1, source_target_pairs={{0,128},{64,192},{128,0},{192,64},{1,129},{65,193},{129,1},{193,65... | collective-permute-start | bytes 589832 | tf_op jit(solution)/shard_map/ppermute | solution.py:361
  19.3 6.2 %copy-start = (bf16[128,768]{1,0:T(8,128)(2,1)S(1)}, bf16[128,768]{1,0:T(8,128)(2,1)}, u32[]{:S(2)}) copy-start(bf16[128,768]{1,0:T(8,128)(2,1)} %cls_ref.1) | copy-start | bytes 589828
  19.3 26.1 %copy-start.6 = (bf16[1,768]{1,0:T(2,128)(2,1)S(1)}, bf16[1,768]{1,0:T(2,128)(2,1)}, u32[]{:S(2)}) copy-start(bf16[1,768]{1,0:T(2,128)(2,1)} %param.14) | copy-start | bytes 4612
  19.3 26.2 %copy-start.4 = (s32[64,64]{1,0:T(8,128)S(1)}, s32[64,64]{1,0:T(8,128)}, u32[]{:S(2)}) copy-start(s32[64,64]{1,0:T(8,128)} %param.16) | copy-start | bytes 49156
  19.3 26.2 %copy-start.5 = (s32[64,64]{1,0:T(8,128)S(1)}, s32[64,64]{1,0:T(8,128)}, u32[]{:S(2)}) copy-start(s32[64,64]{1,0:T(8,128)} %param.15) | copy-start | bytes 49156
  19.3 23.1 %all-to-all-start = ((bf16[8,48,1536]{2,1,0:T(8,128)(2,1)}), bf16[8,48,1536]{2,1,0:T(8,128)(2,1)S(1)}, u32[]{:S(2)}, u32[]{:S(2)}) async-start(bf16[8,48,1536]{2,1,0:T(8,128)(2,1)} %broadcast_in_dim.15), calls=%async_computation | async-start | bytes 2359296 | tf_op jit(solution)/shard_map/all_to_all | solution.py:338
  25.5 5.8 %collective-permute-start.5 = (bf16[128,768]{1,0:T(8,128)(2,1)S(1)}, bf16[128,768]{1,0:T(8,128)(2,1)S(1)}, u32[]{:S(2)}, u32[]{:S(2)}) collective-permute-start(bf16[128,768]{1,0:T(8,128)(2,1)S(1)} %copy-done), channel_id=1, source_target_pairs={{0,2},{1,3},{2,0},{3,1},{4,6},{5,7},{6,4},{7,5},{8,10},{9,11},{10,... | collective-permute-start | bytes 589832 | tf_op jit(solution)/shard_map/ppermute | solution.py:364
  27.1 7.7 %collective-permute-start.6 = (bf16[128,768]{1,0:T(8,128)(2,1)S(1)}, bf16[128,768]{1,0:T(8,128)(2,1)S(1)}, u32[]{:S(2)}, u32[]{:S(2)}) collective-permute-start(bf16[128,768]{1,0:T(8,128)(2,1)S(1)} %collective-permute-done.4.across_ref.refs_0_), channel_id=1, source_target_pairs={{0,2},{1,3},{2,0},{3,1},{4,6},{5,7},{6,4},{7,5},{8,10},{9,11},{10,... | collective-permute-start | bytes 589832 | tf_op jit(solution)/shard_map/ppermute | solution.py:364
  42.5 5.4 %collective-permute-start.7 = (bf16[384,1536]{1,0:T(8,128)(2,1)S(1)}, bf16[384,1536]{1,0:T(8,128)(2,1)S(1)}, u32[]{:S(2)}, u32[]{:S(2)}) collective-permute-start(bf16[384,1536]{1,0:T(8,128)(2,1)S(1)} %bitcast.18), channel_id=1, source_target_pairs={{0,64},{64,0},{128,192},{192,128},{1,65},{65,1},{129,193},{193,129... | collective-permute-start | bytes 3538952 | tf_op jit(solution)/shard_map/ppermute | solution.py:358
  48.4 12.4 %collective-permute-start.10 = (bf16[128,768]{1,0:T(8,128)(2,1)S(1)}, bf16[128,768]{1,0:T(8,128)(2,1)S(1)}, u32[]{:S(2)}, u32[]{:S(2)}) collective-permute-start(bf16[128,768]{1,0:T(8,128)(2,1)S(1)} %encode_rest.3), channel_id=1, source_target_pairs={{0,130},{1,131},{2,128},{3,129},{4,134},{5,135},{6,132},{7,133},{8... | collective-permute-start | bytes 589832 | tf_op jit(solution)/shard_map/ppermute | solution.py:374
  49.6 11.2 %collective-permute-start.8 = (bf16[128,768]{1,0:T(8,128)(2,1)S(1)}, bf16[128,768]{1,0:T(8,128)(2,1)S(1)}, u32[]{:S(2)}, u32[]{:S(2)}) collective-permute-start(bf16[128,768]{1,0:T(8,128)(2,1)S(1)} %get-tuple-element.34), channel_id=1, source_target_pairs={{0,128},{64,192},{128,0},{192,64},{1,129},{65,193},{129,1},{193,65... | collective-permute-start | bytes 589832 | tf_op jit(solution)/shard_map/ppermute | solution.py:361
  52.7 8.1 %collective-permute-start.9 = (bf16[128,768]{1,0:T(8,128)(2,1)S(1)}, bf16[128,768]{1,0:T(8,128)(2,1)S(1)}, u32[]{:S(2)}, u32[]{:S(2)}) collective-permute-start(bf16[128,768]{1,0:T(8,128)(2,1)S(1)} %get-tuple-element.35), channel_id=1, source_target_pairs={{0,2},{1,3},{2,0},{3,1},{4,6},{5,7},{6,4},{7,5},{8,10},{9,11},{10,... | collective-permute-start | bytes 589832 | tf_op jit(solution)/shard_map/ppermute | solution.py:364
  53.3 7.6 %copy-start.3 = (s32[64,1]{0,1:T(1,128)S(1)}, s32[64,1]{0,1:T(1,128)}, u32[]{:S(2)}) copy-start(s32[64,1]{0,1:T(1,128)} %param.13) | copy-start | bytes 772
  60.8 27.7 %copy-start.1 = (bf16[256,768]{1,0:T(8,128)(2,1)S(1)}, bf16[256,768]{1,0:T(8,128)(2,1)}, u32[]{:S(2)}) copy-start(bf16[256,768]{1,0:T(8,128)(2,1)} %stale_ref.1) | copy-start | bytes 1179652
  62.4 45.4 %copy-start.2 = (f32[32,128]{1,0:T(8,128)S(1)}, f32[32,128]{1,0:T(8,128)}, u32[]{:S(2)}) copy-start(f32[32,128]{1,0:T(8,128)} %constant.2.clone.discount_ref) | copy-start | bytes 49156

commit v8 on v7

--- a/solution.py
+++ b/solution.py
@@ -64,7 +64,7 @@
     )(*(xs[n] for n in at), units, so_far)
 
 
-ROWS = 32
+ROWS, SUB = 32, 8
 
 
 def place_kernel(
@@ -72,8 +72,7 @@
 ):
     rows, width = cls_ref.shape
     blocks = owner_ref.shape[1]
-    total = out_ref.shape[0]
-    shards = total // ROWS
+    shards = out_ref.shape[0] // SUB
     chunks = width // LANES
     resid = cls_ref[...].astype(f32) + own_ref[...]
     for part_ref in (across_ref, along_ref, diagonal_ref):
@@ -98,11 +97,12 @@
     )
     both = jnp.dot(both.astype(bf16), widen, preferred_element_type=f32)
     parity = lax.broadcasted_iota(jnp.int32, (1, rows), 1) & 1
-    target = both[0:1] * ROWS + (both[8:9] * 2.0 + parity.astype(f32)) * chunks
-
-    row = lax.broadcasted_iota(jnp.int32, (total, rows), 0).astype(f32)
-    placed = jnp.zeros((total, LANES), f32)
-    taken = jnp.zeros((total, rows), f32)
+    target = both[0:1] * (2.0 * CAP * chunks) + (both[8:9] * 2.0 + parity.astype(f32)) * chunks
+
+    passage_rows = 2 * CAP * chunks
+    row = lax.broadcasted_iota(jnp.int32, (shards * passage_rows, rows), 0).astype(f32)
+    placed = jnp.zeros((shards * passage_rows, LANES), f32)
+    taken = jnp.zeros((shards * passage_rows, rows), f32)
     for j in range(chunks):
         onto = (row == target + float(j)).astype(f32)
         taken = taken + onto
@@ -110,14 +110,20 @@
             onto.astype(bf16), fresh[:, j * LANES : (j + 1) * LANES], preferred_element_type=f32
         )
     filled = jnp.dot(taken.astype(bf16), jnp.ones((rows, LANES), bf16), preferred_element_type=f32)
-    rest = jnp.broadcast_to(query_ref[...].astype(f32)[None], (shards, ROWS, LANES))
-    out_ref[...] = jnp.where(filled > 0.5, placed, rest.reshape(total, LANES)).astype(bf16)
+    placed = jnp.where(filled > 0.5, placed, EMPTY).reshape(shards, passage_rows, LANES)
+    for tile in range(ROWS // SUB):
+        if tile < passage_rows // SUB:
+            part = placed[:, tile * SUB : (tile + 1) * SUB]
+        else:
+            part = jnp.broadcast_to(query_ref[...].astype(f32)[None], (shards, SUB, LANES))
+        part = part.reshape(shards * SUB, LANES).astype(bf16)
+        out_ref[:, tile * LANES : (tile + 1) * LANES] = part
 
 
 def place(cls_states, own, across, along, diagonal, owner, query, shards):
     return pl.pallas_call(
         place_kernel,
-        out_shape=jax.ShapeDtypeStruct((shards * ROWS, LANES), bf16),
+        out_shape=jax.ShapeDtypeStruct((shards * SUB, ROWS // SUB * LANES), bf16),
         compiler_params=params(),
         name="place",
     )(cls_states, own, across, along, diagonal, owner, query)
@@ -127,17 +133,20 @@
     recv_ref, stale_ref, idsg_ref, refreshed_ref, again_ref, packed_ref, recv_s, arrived_s
 ):
     cache_rows, width = stale_ref.shape
-    shards = recv_ref.shape[0] // ROWS
+    shards = recv_ref.shape[0] // SUB
     chunks = width // LANES
     per_shard = cache_rows // shards
-    recv_s[...] = recv_ref[...].astype(f32)
+    for tile in range(ROWS // SUB):
+        recv_s[tile] = recv_ref[:, tile * LANES : (tile + 1) * LANES].astype(f32)
+
+    def arrived_row(r):
+        return recv_s[r // SUB, pl.ds(r % SUB, shards, stride=SUB), :]
+
     queries = []
     for j in range(chunks):
         for c in range(per_shard):
-            arrived_s[j, pl.ds(c, shards, stride=per_shard), :] = recv_s[
-                pl.ds(c * chunks + j, shards, stride=ROWS), :
-            ]
-        queries.append(recv_s[pl.ds(per_shard * chunks + j, shards, stride=ROWS), :])
+            arrived_s[j, pl.ds(c, shards, stride=per_shard), :] = arrived_row(c * chunks + j)
+        queries.append(arrived_row(per_shard * chunks + j))
     queries = jnp.concatenate(queries, 1).astype(bf16)
     arrived = jnp.concatenate([arrived_s[j] for j in range(chunks)], 1)
     refreshed = jnp.where(arrived > 0.5 * EMPTY, stale_ref[...].astype(f32), arrived).astype(bf16)
@@ -163,7 +172,7 @@
             jax.ShapeDtypeStruct(idsg.shape, f32),
         ),
         scratch_shapes=[
-            pltpu.VMEM(recv.shape, f32),
+            pltpu.VMEM((ROWS // SUB, recv.shape[0], LANES), f32),
             pltpu.VMEM((stale.shape[1] // LANES, stale.shape[0], LANES), f32),
         ],
         compiler_params=params(),
@@ -381,13 +390,17 @@
             ],
         )
 
+    role_of = (0, 2, 1, 3)
     axes = ("role", "shard")
     mine = jnp.concatenate((trainer_in[0], trainer_out[0]), 1)
     mine = lax.ppermute(
         mine,
         axes,
         [
-            ((roles - 1) * shards + shard_at(y, zz, zl, x), zz * shards + shard_at(y, zz, zl, x))
+            (
+                (roles - 1) * shards + shard_at(y, zz, zl, x),
+                role_of[zz] * shards + shard_at(y, zz, zl, x),
+            )
             for y, zz, zl, x in everywhere()
         ],
     )
@@ -395,7 +408,10 @@
     block = mine
     for by in range(1, ZZ):
         turn = [
-            (zz * shards + shard_at(y, zz, zl, x), zz * shards + shard_at(y, (zz + by) % ZZ, zl, x))
+            (
+                role_of[zz] * shards + shard_at(y, zz, zl, x),
+                role_of[zz] * shards + shard_at(y, (zz + by) % ZZ, zl, x),
+            )
             for y, zz, zl, x in everywhere()
         ]
         block = block + lax.ppermute(mine, axes, turn)
@@ -413,15 +429,7 @@
     from_across = to_across(across)
     from_along = to_along(along)
     (own,) = second_half(xs, other_units, so_far, (0,), f32)
-    chunks = width // LANES
-    rest = jnp.concatenate(
-        (
-            jnp.full((2 * CAP * chunks, LANES), EMPTY, bf16),
-            queries.reshape(chunks, LANES),
-            jnp.full((ROWS - (2 * CAP + 1) * chunks, LANES), EMPTY, bf16),
-        ),
-        0,
-    )
+    query = jnp.pad(queries.reshape(-1, LANES), ((0, SUB - width // LANES), (0, 0)))
     idsg = jnp.concatenate((neg_ids, grades), 1)
     outgoing = place(
         cls_states,
@@ -430,14 +438,14 @@
         from_along,
         from_diagonal,
         block_owner.reshape(1, -1),
-        rest,
+        query,
         shards,
     )
-    outgoing, idsg = lax.optimization_barrier((outgoing, idsg))
+    outgoing, idsg = barrier((outgoing, idsg))
     arrived = lax.all_to_all(
-        outgoing.reshape(shards, ROWS, LANES), "shard", split_axis=0, concat_axis=0, tiled=True
-    )
-    refreshed, again, packed = score(arrived.reshape(-1, LANES), stale_cache, idsg)
+        outgoing.reshape(shards, SUB, -1), "shard", split_axis=0, concat_axis=0, tiled=True
+    )
+    refreshed, again, packed = score(arrived.reshape(shards * SUB, -1), stale_cache, idsg)
     packed = lax.all_to_all(packed, "shard", split_axis=0, concat_axis=0, tiled=True)
     count = shards * neg_ids.shape[1]
     position = np.arange(1, count + 1, dtype=np.float64)

time: 159 us -> 161 us (1.013)
  waiting for transfers between devices: 25.9 us -> 28.5 us
  Pallas kernels: 24.8 us -> 26.8 us
  starting transfers between devices: 27.5 us -> 25.5 us
    ppermute x3, waiting for transfers between devices: 3.6 us -> 0.01 us  [per_device(): block = block + lax.ppermute(mine, axes, turn)]
    ppermute x1, waiting for transfers between devices: 0.01 us -> 3.24 us  [to_diagonal(): lax.ppermute(v, ('role', 'shard'), [(r * shards + shard_at(y, zz, zl, x),...]
    ppermute x3, waiting for transfers between devices: 7.18 us -> 9.65 us  [to_along(): lax.ppermute(v, 'shard', [(shard_at(y, zz, zl, x), shard_at(y, zz, 1 - zl...]
    ppermute x1, starting transfers between devices: 2.89 us -> 1.06 us  [to_core(): return lax.ppermute(v, 'role', [(0, 1), (1, 0), (2, 3), (3, 2)])]
    all_to_all x1, waiting for transfers between devices: 7.7 us -> 9.33 us  [gather_units(): lax.all_to_all(jnp.broadcast_to(block[None], (parts, units, width)), 'sha...]
  transfers between devices with their start and end apart: 12 -> 12, of which waited for: 7 -> 7; matrix products, arithmetic and copies ran while one was open for 0% -> 1% of each run, Pallas kernels for 2% -> 2%
where the time goes in v8:
time: 161 us
  blocking collectives  75.3 us (47%)
  waiting for transfers between devices  28.5 us (18%)
  Pallas kernels  26.8 us (17%)
  starting transfers between devices  25.5 us (16%)
  other arithmetic  1.99 us (1%)
  local copies, waits for them, and re-layouts  1.93 us (1%)
    all_to_all x1, blocking collectives, per_device(): lax.all_to_all(outgoing.reshape(shards, SUB, -1), 'shard', split_axis=0,...  25.7 us
    all_to_all x1, blocking collectives, per_device(): lax.all_to_all(packed, 'shard', split_axis=0, concat_axis=0, tiled=True)  17.6 us
    all_to_all x1, blocking collectives, per_device(): lax.all_to_all(shares, 'shard', split_axis=0, concat_axis=0, tiled=True)  16.2 us
    all_to_all x1, blocking collectives, per_device(): lax.all_to_all(grads, 'shard', split_axis=0, concat_axis=0, tiled=True)  15.8 us
    pallas_call x1, Pallas kernels, pair(): pl.pallas_call(pair_kernel, out_shape=(jax.ShapeDtypeStruct(x.shape, f32)...  15.4 us
    ppermute x2, starting transfers between devices, to_across(): return lax.ppermute(v, 'role', [(0, 2), (1, 3), (2, 0), (3, 1)])  11 us
    ppermute x3, waiting for transfers between devices, to_along(): lax.ppermute(v, 'shard', [(shard_at(y, zz, zl, x), shard_at(y, zz, 1 - zl...  9.65 us
    all_to_all x1, waiting for transfers between devices, gather_units(): lax.all_to_all(jnp.broadcast_to(block[None], (parts, units, width)), 'sha...  9.33 us
  transfers between devices with their start and end apart: 12, of which 7 were waited for; matrix products, arithmetic and copies ran while one was open for 1% of the time, Pallas kernels for 2%

profile of v8, /device:TPU:2, one launch (start us, length us, event | category | flops | bytes accessed | tf_op | source)
XLA Modules:
  0.0 160.7 jit_solution(13344461848614101875)
XLA Ops:
  0.6 0.9 pad_maximum_fusion
  1.6 0.7 collective-permute-start
  2.3 1.3 collective-permute-start.3
  3.6 0.7 collective-permute-start.2
  4.2 0.7 collective-permute-start.1
  4.9 9.4 %collective-permute-start.4 = (bf16[128,768]{1,0:T(8,128)(2,1)}, bf16[128,768]{1,0:T(8,128)(2,1)S(1)}, u32[]{:S(2)}, u32[]{:S(2)}) collective-permute-start(bf16[128,768]{1,0:T(8,128)(2,1)} %cls_ref.1), channel_id=1, source_target_pairs={{0,128},{64,192},{128,0},{192,64},{1,129},{65,193},{129,1},{193,65... | collective-permute-start | bytes 589832 | tf_op jit(solution)/shard_map/ppermute | solution.py:370
  14.3 3.8 %collective-permute-done.4.across_ref.refs_0_ = bf16[128,768]{1,0:T(8,128)(2,1)S(1)} collective-permute-done((bf16[128,768]{1,0:T(8,128)(2,1)}, bf16[128,768]{1,0:T(8,128)(2,1)S(1)}, u32[]{:S(2)}, u32[]{:S(2)}) %collective-permute-start.4) | collective-permute-done | bytes 196640 | tf_op jit(solution)/shard_map/ppermute | solution.py:370
  18.2 1.1 broadcast_in_dim.4
  19.3 6.1 %all-to-all-start = ((bf16[8,48,1536]{2,1,0:T(8,128)(2,1)}), bf16[8,48,1536]{2,1,0:T(8,128)(2,1)}, u32[]{:S(2)}, u32[]{:S(2)}) async-start(bf16[8,48,1536]{2,1,0:T(8,128)(2,1)} %broadcast_in_dim.4), calls=%async_computation | async-start | bytes 2359296 | tf_op jit(solution)/shard_map/all_to_all | solution.py:347
  25.4 1.1 collective-permute-start.5
  26.5 1.0 collective-permute-start.6
  27.5 3.6 %collective-permute-done.5.along_ref.refs_1_ = bf16[128,768]{1,0:T(8,128)(2,1)S(1)} collective-permute-done((bf16[128,768]{1,0:T(8,128)(2,1)S(1)}, bf16[128,768]{1,0:T(8,128)(2,1)S(1)}, u32[]{:S(2)}, u32[]{:S(2)}) %collective-permute-start.5) | collective-permute-done | bytes 196640 | tf_op jit(solution)/shard_map/ppermute | solution.py:373
  31.2 3.8 %collective-permute-done.6.diagonal_ref.refs_0_ = bf16[128,768]{1,0:T(8,128)(2,1)S(1)} collective-permute-done((bf16[128,768]{1,0:T(8,128)(2,1)S(1)}, bf16[128,768]{1,0:T(8,128)(2,1)S(1)}, u32[]{:S(2)}, u32[]{:S(2)}) %collective-permute-start.6) | collective-permute-done | bytes 196640 | tf_op jit(solution)/shard_map/ppermute | solution.py:373
  35.0 9.3 %all-to-all-done = bf16[8,48,1536]{2,1,0:T(8,128)(2,1)} async-done(((bf16[8,48,1536]{2,1,0:T(8,128)(2,1)}), bf16[8,48,1536]{2,1,0:T(8,128)(2,1)}, u32[]{:S(2)}, u32[]{:S(2)}) %all-to-all-start) | async-done | bytes 1179680 | tf_op jit(solution)/shard_map/all_to_all | solution.py:347
  44.3 1.1 collective-permute-start.7
  45.4 3.3 %encode.1.refs_2_.refs_3_ = f32[4,128,768]{2,1,0:T(8,128)S(1)} custom-call(bf16[128,768]{1,0:T(8,128)(2,1)S(1)} %copy-done, bf16[128,768]{1,0:T(8,128)(2,1)S(1)} %collective-permute-done.4.across_ref.refs_0_, bf16[128,768]{1,0:T(8,128)(2,1)S(1)} %collective-permute-done.5.along_ref.refs_1_, bf16[128,768]{1,0:T(8,128)(2,1)S(1)} %collective-permute-done.6.diagonal_ref.refs_0_, ...), custom_call_target="tpu_custom_call" | custom-call | tf_op jit(solution)/shard_map/encode/pallas_call | solution.py:43
  48.7 1.3 encode_rest.3
  50.0 1.7 %encode_rest.5 = (bf16[128,768]{1,0:T(8,128)(2,1)}, bf16[128,768]{1,0:T(8,128)(2,1)}) custom-call(bf16[128,768]{1,0:T(8,128)(2,1)S(1)} %collective-permute-done.4.across_ref.refs_0_, bf16[128,768]{1,0:T(8,128)(2,1)S(1)} %collective-permute-done.5.along_ref.refs_1_, bf16[384,1536]{1,0:T(8,128)(2,1)S(1)} %collective-permute-done.7.refs_1_.refs_2_, ...), custom_call_target="tpu_custom_call" | custom-call | tf_op jit(solution)/shard_map/encode_rest/pallas_call | solution.py:59
  51.7 1.7 %collective-permute-start.8 = (bf16[128,768]{1,0:T(8,128)(2,1)}, bf16[128,768]{1,0:T(8,128)(2,1)S(1)}, u32[]{:S(2)}, u32[]{:S(2)}) collective-permute-start(bf16[128,768]{1,0:T(8,128)(2,1)} %get-tuple-element.34), channel_id=1, source_target_pairs={{0,128},{64,192},{128,0},{192,64},{1,129},{65,193},{129,1},{193,65... | collective-permute-start | bytes 589832 | tf_op jit(solution)/shard_map/ppermute | solution.py:370
  53.4 1.3 collective-permute-start.9
  55.3 0.9 pad_add_fusion.idsg_ref
  56.7 2.4 %collective-permute-done.8.across_ref = bf16[128,768]{1,0:T(8,128)(2,1)S(1)} collective-permute-done((bf16[128,768]{1,0:T(8,128)(2,1)}, bf16[128,768]{1,0:T(8,128)(2,1)S(1)}, u32[]{:S(2)}, u32[]{:S(2)}) %collective-permute-start.8) | collective-permute-done | bytes 196640 | tf_op jit(solution)/shard_map/ppermute | solution.py:370
  59.2 2.2 %collective-permute-done.9.along_ref = bf16[128,768]{1,0:T(8,128)(2,1)S(1)} collective-permute-done((bf16[128,768]{1,0:T(8,128)(2,1)}, bf16[128,768]{1,0:T(8,128)(2,1)S(1)}, u32[]{:S(2)}, u32[]{:S(2)}) %collective-permute-start.9) | collective-permute-done | bytes 196640 | tf_op jit(solution)/shard_map/ppermute | solution.py:373
  61.3 3.2 %collective-permute-done.10.diagonal_ref = bf16[128,768]{1,0:T(8,128)(2,1)S(1)} collective-permute-done((bf16[128,768]{1,0:T(8,128)(2,1)}, bf16[128,768]{1,0:T(8,128)(2,1)S(1)}, u32[]{:S(2)}, u32[]{:S(2)}) %collective-permute-start.10) | collective-permute-done | bytes 196640 | tf_op jit(solution)/shard_map/ppermute | solution.py:383
  64.6 1.3 place.1
  65.9 25.7 %all_to_all.41 = bf16[64,8,512]{2,1,0:T(8,128)(2,1)S(1)} all-to-all(bf16[64,8,512]{2,1,0:T(8,128)(2,1)S(1)} %bitcast.18), channel_id=1, replica_groups=mesh['role'=4,'shard'=64] {'shard'}, dimensions={0} | all-to-all | bytes 1048576 | tf_op jit(solution)/shard_map/all_to_all | solution.py:445
  91.6 1.2 score.1
  92.8 17.6 %all_to_all.42 = f32[64,1,128]{2,1,0:T(1,128)S(1)} all-to-all(f32[64,1,128]{2,1,0:T(1,128)S(1)} %bitcast.23), channel_id=1, replica_groups=mesh['role'=4,'shard'=64] {'shard'}, dimensions={0} | all-to-all | bytes 65536 | tf_op jit(solution)/shard_map/all_to_all | solution.py:449
  110.4 15.4 %pair.1 = (f32[64,128]{1,0:T(8,128)S(1)}, f32[1,128]{1,0:T(1,128)}) custom-call(f32[64,128]{1,0:T(8,128)S(1)} %bitcast.22, f32[32,128]{1,0:T(8,128)S(1)} %copy-done.2), custom_call_target="tpu_custom_call" | custom-call | tf_op jit(solution)/shard_map/pair/pallas_call | solution.py:269
  125.8 15.8 %all_to_all.43 = f32[64,1,128]{2,1,0:T(1,128)S(1)} all-to-all(f32[64,1,128]{2,1,0:T(1,128)S(1)} %bitcast.24), channel_id=1, replica_groups=mesh['role'=4,'shard'=64] {'shard'}, dimensions={0} | all-to-all | bytes 65536 | tf_op jit(solution)/shard_map/all_to_all | solution.py:454
  141.6 2.0 %share.1 = f32[64,768]{1,0:T(8,128)S(1)} custom-call(f32[64,128]{1,0:T(8,128)S(1)} %bitcast.21, s32[64,128]{1,0:T(8,128)S(1)} %pad_add_fusion.idsg_ref, bf16[256,768]{1,0:T(8,128)(2,1)S(1)} %get-tuple-element.41.refreshed_ref), custom_call_target="tpu_custom_call" | custom-call | tf_op jit(solution)/shard_map/share/pallas_call | solution.py:317
  143.8 16.2 %all_to_all.44 = f32[64,1,768]{2,1,0:T(1,128)S(1)} all-to-all(f32[64,1,768]{2,1,0:T(1,128)S(1)} %copy.14), channel_id=1, replica_groups=mesh['role'=4,'shard'=64] {'shard'}, dimensions={0} | all-to-all | bytes 393216 | tf_op jit(solution)/shard_map/all_to_all | solution.py:456
  (23 shorter events, 2.2 us)
Async XLA Ops:
  1.6 0.7 collective-permute-start
  2.3 12.0 %collective-permute-start.3 = (bf16[48,1536]{1,0:T(8,128)(2,1)S(1)}, bf16[48,1536]{1,0:T(8,128)(2,1)S(1)}, u32[]{:S(2)}, u32[]{:S(2)}) collective-permute-start(bf16[48,1536]{1,0:T(8,128)(2,1)S(1)} %collective-permute-done), channel_id=1, source_target_pairs={{0,12},{1,13},{2,14},{3,15},{132,128},{133,129},{134,130},{135,131... | collective-permute-start | bytes 442376 | tf_op jit(solution)/shard_map/ppermute | solution.py:417
  3.6 10.7 %collective-permute-start.2 = (bf16[48,1536]{1,0:T(8,128)(2,1)S(1)}, bf16[48,1536]{1,0:T(8,128)(2,1)S(1)}, u32[]{:S(2)}, u32[]{:S(2)}) collective-permute-start(bf16[48,1536]{1,0:T(8,128)(2,1)S(1)} %collective-permute-done), channel_id=1, source_target_pairs={{0,8},{1,9},{2,10},{3,11},{132,140},{133,141},{134,142},{135,143},... | collective-permute-start | bytes 442376 | tf_op jit(solution)/shard_map/ppermute | solution.py:417
  4.2 10.1 %collective-permute-start.1 = (bf16[48,1536]{1,0:T(8,128)(2,1)S(1)}, bf16[48,1536]{1,0:T(8,128)(2,1)S(1)}, u32[]{:S(2)}, u32[]{:S(2)}) collective-permute-start(bf16[48,1536]{1,0:T(8,128)(2,1)S(1)} %collective-permute-done), channel_id=1, source_target_pairs={{0,4},{1,5},{2,6},{3,7},{132,136},{133,137},{134,138},{135,139},{7... | collective-permute-start | bytes 442376 | tf_op jit(solution)/shard_map/ppermute | solution.py:417
  4.9 13.2 %collective-permute-start.4 = (bf16[128,768]{1,0:T(8,128)(2,1)}, bf16[128,768]{1,0:T(8,128)(2,1)S(1)}, u32[]{:S(2)}, u32[]{:S(2)}) collective-permute-start(bf16[128,768]{1,0:T(8,128)(2,1)} %cls_ref.1), channel_id=1, source_target_pairs={{0,128},{64,192},{128,0},{192,64},{1,129},{65,193},{129,1},{193,65... | collective-permute-start | bytes 589832 | tf_op jit(solution)/shard_map/ppermute | solution.py:370
  19.3 6.1 %copy-start = (bf16[128,768]{1,0:T(8,128)(2,1)S(1)}, bf16[128,768]{1,0:T(8,128)(2,1)}, u32[]{:S(2)}) copy-start(bf16[128,768]{1,0:T(8,128)(2,1)} %cls_ref.1) | copy-start | bytes 589828
  19.3 25.1 %all-to-all-start = ((bf16[8,48,1536]{2,1,0:T(8,128)(2,1)}), bf16[8,48,1536]{2,1,0:T(8,128)(2,1)}, u32[]{:S(2)}, u32[]{:S(2)}) async-start(bf16[8,48,1536]{2,1,0:T(8,128)(2,1)} %broadcast_in_dim.4), calls=%async_computation | async-start | bytes 2359296 | tf_op jit(solution)/shard_map/all_to_all | solution.py:347
  25.4 5.8 %collective-permute-start.5 = (bf16[128,768]{1,0:T(8,128)(2,1)S(1)}, bf16[128,768]{1,0:T(8,128)(2,1)S(1)}, u32[]{:S(2)}, u32[]{:S(2)}) collective-permute-start(bf16[128,768]{1,0:T(8,128)(2,1)S(1)} %copy-done), channel_id=1, source_target_pairs={{0,2},{1,3},{2,0},{3,1},{4,6},{5,7},{6,4},{7,5},{8,10},{9,11},{10,... | collective-permute-start | bytes 589832 | tf_op jit(solution)/shard_map/ppermute | solution.py:373
  26.5 8.5 %collective-permute-start.6 = (bf16[128,768]{1,0:T(8,128)(2,1)S(1)}, bf16[128,768]{1,0:T(8,128)(2,1)S(1)}, u32[]{:S(2)}, u32[]{:S(2)}) collective-permute-start(bf16[128,768]{1,0:T(8,128)(2,1)S(1)} %collective-permute-done.4.across_ref.refs_0_), channel_id=1, source_target_pairs={{0,2},{1,3},{2,0},{3,1},{4,6},{5,7},{6,4},{7,5},{8,10},{9,11},{10,... | collective-permute-start | bytes 589832 | tf_op jit(solution)/shard_map/ppermute | solution.py:373
  44.3 4.3 %collective-permute-start.7 = (bf16[384,1536]{1,0:T(8,128)(2,1)}, bf16[384,1536]{1,0:T(8,128)(2,1)S(1)}, u32[]{:S(2)}, u32[]{:S(2)}) collective-permute-start(bf16[384,1536]{1,0:T(8,128)(2,1)} %bitcast.2.w_ref), channel_id=1, source_target_pairs={{0,64},{64,0},{128,192},{192,128},{1,65},{65,1},{129,193},{193,129... | collective-permute-start | bytes 3538952 | tf_op jit(solution)/shard_map/ppermute | solution.py:367
  50.0 5.2 %copy-start.4 = (bf16[1,768]{1,0:T(2,128)(2,1)S(1)}, bf16[1,768]{1,0:T(2,128)(2,1)}, u32[]{:S(2)}) copy-start(bf16[1,768]{1,0:T(2,128)(2,1)} %param.14) | copy-start | bytes 4612
  51.7 7.4 %collective-permute-start.8 = (bf16[128,768]{1,0:T(8,128)(2,1)}, bf16[128,768]{1,0:T(8,128)(2,1)S(1)}, u32[]{:S(2)}, u32[]{:S(2)}) collective-permute-start(bf16[128,768]{1,0:T(8,128)(2,1)} %get-tuple-element.34), channel_id=1, source_target_pairs={{0,128},{64,192},{128,0},{192,64},{1,129},{65,193},{129,1},{193,65... | collective-permute-start | bytes 589832 | tf_op jit(solution)/shard_map/ppermute | solution.py:370
  53.4 7.9 %collective-permute-start.9 = (bf16[128,768]{1,0:T(8,128)(2,1)}, bf16[128,768]{1,0:T(8,128)(2,1)S(1)}, u32[]{:S(2)}, u32[]{:S(2)}) collective-permute-start(bf16[128,768]{1,0:T(8,128)(2,1)} %get-tuple-element.35), channel_id=1, source_target_pairs={{0,2},{1,3},{2,0},{3,1},{4,6},{5,7},{6,4},{7,5},{8,10},{9,11},{10,... | collective-permute-start | bytes 589832 | tf_op jit(solution)/shard_map/ppermute | solution.py:373
  54.7 9.8 %collective-permute-start.10 = (bf16[128,768]{1,0:T(8,128)(2,1)}, bf16[128,768]{1,0:T(8,128)(2,1)S(1)}, u32[]{:S(2)}, u32[]{:S(2)}) collective-permute-start(bf16[128,768]{1,0:T(8,128)(2,1)} %encode_rest.3), channel_id=1, source_target_pairs={{0,130},{1,131},{2,128},{3,129},{4,134},{5,135},{6,132},{7,133},{8... | collective-permute-start | bytes 589832 | tf_op jit(solution)/shard_map/ppermute | solution.py:383
  56.1 8.5 %copy-start.3 = (s32[64,1]{0,1:T(1,128)S(1)}, s32[64,1]{0,1:T(1,128)}, u32[]{:S(2)}) copy-start(s32[64,1]{0,1:T(1,128)} %param.13) | copy-start | bytes 772
  64.6 27.0 %copy-start.1 = (bf16[256,768]{1,0:T(8,128)(2,1)S(1)}, bf16[256,768]{1,0:T(8,128)(2,1)}, u32[]{:S(2)}) copy-start(bf16[256,768]{1,0:T(8,128)(2,1)} %stale_ref.1) | copy-start | bytes 1179652
  65.8 44.5 %copy-start.2 = (f32[32,128]{1,0:T(8,128)S(1)}, f32[32,128]{1,0:T(8,128)}, u32[]{:S(2)}) copy-start(f32[32,128]{1,0:T(8,128)} %constant.7.clone.discount_ref) | copy-start | bytes 49156

commit v9 on v8

--- a/solution.py
+++ b/solution.py
@@ -19,8 +19,8 @@
 LANES = 128
 
 
-def params():
-    return pltpu.CompilerParams(vmem_limit_bytes=48 * 1024 * 1024)
+def params(mebibytes=16):
+    return pltpu.CompilerParams(vmem_limit_bytes=mebibytes * 1024 * 1024)
 
 
 def contract_last(a, b):
@@ -282,7 +282,7 @@
             pltpu.VMEM((n_blocks, span, LANES, LANES), f32),
             pltpu.VMEM((span, LANES, LANES), f32),
         ],
-        compiler_params=params(),
+        compiler_params=params(44),
         name="pair",
     )(x, discount)
 
@@ -419,7 +419,9 @@
     block, x_across, cls_after = barrier((block, x_across, cls_after))
     units = gather_units(block)
     xs = (cls_states, x_across, to_along(cls_after), to_along(x_across))
-    units, xs = barrier((units, xs))
+    query = jnp.pad(queries.reshape(-1, LANES), ((0, SUB - width // LANES), (0, 0)))
+    idsg = jnp.concatenate((neg_ids, grades), 1)
+    units, xs, query, idsg = barrier((units, xs, query, idsg))
     other_units = to_core(units)
     so_far = first_half(xs, units)
     (diagonal,) = second_half(xs, other_units, so_far, (3,), bf16)
@@ -429,8 +431,6 @@
     from_across = to_across(across)
     from_along = to_along(along)
     (own,) = second_half(xs, other_units, so_far, (0,), f32)
-    query = jnp.pad(queries.reshape(-1, LANES), ((0, SUB - width // LANES), (0, 0)))
-    idsg = jnp.concatenate((neg_ids, grades), 1)
     outgoing = place(
         cls_states,
         own,

time: 161 us -> 158 us (0.981)
  Pallas kernels: 26.8 us -> 24.1 us
  transfers between devices with their start and end apart: 12 -> 12, of which waited for: 7 -> 8; matrix products, arithmetic and copies ran while one was open for 1% -> 0% of each run, Pallas kernels for 2% -> 2%
where the time goes in v9:
time: 158 us
  blocking collectives  74.9 us (47%)
  waiting for transfers between devices  29.4 us (19%)
  starting transfers between devices  25.7 us (16%)
  Pallas kernels  24.1 us (15%)
  local copies, waits for them, and re-layouts  1.96 us (1%)
    all_to_all x1, blocking collectives, per_device(): lax.all_to_all(outgoing.reshape(shards, SUB, -1), 'shard', split_axis=0,...  25.3 us
    all_to_all x1, blocking collectives, per_device(): lax.all_to_all(packed, 'shard', split_axis=0, concat_axis=0, tiled=True)  17.5 us
    all_to_all x1, blocking collectives, per_device(): lax.all_to_all(shares, 'shard', split_axis=0, concat_axis=0, tiled=True)  16.2 us
    all_to_all x1, blocking collectives, per_device(): lax.all_to_all(grads, 'shard', split_axis=0, concat_axis=0, tiled=True)  15.8 us
    pallas_call x1, Pallas kernels, pair(): pl.pallas_call(pair_kernel, out_shape=(jax.ShapeDtypeStruct(x.shape, f32)...  15.4 us
    ppermute x2, starting transfers between devices, to_across(): return lax.ppermute(v, 'role', [(0, 2), (1, 3), (2, 0), (3, 1)])  11.5 us
    ppermute x3, waiting for transfers between devices, to_along(): lax.ppermute(v, 'shard', [(shard_at(y, zz, zl, x), shard_at(y, zz, 1 - zl...  9.96 us
    all_to_all x1, waiting for transfers between devices, gather_units(): lax.all_to_all(jnp.broadcast_to(block[None], (parts, units, width)), 'sha...  9.22 us
  transfers between devices with their start and end apart: 12, of which 8 were waited for; matrix products, arithmetic and copies ran while one was open for 0% of the time, Pallas kernels for 2%

profile of v9, /device:TPU:2, one launch (start us, length us, event | category | flops | bytes accessed | tf_op | source)
XLA Modules:
  0.0 158.0 jit_solution(5786632069679117180)
XLA Ops:
  0.6 0.9 pad_maximum_fusion
  1.6 0.7 collective-permute-start
  2.3 1.3 collective-permute-start.3
  3.6 0.7 collective-permute-start.2
  4.2 0.7 collective-permute-start.1
  4.9 9.4 %collective-permute-start.4 = (bf16[128,768]{1,0:T(8,128)(2,1)}, bf16[128,768]{1,0:T(8,128)(2,1)S(1)}, u32[]{:S(2)}, u32[]{:S(2)}) collective-permute-start(bf16[128,768]{1,0:T(8,128)(2,1)} %cls_ref.1), channel_id=1, source_target_pairs={{0,128},{64,192},{128,0},{192,64},{1,129},{65,193},{129,1},{193,65... | collective-permute-start | bytes 589832 | tf_op jit(solution)/shard_map/ppermute | solution.py:370
  14.3 3.8 %collective-permute-done.4.across_ref.refs_0_ = bf16[128,768]{1,0:T(8,128)(2,1)S(1)} collective-permute-done((bf16[128,768]{1,0:T(8,128)(2,1)}, bf16[128,768]{1,0:T(8,128)(2,1)S(1)}, u32[]{:S(2)}, u32[]{:S(2)}) %collective-permute-start.4) | collective-permute-done | bytes 196640 | tf_op jit(solution)/shard_map/ppermute | solution.py:370
  18.2 1.1 broadcast_in_dim.4
  19.3 6.1 %all-to-all-start = ((bf16[8,48,1536]{2,1,0:T(8,128)(2,1)}), bf16[8,48,1536]{2,1,0:T(8,128)(2,1)S(1)}, u32[]{:S(2)}, u32[]{:S(2)}) async-start(bf16[8,48,1536]{2,1,0:T(8,128)(2,1)} %broadcast_in_dim.4), calls=%async_computation | async-start | bytes 2359296 | tf_op jit(solution)/shard_map/all_to_all | solution.py:347
  25.5 1.1 collective-permute-start.5
  26.6 1.0 collective-permute-start.6
  27.7 3.5 %collective-permute-done.5.along_ref.refs_1_ = bf16[128,768]{1,0:T(8,128)(2,1)S(1)} collective-permute-done((bf16[128,768]{1,0:T(8,128)(2,1)S(1)}, bf16[128,768]{1,0:T(8,128)(2,1)S(1)}, u32[]{:S(2)}, u32[]{:S(2)}) %collective-permute-start.5) | collective-permute-done | bytes 196640 | tf_op jit(solution)/shard_map/ppermute | solution.py:373
  31.2 3.8 %collective-permute-done.6.diagonal_ref.refs_0_ = bf16[128,768]{1,0:T(8,128)(2,1)S(1)} collective-permute-done((bf16[128,768]{1,0:T(8,128)(2,1)S(1)}, bf16[128,768]{1,0:T(8,128)(2,1)S(1)}, u32[]{:S(2)}, u32[]{:S(2)}) %collective-permute-start.6) | collective-permute-done | bytes 196640 | tf_op jit(solution)/shard_map/ppermute | solution.py:373
  35.1 9.2 %all-to-all-done = bf16[8,48,1536]{2,1,0:T(8,128)(2,1)S(1)} async-done(((bf16[8,48,1536]{2,1,0:T(8,128)(2,1)}), bf16[8,48,1536]{2,1,0:T(8,128)(2,1)S(1)}, u32[]{:S(2)}, u32[]{:S(2)}) %all-to-all-start) | async-done | bytes 1179680 | tf_op jit(solution)/shard_map/all_to_all | solution.py:347
  44.3 1.1 collective-permute-start.7
  45.3 2.0 %encode.1.refs_2_.refs_3_ = f32[4,128,768]{2,1,0:T(8,128)S(1)} custom-call(bf16[128,768]{1,0:T(8,128)(2,1)S(1)} %copy-done, bf16[128,768]{1,0:T(8,128)(2,1)S(1)} %collective-permute-done.4.across_ref.refs_0_, bf16[128,768]{1,0:T(8,128)(2,1)S(1)} %collective-permute-done.5.along_ref.refs_1_, bf16[128,768]{1,0:T(8,128)(2,1)S(1)} %collective-permute-done.6.diagonal_ref.refs_0_, ...), custom_call_target="tpu_custom_call" | custom-call | tf_op jit(solution)/shard_map/encode/pallas_call | solution.py:43
  47.8 0.6 encode_rest.3
  48.4 1.1 encode_rest.5
  49.5 2.1 %collective-permute-start.8 = (bf16[128,768]{1,0:T(8,128)(2,1)S(1)}, bf16[128,768]{1,0:T(8,128)(2,1)S(1)}, u32[]{:S(2)}, u32[]{:S(2)}) collective-permute-start(bf16[128,768]{1,0:T(8,128)(2,1)S(1)} %get-tuple-element.36), channel_id=1, source_target_pairs={{0,128},{64,192},{128,0},{192,64},{1,129},{65,193},{129,1},{193,65... | collective-permute-start | bytes 589832 | tf_op jit(solution)/shard_map/ppermute | solution.py:370
  51.7 1.3 collective-permute-start.9
  53.2 0.6 encode_rest.4.own_ref
  53.9 3.0 %collective-permute-done.8.across_ref = bf16[128,768]{1,0:T(8,128)(2,1)S(1)} collective-permute-done((bf16[128,768]{1,0:T(8,128)(2,1)S(1)}, bf16[128,768]{1,0:T(8,128)(2,1)S(1)}, u32[]{:S(2)}, u32[]{:S(2)}) %collective-permute-start.8) | collective-permute-done | bytes 196640 | tf_op jit(solution)/shard_map/ppermute | solution.py:370
  56.8 2.6 %collective-permute-done.9.along_ref = bf16[128,768]{1,0:T(8,128)(2,1)S(1)} collective-permute-done((bf16[128,768]{1,0:T(8,128)(2,1)S(1)}, bf16[128,768]{1,0:T(8,128)(2,1)S(1)}, u32[]{:S(2)}, u32[]{:S(2)}) %collective-permute-start.9) | collective-permute-done | bytes 196640 | tf_op jit(solution)/shard_map/ppermute | solution.py:373
  59.4 2.9 %collective-permute-done.10.diagonal_ref = bf16[128,768]{1,0:T(8,128)(2,1)S(1)} collective-permute-done((bf16[128,768]{1,0:T(8,128)(2,1)S(1)}, bf16[128,768]{1,0:T(8,128)(2,1)S(1)}, u32[]{:S(2)}, u32[]{:S(2)}) %collective-permute-start.10) | collective-permute-done | bytes 196640 | tf_op jit(solution)/shard_map/ppermute | solution.py:383
  62.4 1.3 place.1
  63.6 25.3 %all_to_all.41 = bf16[64,8,512]{2,1,0:T(8,128)(2,1)S(1)} all-to-all(bf16[64,8,512]{2,1,0:T(8,128)(2,1)S(1)} %bitcast.20), channel_id=1, replica_groups=mesh['role'=4,'shard'=64] {'shard'}, dimensions={0} | all-to-all | bytes 1048576 | tf_op jit(solution)/shard_map/all_to_all | solution.py:445
  89.0 1.2 score.1
  90.2 17.5 %all_to_all.42 = f32[64,1,128]{2,1,0:T(1,128)S(1)} all-to-all(f32[64,1,128]{2,1,0:T(1,128)S(1)} %bitcast.25), channel_id=1, replica_groups=mesh['role'=4,'shard'=64] {'shard'}, dimensions={0} | all-to-all | bytes 65536 | tf_op jit(solution)/shard_map/all_to_all | solution.py:449
  107.7 15.4 %pair.1 = (f32[64,128]{1,0:T(8,128)S(1)}, f32[1,128]{1,0:T(1,128)}) custom-call(f32[64,128]{1,0:T(8,128)S(1)} %bitcast.24, f32[32,128]{1,0:T(8,128)S(1)} %copy-done.2), custom_call_target="tpu_custom_call" | custom-call | tf_op jit(solution)/shard_map/pair/pallas_call | solution.py:269
  123.1 15.8 %all_to_all.43 = f32[64,1,128]{2,1,0:T(1,128)S(1)} all-to-all(f32[64,1,128]{2,1,0:T(1,128)S(1)} %bitcast.26), channel_id=1, replica_groups=mesh['role'=4,'shard'=64] {'shard'}, dimensions={0} | all-to-all | bytes 65536 | tf_op jit(solution)/shard_map/all_to_all | solution.py:454
  138.9 2.0 %share.1 = f32[64,768]{1,0:T(8,128)S(1)} custom-call(f32[64,128]{1,0:T(8,128)S(1)} %bitcast.23, s32[64,128]{1,0:T(8,128)S(1)} %pad_add_fusion.idsg_ref, bf16[256,768]{1,0:T(8,128)(2,1)S(1)} %get-tuple-element.45.refreshed_ref), custom_call_target="tpu_custom_call" | custom-call | tf_op jit(solution)/shard_map/share/pallas_call | solution.py:317
  141.1 16.2 %all_to_all.44 = f32[64,1,768]{2,1,0:T(1,128)S(1)} all-to-all(f32[64,1,768]{2,1,0:T(1,128)S(1)} %copy.14), channel_id=1, replica_groups=mesh['role'=4,'shard'=64] {'shard'}, dimensions={0} | all-to-all | bytes 393216 | tf_op jit(solution)/shard_map/all_to_all | solution.py:456
  (27 shorter events, 1.8 us)
Async XLA Ops:
  1.6 0.7 collective-permute-start
  2.3 12.0 %collective-permute-start.3 = (bf16[48,1536]{1,0:T(8,128)(2,1)S(1)}, bf16[48,1536]{1,0:T(8,128)(2,1)S(1)}, u32[]{:S(2)}, u32[]{:S(2)}) collective-permute-start(bf16[48,1536]{1,0:T(8,128)(2,1)S(1)} %collective-permute-done), channel_id=1, source_target_pairs={{0,12},{1,13},{2,14},{3,15},{132,128},{133,129},{134,130},{135,131... | collective-permute-start | bytes 442376 | tf_op jit(solution)/shard_map/ppermute | solution.py:417
  3.6 10.7 %collective-permute-start.2 = (bf16[48,1536]{1,0:T(8,128)(2,1)S(1)}, bf16[48,1536]{1,0:T(8,128)(2,1)S(1)}, u32[]{:S(2)}, u32[]{:S(2)}) collective-permute-start(bf16[48,1536]{1,0:T(8,128)(2,1)S(1)} %collective-permute-done), channel_id=1, source_target_pairs={{0,8},{1,9},{2,10},{3,11},{132,140},{133,141},{134,142},{135,143},... | collective-permute-start | bytes 442376 | tf_op jit(solution)/shard_map/ppermute | solution.py:417
  4.2 10.1 %collective-permute-start.1 = (bf16[48,1536]{1,0:T(8,128)(2,1)S(1)}, bf16[48,1536]{1,0:T(8,128)(2,1)S(1)}, u32[]{:S(2)}, u32[]{:S(2)}) collective-permute-start(bf16[48,1536]{1,0:T(8,128)(2,1)S(1)} %collective-permute-done), channel_id=1, source_target_pairs={{0,4},{1,5},{2,6},{3,7},{132,136},{133,137},{134,138},{135,139},{7... | collective-permute-start | bytes 442376 | tf_op jit(solution)/shard_map/ppermute | solution.py:417
  4.9 13.2 %collective-permute-start.4 = (bf16[128,768]{1,0:T(8,128)(2,1)}, bf16[128,768]{1,0:T(8,128)(2,1)S(1)}, u32[]{:S(2)}, u32[]{:S(2)}) collective-permute-start(bf16[128,768]{1,0:T(8,128)(2,1)} %cls_ref.1), channel_id=1, source_target_pairs={{0,128},{64,192},{128,0},{192,64},{1,129},{65,193},{129,1},{193,65... | collective-permute-start | bytes 589832 | tf_op jit(solution)/shard_map/ppermute | solution.py:370
  19.3 6.2 %copy-start = (bf16[128,768]{1,0:T(8,128)(2,1)S(1)}, bf16[128,768]{1,0:T(8,128)(2,1)}, u32[]{:S(2)}) copy-start(bf16[128,768]{1,0:T(8,128)(2,1)} %cls_ref.1) | copy-start | bytes 589828
  19.3 8.3 %copy-start.6 = (bf16[1,768]{1,0:T(2,128)(2,1)S(1)}, bf16[1,768]{1,0:T(2,128)(2,1)}, u32[]{:S(2)}) copy-start(bf16[1,768]{1,0:T(2,128)(2,1)} %param.14) | copy-start | bytes 4612
  19.3 8.3 %copy-start.4 = (s32[64,64]{1,0:T(8,128)S(1)}, s32[64,64]{1,0:T(8,128)}, u32[]{:S(2)}) copy-start(s32[64,64]{1,0:T(8,128)} %param.16) | copy-start | bytes 49156
  19.3 8.3 %copy-start.5 = (s32[64,64]{1,0:T(8,128)S(1)}, s32[64,64]{1,0:T(8,128)}, u32[]{:S(2)}) copy-start(s32[64,64]{1,0:T(8,128)} %param.15) | copy-start | bytes 49156
  19.3 25.0 %all-to-all-start = ((bf16[8,48,1536]{2,1,0:T(8,128)(2,1)}), bf16[8,48,1536]{2,1,0:T(8,128)(2,1)S(1)}, u32[]{:S(2)}, u32[]{:S(2)}) async-start(bf16[8,48,1536]{2,1,0:T(8,128)(2,1)} %broadcast_in_dim.4), calls=%async_computation | async-start | bytes 2359296 | tf_op jit(solution)/shard_map/all_to_all | solution.py:347
  25.5 5.8 %collective-permute-start.5 = (bf16[128,768]{1,0:T(8,128)(2,1)S(1)}, bf16[128,768]{1,0:T(8,128)(2,1)S(1)}, u32[]{:S(2)}, u32[]{:S(2)}) collective-permute-start(bf16[128,768]{1,0:T(8,128)(2,1)S(1)} %copy-done), channel_id=1, source_target_pairs={{0,2},{1,3},{2,0},{3,1},{4,6},{5,7},{6,4},{7,5},{8,10},{9,11},{10,... | collective-permute-start | bytes 589832 | tf_op jit(solution)/shard_map/ppermute | solution.py:373
  26.6 8.5 %collective-permute-start.6 = (bf16[128,768]{1,0:T(8,128)(2,1)S(1)}, bf16[128,768]{1,0:T(8,128)(2,1)S(1)}, u32[]{:S(2)}, u32[]{:S(2)}) collective-permute-start(bf16[128,768]{1,0:T(8,128)(2,1)S(1)} %collective-permute-done.4.across_ref.refs_0_), channel_id=1, source_target_pairs={{0,2},{1,3},{2,0},{3,1},{4,6},{5,7},{6,4},{7,5},{8,10},{9,11},{10,... | collective-permute-start | bytes 589832 | tf_op jit(solution)/shard_map/ppermute | solution.py:373
  44.3 3.5 %collective-permute-start.7 = (bf16[384,1536]{1,0:T(8,128)(2,1)S(1)}, bf16[384,1536]{1,0:T(8,128)(2,1)S(1)}, u32[]{:S(2)}, u32[]{:S(2)}) collective-permute-start(bf16[384,1536]{1,0:T(8,128)(2,1)S(1)} %bitcast.18), channel_id=1, source_target_pairs={{0,64},{64,0},{128,192},{192,128},{1,65},{65,1},{129,193},{193,129... | collective-permute-start | bytes 3538952 | tf_op jit(solution)/shard_map/ppermute | solution.py:367
  49.5 7.3 %collective-permute-start.8 = (bf16[128,768]{1,0:T(8,128)(2,1)S(1)}, bf16[128,768]{1,0:T(8,128)(2,1)S(1)}, u32[]{:S(2)}, u32[]{:S(2)}) collective-permute-start(bf16[128,768]{1,0:T(8,128)(2,1)S(1)} %get-tuple-element.36), channel_id=1, source_target_pairs={{0,128},{64,192},{128,0},{192,64},{1,129},{65,193},{129,1},{193,65... | collective-permute-start | bytes 589832 | tf_op jit(solution)/shard_map/ppermute | solution.py:370
  51.7 10.7 %copy-start.3 = (s32[64,1]{0,1:T(1,128)S(1)}, s32[64,1]{0,1:T(1,128)}, u32[]{:S(2)}) copy-start(s32[64,1]{0,1:T(1,128)} %param.13) | copy-start | bytes 772
  51.7 7.8 %collective-permute-start.9 = (bf16[128,768]{1,0:T(8,128)(2,1)S(1)}, bf16[128,768]{1,0:T(8,128)(2,1)S(1)}, u32[]{:S(2)}, u32[]{:S(2)}) collective-permute-start(bf16[128,768]{1,0:T(8,128)(2,1)S(1)} %get-tuple-element.37), channel_id=1, source_target_pairs={{0,2},{1,3},{2,0},{3,1},{4,6},{5,7},{6,4},{7,5},{8,10},{9,11},{10,... | collective-permute-start | bytes 589832 | tf_op jit(solution)/shard_map/ppermute | solution.py:373
  53.0 9.4 %collective-permute-start.10 = (bf16[128,768]{1,0:T(8,128)(2,1)S(1)}, bf16[128,768]{1,0:T(8,128)(2,1)S(1)}, u32[]{:S(2)}, u32[]{:S(2)}) collective-permute-start(bf16[128,768]{1,0:T(8,128)(2,1)S(1)} %encode_rest.3), channel_id=1, source_target_pairs={{0,130},{1,131},{2,128},{3,129},{4,134},{5,135},{6,132},{7,133},{8... | collective-permute-start | bytes 589832 | tf_op jit(solution)/shard_map/ppermute | solution.py:383
  62.3 26.6 %copy-start.1 = (bf16[256,768]{1,0:T(8,128)(2,1)S(1)}, bf16[256,768]{1,0:T(8,128)(2,1)}, u32[]{:S(2)}) copy-start(bf16[256,768]{1,0:T(8,128)(2,1)} %stale_ref.1) | copy-start | bytes 1179652
  63.6 44.1 %copy-start.2 = (f32[32,128]{1,0:T(8,128)S(1)}, f32[32,128]{1,0:T(8,128)}, u32[]{:S(2)}) copy-start(f32[32,128]{1,0:T(8,128)} %constant.7.clone.discount_ref) | copy-start | bytes 49156

commit v10 on v9

--- a/solution.py
+++ b/solution.py
@@ -237,8 +237,8 @@
 
         rows_s[0] = jnp.zeros((LANES, LANES), f32)
         spread(0)
-        lax.fori_loop(0, span, lambda i, _: block(i, span), 0)
-        lax.fori_loop(span, n_blocks, lambda i, _: block(i, span - 1), 0)
+        lax.fori_loop(0, span, lambda i, _: block(i, span), 0, unroll=2)
+        lax.fori_loop(span, n_blocks, lambda i, _: block(i, span - 1), 0, unroll=2)
         collect(n_blocks)
         folded = jnp.sum(columns[...], 1)
         wrapped = jnp.concatenate((folded[n_blocks:], jnp.zeros((span, LANES), f32)), 0)
@@ -321,6 +321,19 @@
         compiler_params=params(),
         name="share",
     )(grads, idsg, refreshed)
+
+
+def total_kernel(x_ref, out_ref):
+    out_ref[...] = jnp.sum(x_ref[...], 0)
+
+
+def total(x):
+    return pl.pallas_call(
+        total_kernel,
+        out_shape=jax.ShapeDtypeStruct(x.shape[1:], f32),
+        compiler_params=params(),
+        name="total",
+    )(x)
 
 
 Y, ZZ, ZL, X = 4, 4, 2, 2
@@ -452,9 +465,9 @@
     discount = (1.0 / np.log2(1.0 + position)).astype(np.float32).reshape(-1, LANES)
     grads, loss = pair(packed, jnp.asarray(discount))
     grads = lax.all_to_all(grads, "shard", split_axis=0, concat_axis=0, tiled=True)
-    shares = share(grads, idsg, again)
+    shares = share(grads, idsg, again).reshape(shards, 1, width)
     shares = lax.all_to_all(shares, "shard", split_axis=0, concat_axis=0, tiled=True)
-    return refreshed, jnp.sum(shares, 0, keepdims=True), loss[0, :1]
+    return refreshed, total(shares), loss[0, :1]
 
 
 def solution(mesh):

time: 158 us -> 157 us (level)
  no operation moved by 1% of the time
where the time goes in v10:
time: 157 us
  blocking collectives  74.7 us (48%)
  waiting for transfers between devices  29.4 us (19%)
  starting transfers between devices  25.7 us (16%)
  Pallas kernels  24 us (15%)
    all_to_all x1, blocking collectives, per_device(): lax.all_to_all(outgoing.reshape(shards, SUB, -1), 'shard', split_axis=0,...  25.4 us
    all_to_all x1, blocking collectives, per_device(): lax.all_to_all(packed, 'shard', split_axis=0, concat_axis=0, tiled=True)  17.5 us
    all_to_all x1, blocking collectives, per_device(): lax.all_to_all(shares, 'shard', split_axis=0, concat_axis=0, tiled=True)  16.2 us
    all_to_all x1, blocking collectives, per_device(): lax.all_to_all(grads, 'shard', split_axis=0, concat_axis=0, tiled=True)  15.7 us
    pallas_call x1, Pallas kernels, pair(): pl.pallas_call(pair_kernel, out_shape=(jax.ShapeDtypeStruct(x.shape, f32)...  14.5 us
    ppermute x2, starting transfers between devices, to_across(): return lax.ppermute(v, 'role', [(0, 2), (1, 3), (2, 0), (3, 1)])  11.5 us
    ppermute x3, waiting for transfers between devices, to_along(): lax.ppermute(v, 'shard', [(shard_at(y, zz, zl, x), shard_at(y, zz, 1 - zl...  9.93 us
    all_to_all x1, waiting for transfers between devices, gather_units(): lax.all_to_all(jnp.broadcast_to(block[None], (parts, units, width)), 'sha...  9.22 us
  transfers between devices with their start and end apart: 12, of which 8 were waited for; matrix products, arithmetic and copies ran while one was open for 0% of the time, Pallas kernels for 2%

profile of v10, /device:TPU:2, one launch (start us, length us, event | category | flops | bytes accessed | tf_op | source)
XLA Modules:
  0.0 156.9 jit_solution(18008115837231018075)
XLA Ops:
  0.6 0.9 pad_maximum_fusion
  1.6 0.7 collective-permute-start
  2.3 1.3 collective-permute-start.3
  3.6 0.7 collective-permute-start.2
  4.2 0.7 collective-permute-start.1
  4.9 9.4 %collective-permute-start.4 = (bf16[128,768]{1,0:T(8,128)(2,1)}, bf16[128,768]{1,0:T(8,128)(2,1)S(1)}, u32[]{:S(2)}, u32[]{:S(2)}) collective-permute-start(bf16[128,768]{1,0:T(8,128)(2,1)} %cls_ref.1), channel_id=1, source_target_pairs={{0,128},{64,192},{128,0},{192,64},{1,129},{65,193},{129,1},{193,65... | collective-permute-start | bytes 589832 | tf_op jit(solution)/shard_map/ppermute | solution.py:383
  14.3 3.8 %collective-permute-done.4.across_ref.refs_0_ = bf16[128,768]{1,0:T(8,128)(2,1)S(1)} collective-permute-done((bf16[128,768]{1,0:T(8,128)(2,1)}, bf16[128,768]{1,0:T(8,128)(2,1)S(1)}, u32[]{:S(2)}, u32[]{:S(2)}) %collective-permute-start.4) | collective-permute-done | bytes 196640 | tf_op jit(solution)/shard_map/ppermute | solution.py:383
  18.2 1.1 broadcast_in_dim.2
  19.3 6.1 %all-to-all-start = ((bf16[8,48,1536]{2,1,0:T(8,128)(2,1)}), bf16[8,48,1536]{2,1,0:T(8,128)(2,1)S(1)}, u32[]{:S(2)}, u32[]{:S(2)}) async-start(bf16[8,48,1536]{2,1,0:T(8,128)(2,1)} %broadcast_in_dim.2), calls=%async_computation | async-start | bytes 2359296 | tf_op jit(solution)/shard_map/all_to_all | solution.py:360
  25.5 1.1 collective-permute-start.5
  26.6 1.0 collective-permute-start.6
  27.7 3.5 %collective-permute-done.5.along_ref.refs_1_ = bf16[128,768]{1,0:T(8,128)(2,1)S(1)} collective-permute-done((bf16[128,768]{1,0:T(8,128)(2,1)S(1)}, bf16[128,768]{1,0:T(8,128)(2,1)S(1)}, u32[]{:S(2)}, u32[]{:S(2)}) %collective-permute-start.5) | collective-permute-done | bytes 196640 | tf_op jit(solution)/shard_map/ppermute | solution.py:386
  31.2 3.8 %collective-permute-done.6.diagonal_ref.refs_0_ = bf16[128,768]{1,0:T(8,128)(2,1)S(1)} collective-permute-done((bf16[128,768]{1,0:T(8,128)(2,1)S(1)}, bf16[128,768]{1,0:T(8,128)(2,1)S(1)}, u32[]{:S(2)}, u32[]{:S(2)}) %collective-permute-start.6) | collective-permute-done | bytes 196640 | tf_op jit(solution)/shard_map/ppermute | solution.py:386
  35.1 9.2 %all-to-all-done = bf16[8,48,1536]{2,1,0:T(8,128)(2,1)S(1)} async-done(((bf16[8,48,1536]{2,1,0:T(8,128)(2,1)}), bf16[8,48,1536]{2,1,0:T(8,128)(2,1)S(1)}, u32[]{:S(2)}, u32[]{:S(2)}) %all-to-all-start) | async-done | bytes 1179680 | tf_op jit(solution)/shard_map/all_to_all | solution.py:360
  44.3 1.1 collective-permute-start.7
  45.3 2.0 %encode.1.refs_2_.refs_3_ = f32[4,128,768]{2,1,0:T(8,128)S(1)} custom-call(bf16[128,768]{1,0:T(8,128)(2,1)S(1)} %copy-done, bf16[128,768]{1,0:T(8,128)(2,1)S(1)} %collective-permute-done.4.across_ref.refs_0_, bf16[128,768]{1,0:T(8,128)(2,1)S(1)} %collective-permute-done.5.along_ref.refs_1_, bf16[128,768]{1,0:T(8,128)(2,1)S(1)} %collective-permute-done.6.diagonal_ref.refs_0_, ...), custom_call_target="tpu_custom_call" | custom-call | tf_op jit(solution)/shard_map/encode/pallas_call | solution.py:43
  47.8 0.6 encode_rest.3
  48.4 1.1 encode_rest.5
  49.5 2.1 %collective-permute-start.8 = (bf16[128,768]{1,0:T(8,128)(2,1)S(1)}, bf16[128,768]{1,0:T(8,128)(2,1)S(1)}, u32[]{:S(2)}, u32[]{:S(2)}) collective-permute-start(bf16[128,768]{1,0:T(8,128)(2,1)S(1)} %get-tuple-element.36), channel_id=1, source_target_pairs={{0,128},{64,192},{128,0},{192,64},{1,129},{65,193},{129,1},{193,65... | collective-permute-start | bytes 589832 | tf_op jit(solution)/shard_map/ppermute | solution.py:383
  51.6 1.3 collective-permute-start.9
  53.8 3.0 %collective-permute-done.8.across_ref = bf16[128,768]{1,0:T(8,128)(2,1)S(1)} collective-permute-done((bf16[128,768]{1,0:T(8,128)(2,1)S(1)}, bf16[128,768]{1,0:T(8,128)(2,1)S(1)}, u32[]{:S(2)}, u32[]{:S(2)}) %collective-permute-start.8) | collective-permute-done | bytes 196640 | tf_op jit(solution)/shard_map/ppermute | solution.py:383
  56.9 2.6 %collective-permute-done.9.along_ref = bf16[128,768]{1,0:T(8,128)(2,1)S(1)} collective-permute-done((bf16[128,768]{1,0:T(8,128)(2,1)S(1)}, bf16[128,768]{1,0:T(8,128)(2,1)S(1)}, u32[]{:S(2)}, u32[]{:S(2)}) %collective-permute-start.9) | collective-permute-done | bytes 196640 | tf_op jit(solution)/shard_map/ppermute | solution.py:386
  59.4 2.9 %collective-permute-done.10.diagonal_ref = bf16[128,768]{1,0:T(8,128)(2,1)S(1)} collective-permute-done((bf16[128,768]{1,0:T(8,128)(2,1)S(1)}, bf16[128,768]{1,0:T(8,128)(2,1)S(1)}, u32[]{:S(2)}, u32[]{:S(2)}) %collective-permute-start.10) | collective-permute-done | bytes 196640 | tf_op jit(solution)/shard_map/ppermute | solution.py:396
  62.4 1.3 place.1
  63.7 25.4 %all_to_all.37 = bf16[64,8,512]{2,1,0:T(8,128)(2,1)S(1)} all-to-all(bf16[64,8,512]{2,1,0:T(8,128)(2,1)S(1)} %bitcast.19), channel_id=1, replica_groups=mesh['role'=4,'shard'=64] {'shard'}, dimensions={0} | all-to-all | bytes 1048576 | tf_op jit(solution)/shard_map/all_to_all | solution.py:458
  89.0 1.2 score.1
  90.2 17.5 %all_to_all.38 = f32[64,1,128]{2,1,0:T(1,128)S(1)} all-to-all(f32[64,1,128]{2,1,0:T(1,128)S(1)} %bitcast.23), channel_id=1, replica_groups=mesh['role'=4,'shard'=64] {'shard'}, dimensions={0} | all-to-all | bytes 65536 | tf_op jit(solution)/shard_map/all_to_all | solution.py:462
  107.7 14.5 %pair.1 = (f32[64,128]{1,0:T(8,128)S(1)}, f32[1,128]{1,0:T(1,128)}) custom-call(f32[64,128]{1,0:T(8,128)S(1)} %bitcast.22, f32[32,128]{1,0:T(8,128)S(1)} %copy-done.2), custom_call_target="tpu_custom_call" | custom-call | tf_op jit(solution)/shard_map/pair/pallas_call | solution.py:269
  122.3 15.7 %all_to_all.39 = f32[64,1,128]{2,1,0:T(1,128)S(1)} all-to-all(f32[64,1,128]{2,1,0:T(1,128)S(1)} %bitcast.24), channel_id=1, replica_groups=mesh['role'=4,'shard'=64] {'shard'}, dimensions={0} | all-to-all | bytes 65536 | tf_op jit(solution)/shard_map/all_to_all | solution.py:467
  137.9 2.0 %share.1 = f32[64,768]{1,0:T(8,128)S(1)} custom-call(f32[64,128]{1,0:T(8,128)S(1)} %bitcast.21, s32[64,128]{1,0:T(8,128)S(1)} %pad_add_fusion.idsg_ref, bf16[256,768]{1,0:T(8,128)(2,1)S(1)} %get-tuple-element.45.refreshed_ref), custom_call_target="tpu_custom_call" | custom-call | tf_op jit(solution)/shard_map/share/pallas_call | solution.py:317
  140.0 16.2 %all_to_all.40.x_ref = f32[64,1,768]{2,1,0:T(1,128)S(1)} all-to-all(f32[64,1,768]{2,1,0:T(1,128)S(1)} %reshape.34), channel_id=1, replica_groups=mesh['role'=4,'shard'=64] {'shard'}, dimensions={0} | all-to-all | bytes 393216 | tf_op jit(solution)/shard_map/all_to_all | solution.py:469
  156.2 0.7 total.1
  (26 shorter events, 1.6 us)
Async XLA Ops:
  1.6 0.7 collective-permute-start
  2.3 12.0 %collective-permute-start.3 = (bf16[48,1536]{1,0:T(8,128)(2,1)S(1)}, bf16[48,1536]{1,0:T(8,128)(2,1)S(1)}, u32[]{:S(2)}, u32[]{:S(2)}) collective-permute-start(bf16[48,1536]{1,0:T(8,128)(2,1)S(1)} %collective-permute-done), channel_id=1, source_target_pairs={{0,12},{1,13},{2,14},{3,15},{132,128},{133,129},{134,130},{135,131... | collective-permute-start | bytes 442376 | tf_op jit(solution)/shard_map/ppermute | solution.py:430
  3.6 10.7 %collective-permute-start.2 = (bf16[48,1536]{1,0:T(8,128)(2,1)S(1)}, bf16[48,1536]{1,0:T(8,128)(2,1)S(1)}, u32[]{:S(2)}, u32[]{:S(2)}) collective-permute-start(bf16[48,1536]{1,0:T(8,128)(2,1)S(1)} %collective-permute-done), channel_id=1, source_target_pairs={{0,8},{1,9},{2,10},{3,11},{132,140},{133,141},{134,142},{135,143},... | collective-permute-start | bytes 442376 | tf_op jit(solution)/shard_map/ppermute | solution.py:430
  4.2 10.1 %collective-permute-start.1 = (bf16[48,1536]{1,0:T(8,128)(2,1)S(1)}, bf16[48,1536]{1,0:T(8,128)(2,1)S(1)}, u32[]{:S(2)}, u32[]{:S(2)}) collective-permute-start(bf16[48,1536]{1,0:T(8,128)(2,1)S(1)} %collective-permute-done), channel_id=1, source_target_pairs={{0,4},{1,5},{2,6},{3,7},{132,136},{133,137},{134,138},{135,139},{7... | collective-permute-start | bytes 442376 | tf_op jit(solution)/shard_map/ppermute | solution.py:430
  4.9 13.2 %collective-permute-start.4 = (bf16[128,768]{1,0:T(8,128)(2,1)}, bf16[128,768]{1,0:T(8,128)(2,1)S(1)}, u32[]{:S(2)}, u32[]{:S(2)}) collective-permute-start(bf16[128,768]{1,0:T(8,128)(2,1)} %cls_ref.1), channel_id=1, source_target_pairs={{0,128},{64,192},{128,0},{192,64},{1,129},{65,193},{129,1},{193,65... | collective-permute-start | bytes 589832 | tf_op jit(solution)/shard_map/ppermute | solution.py:383
  19.3 6.2 %copy-start = (bf16[128,768]{1,0:T(8,128)(2,1)S(1)}, bf16[128,768]{1,0:T(8,128)(2,1)}, u32[]{:S(2)}) copy-start(bf16[128,768]{1,0:T(8,128)(2,1)} %cls_ref.1) | copy-start | bytes 589828
  19.3 8.3 %copy-start.6 = (bf16[1,768]{1,0:T(2,128)(2,1)S(1)}, bf16[1,768]{1,0:T(2,128)(2,1)}, u32[]{:S(2)}) copy-start(bf16[1,768]{1,0:T(2,128)(2,1)} %param.14) | copy-start | bytes 4612
  19.3 8.3 %copy-start.4 = (s32[64,64]{1,0:T(8,128)S(1)}, s32[64,64]{1,0:T(8,128)}, u32[]{:S(2)}) copy-start(s32[64,64]{1,0:T(8,128)} %param.16) | copy-start | bytes 49156
  19.3 8.3 %copy-start.5 = (s32[64,64]{1,0:T(8,128)S(1)}, s32[64,64]{1,0:T(8,128)}, u32[]{:S(2)}) copy-start(s32[64,64]{1,0:T(8,128)} %param.15) | copy-start | bytes 49156
  19.3 25.0 %all-to-all-start = ((bf16[8,48,1536]{2,1,0:T(8,128)(2,1)}), bf16[8,48,1536]{2,1,0:T(8,128)(2,1)S(1)}, u32[]{:S(2)}, u32[]{:S(2)}) async-start(bf16[8,48,1536]{2,1,0:T(8,128)(2,1)} %broadcast_in_dim.2), calls=%async_computation | async-start | bytes 2359296 | tf_op jit(solution)/shard_map/all_to_all | solution.py:360
  25.5 5.8 %collective-permute-start.5 = (bf16[128,768]{1,0:T(8,128)(2,1)S(1)}, bf16[128,768]{1,0:T(8,128)(2,1)S(1)}, u32[]{:S(2)}, u32[]{:S(2)}) collective-permute-start(bf16[128,768]{1,0:T(8,128)(2,1)S(1)} %copy-done), channel_id=1, source_target_pairs={{0,2},{1,3},{2,0},{3,1},{4,6},{5,7},{6,4},{7,5},{8,10},{9,11},{10,... | collective-permute-start | bytes 589832 | tf_op jit(solution)/shard_map/ppermute | solution.py:386
  26.6 8.5 %collective-permute-start.6 = (bf16[128,768]{1,0:T(8,128)(2,1)S(1)}, bf16[128,768]{1,0:T(8,128)(2,1)S(1)}, u32[]{:S(2)}, u32[]{:S(2)}) collective-permute-start(bf16[128,768]{1,0:T(8,128)(2,1)S(1)} %collective-permute-done.4.across_ref.refs_0_), channel_id=1, source_target_pairs={{0,2},{1,3},{2,0},{3,1},{4,6},{5,7},{6,4},{7,5},{8,10},{9,11},{10,... | collective-permute-start | bytes 589832 | tf_op jit(solution)/shard_map/ppermute | solution.py:386
  44.3 3.5 %collective-permute-start.7 = (bf16[384,1536]{1,0:T(8,128)(2,1)S(1)}, bf16[384,1536]{1,0:T(8,128)(2,1)S(1)}, u32[]{:S(2)}, u32[]{:S(2)}) collective-permute-start(bf16[384,1536]{1,0:T(8,128)(2,1)S(1)} %bitcast.17), channel_id=1, source_target_pairs={{0,64},{64,0},{128,192},{192,128},{1,65},{65,1},{129,193},{193,129... | collective-permute-start | bytes 3538952 | tf_op jit(solution)/shard_map/ppermute | solution.py:380
  49.5 7.3 %collective-permute-start.8 = (bf16[128,768]{1,0:T(8,128)(2,1)S(1)}, bf16[128,768]{1,0:T(8,128)(2,1)S(1)}, u32[]{:S(2)}, u32[]{:S(2)}) collective-permute-start(bf16[128,768]{1,0:T(8,128)(2,1)S(1)} %get-tuple-element.36), channel_id=1, source_target_pairs={{0,128},{64,192},{128,0},{192,64},{1,129},{65,193},{129,1},{193,65... | collective-permute-start | bytes 589832 | tf_op jit(solution)/shard_map/ppermute | solution.py:383
  51.6 10.7 %copy-start.3 = (s32[64,1]{0,1:T(1,128)S(1)}, s32[64,1]{0,1:T(1,128)}, u32[]{:S(2)}) copy-start(s32[64,1]{0,1:T(1,128)} %param.13) | copy-start | bytes 772
  51.6 7.8 %collective-permute-start.9 = (bf16[128,768]{1,0:T(8,128)(2,1)S(1)}, bf16[128,768]{1,0:T(8,128)(2,1)S(1)}, u32[]{:S(2)}, u32[]{:S(2)}) collective-permute-start(bf16[128,768]{1,0:T(8,128)(2,1)S(1)} %get-tuple-element.37), channel_id=1, source_target_pairs={{0,2},{1,3},{2,0},{3,1},{4,6},{5,7},{6,4},{7,5},{8,10},{9,11},{10,... | collective-permute-start | bytes 589832 | tf_op jit(solution)/shard_map/ppermute | solution.py:386
  53.0 9.4 %collective-permute-start.10 = (bf16[128,768]{1,0:T(8,128)(2,1)S(1)}, bf16[128,768]{1,0:T(8,128)(2,1)S(1)}, u32[]{:S(2)}, u32[]{:S(2)}) collective-permute-start(bf16[128,768]{1,0:T(8,128)(2,1)S(1)} %encode_rest.3), channel_id=1, source_target_pairs={{0,130},{1,131},{2,128},{3,129},{4,134},{5,135},{6,132},{7,133},{8... | collective-permute-start | bytes 589832 | tf_op jit(solution)/shard_map/ppermute | solution.py:396
  62.4 26.6 %copy-start.1 = (bf16[256,768]{1,0:T(8,128)(2,1)S(1)}, bf16[256,768]{1,0:T(8,128)(2,1)}, u32[]{:S(2)}) copy-start(bf16[256,768]{1,0:T(8,128)(2,1)} %stale_ref.1) | copy-start | bytes 1179652
  63.6 44.1 %copy-start.2 = (f32[32,128]{1,0:T(8,128)S(1)}, f32[32,128]{1,0:T(8,128)}, u32[]{:S(2)}) copy-start(f32[32,128]{1,0:T(8,128)} %constant.5.clone.discount_ref) | copy-start | bytes 49156

commit v11 on v10

--- a/solution.py
+++ b/solution.py
@@ -437,12 +437,11 @@
     units, xs, query, idsg = barrier((units, xs, query, idsg))
     other_units = to_core(units)
     so_far = first_half(xs, units)
-    (diagonal,) = second_half(xs, other_units, so_far, (3,), bf16)
-    from_diagonal = to_diagonal(diagonal)
-    other_units, diagonal = barrier((other_units, diagonal))
     across, along = second_half(xs, other_units, so_far, (1, 2), bf16)
     from_across = to_across(across)
     from_along = to_along(along)
+    (diagonal,) = second_half(xs, other_units, so_far, (3,), bf16)
+    from_diagonal = to_diagonal(diagonal)
     (own,) = second_half(xs, other_units, so_far, (0,), f32)
     outgoing = place(
         cls_states,

time: 157 us -> 157 us (level)
  no operation moved by 1% of the time
where the time goes in v11:
time: 157 us; the launch traced here: 156 us
  blocking collectives  74.7 us (48%)
  waiting for transfers between devices  28.7 us (18%)
  starting transfers between devices  25.8 us (16%)
  Pallas kernels  24 us (15%)
    all_to_all x1, blocking collectives, per_device(): lax.all_to_all(outgoing.reshape(shards, SUB, -1), 'shard', split_axis=0,...  25.4 us
    all_to_all x1, blocking collectives, per_device(): lax.all_to_all(packed, 'shard', split_axis=0, concat_axis=0, tiled=True)  17.5 us
    all_to_all x1, blocking collectives, per_device(): lax.all_to_all(shares, 'shard', split_axis=0, concat_axis=0, tiled=True)  16.2 us
    all_to_all x1, blocking collectives, per_device(): lax.all_to_all(grads, 'shard', split_axis=0, concat_axis=0, tiled=True)  15.7 us
    pallas_call x1, Pallas kernels, pair(): pl.pallas_call(pair_kernel, out_shape=(jax.ShapeDtypeStruct(x.shape, f32)...  14.5 us
    ppermute x2, starting transfers between devices, to_across(): return lax.ppermute(v, 'role', [(0, 2), (1, 3), (2, 0), (3, 1)])  11.5 us
    ppermute x3, waiting for transfers between devices, to_along(): lax.ppermute(v, 'shard', [(shard_at(y, zz, zl, x), shard_at(y, zz, 1 - zl...  9.94 us
    all_to_all x1, waiting for transfers between devices, gather_units(): lax.all_to_all(jnp.broadcast_to(block[None], (parts, units, width)), 'sha...  9.22 us
  transfers between devices with their start and end apart: 12, of which 8 were waited for; matrix products, arithmetic and copies ran while one was open for 0% of the time, Pallas kernels for 2%

profile of v11, /device:TPU:2, one launch (start us, length us, event | category | flops | bytes accessed | tf_op | source)
XLA Modules:
  0.0 156.3 jit_solution(15333392479414007240)
XLA Ops:
  0.6 0.9 pad_maximum_fusion
  1.6 0.7 collective-permute-start
  2.3 1.3 collective-permute-start.3
  3.6 0.7 collective-permute-start.2
  4.2 0.7 collective-permute-start.1
  4.9 9.4 %collective-permute-start.4 = (bf16[128,768]{1,0:T(8,128)(2,1)}, bf16[128,768]{1,0:T(8,128)(2,1)S(1)}, u32[]{:S(2)}, u32[]{:S(2)}) collective-permute-start(bf16[128,768]{1,0:T(8,128)(2,1)} %cls_ref.1), channel_id=1, source_target_pairs={{0,128},{64,192},{128,0},{192,64},{1,129},{65,193},{129,1},{193,65... | collective-permute-start | bytes 589832 | tf_op jit(solution)/shard_map/ppermute | solution.py:383
  14.3 3.8 %collective-permute-done.4.across_ref.refs_0_ = bf16[128,768]{1,0:T(8,128)(2,1)S(1)} collective-permute-done((bf16[128,768]{1,0:T(8,128)(2,1)}, bf16[128,768]{1,0:T(8,128)(2,1)S(1)}, u32[]{:S(2)}, u32[]{:S(2)}) %collective-permute-start.4) | collective-permute-done | bytes 196640 | tf_op jit(solution)/shard_map/ppermute | solution.py:383
  18.2 1.1 broadcast_in_dim.2
  19.3 6.1 %all-to-all-start = ((bf16[8,48,1536]{2,1,0:T(8,128)(2,1)}), bf16[8,48,1536]{2,1,0:T(8,128)(2,1)S(1)}, u32[]{:S(2)}, u32[]{:S(2)}) async-start(bf16[8,48,1536]{2,1,0:T(8,128)(2,1)} %broadcast_in_dim.2), calls=%async_computation | async-start | bytes 2359296 | tf_op jit(solution)/shard_map/all_to_all | solution.py:360
  25.5 1.1 collective-permute-start.5
  26.6 1.0 collective-permute-start.6
  27.7 3.5 %collective-permute-done.5.along_ref.refs_1_ = bf16[128,768]{1,0:T(8,128)(2,1)S(1)} collective-permute-done((bf16[128,768]{1,0:T(8,128)(2,1)S(1)}, bf16[128,768]{1,0:T(8,128)(2,1)S(1)}, u32[]{:S(2)}, u32[]{:S(2)}) %collective-permute-start.5) | collective-permute-done | bytes 196640 | tf_op jit(solution)/shard_map/ppermute | solution.py:386
  31.2 3.8 %collective-permute-done.6.diagonal_ref.refs_0_ = bf16[128,768]{1,0:T(8,128)(2,1)S(1)} collective-permute-done((bf16[128,768]{1,0:T(8,128)(2,1)S(1)}, bf16[128,768]{1,0:T(8,128)(2,1)S(1)}, u32[]{:S(2)}, u32[]{:S(2)}) %collective-permute-start.6) | collective-permute-done | bytes 196640 | tf_op jit(solution)/shard_map/ppermute | solution.py:386
  35.1 9.2 %all-to-all-done = bf16[8,48,1536]{2,1,0:T(8,128)(2,1)S(1)} async-done(((bf16[8,48,1536]{2,1,0:T(8,128)(2,1)}), bf16[8,48,1536]{2,1,0:T(8,128)(2,1)S(1)}, u32[]{:S(2)}, u32[]{:S(2)}) %all-to-all-start) | async-done | bytes 1179680 | tf_op jit(solution)/shard_map/all_to_all | solution.py:360
  44.3 1.1 collective-permute-start.7
  45.3 2.0 %encode.1.refs_2_.refs_3_ = f32[4,128,768]{2,1,0:T(8,128)S(1)} custom-call(bf16[128,768]{1,0:T(8,128)(2,1)S(1)} %copy-done, bf16[128,768]{1,0:T(8,128)(2,1)S(1)} %collective-permute-done.4.across_ref.refs_0_, bf16[128,768]{1,0:T(8,128)(2,1)S(1)} %collective-permute-done.5.along_ref.refs_1_, bf16[128,768]{1,0:T(8,128)(2,1)S(1)} %collective-permute-done.6.diagonal_ref.refs_0_, ...), custom_call_target="tpu_custom_call" | custom-call | tf_op jit(solution)/shard_map/encode/pallas_call | solution.py:43
  47.8 1.1 encode_rest.4
  48.9 2.1 %collective-permute-start.8 = (bf16[128,768]{1,0:T(8,128)(2,1)S(1)}, bf16[128,768]{1,0:T(8,128)(2,1)S(1)}, u32[]{:S(2)}, u32[]{:S(2)}) collective-permute-start(bf16[128,768]{1,0:T(8,128)(2,1)S(1)} %get-tuple-element.34), channel_id=1, source_target_pairs={{0,128},{64,192},{128,0},{192,64},{1,129},{65,193},{129,1},{193,65... | collective-permute-start | bytes 589832 | tf_op jit(solution)/shard_map/ppermute | solution.py:383
  51.0 1.3 collective-permute-start.9
  52.4 0.6 encode_rest.5
  53.9 2.3 %collective-permute-done.8.across_ref = bf16[128,768]{1,0:T(8,128)(2,1)S(1)} collective-permute-done((bf16[128,768]{1,0:T(8,128)(2,1)S(1)}, bf16[128,768]{1,0:T(8,128)(2,1)S(1)}, u32[]{:S(2)}, u32[]{:S(2)}) %collective-permute-start.8) | collective-permute-done | bytes 196640 | tf_op jit(solution)/shard_map/ppermute | solution.py:383
  56.2 2.6 %collective-permute-done.9.along_ref = bf16[128,768]{1,0:T(8,128)(2,1)S(1)} collective-permute-done((bf16[128,768]{1,0:T(8,128)(2,1)S(1)}, bf16[128,768]{1,0:T(8,128)(2,1)S(1)}, u32[]{:S(2)}, u32[]{:S(2)}) %collective-permute-start.9) | collective-permute-done | bytes 196640 | tf_op jit(solution)/shard_map/ppermute | solution.py:386
  58.8 2.9 %collective-permute-done.10.diagonal_ref = bf16[128,768]{1,0:T(8,128)(2,1)S(1)} collective-permute-done((bf16[128,768]{1,0:T(8,128)(2,1)S(1)}, bf16[128,768]{1,0:T(8,128)(2,1)S(1)}, u32[]{:S(2)}, u32[]{:S(2)}) %collective-permute-start.10) | collective-permute-done | bytes 196640 | tf_op jit(solution)/shard_map/ppermute | solution.py:396
  61.7 1.3 place.1
  63.0 25.4 %all_to_all.37 = bf16[64,8,512]{2,1,0:T(8,128)(2,1)S(1)} all-to-all(bf16[64,8,512]{2,1,0:T(8,128)(2,1)S(1)} %bitcast.19), channel_id=1, replica_groups=mesh['role'=4,'shard'=64] {'shard'}, dimensions={0} | all-to-all | bytes 1048576 | tf_op jit(solution)/shard_map/all_to_all | solution.py:457
  88.4 1.2 score.1
  89.6 17.5 %all_to_all.38 = f32[64,1,128]{2,1,0:T(1,128)S(1)} all-to-all(f32[64,1,128]{2,1,0:T(1,128)S(1)} %bitcast.23), channel_id=1, replica_groups=mesh['role'=4,'shard'=64] {'shard'}, dimensions={0} | all-to-all | bytes 65536 | tf_op jit(solution)/shard_map/all_to_all | solution.py:461
  107.1 14.5 %pair.1 = (f32[64,128]{1,0:T(8,128)S(1)}, f32[1,128]{1,0:T(1,128)}) custom-call(f32[64,128]{1,0:T(8,128)S(1)} %bitcast.22, f32[32,128]{1,0:T(8,128)S(1)} %copy-done.2), custom_call_target="tpu_custom_call" | custom-call | tf_op jit(solution)/shard_map/pair/pallas_call | solution.py:269
  121.6 15.7 %all_to_all.39 = f32[64,1,128]{2,1,0:T(1,128)S(1)} all-to-all(f32[64,1,128]{2,1,0:T(1,128)S(1)} %bitcast.24), channel_id=1, replica_groups=mesh['role'=4,'shard'=64] {'shard'}, dimensions={0} | all-to-all | bytes 65536 | tf_op jit(solution)/shard_map/all_to_all | solution.py:466
  137.3 2.0 %share.1 = f32[64,768]{1,0:T(8,128)S(1)} custom-call(f32[64,128]{1,0:T(8,128)S(1)} %bitcast.21, s32[64,128]{1,0:T(8,128)S(1)} %pad_add_fusion.idsg_ref, bf16[256,768]{1,0:T(8,128)(2,1)S(1)} %get-tuple-element.43.refreshed_ref), custom_call_target="tpu_custom_call" | custom-call | tf_op jit(solution)/shard_map/share/pallas_call | solution.py:317
  139.4 16.2 %all_to_all.40.x_ref = f32[64,1,768]{2,1,0:T(1,128)S(1)} all-to-all(f32[64,1,768]{2,1,0:T(1,128)S(1)} %reshape.34), channel_id=1, replica_groups=mesh['role'=4,'shard'=64] {'shard'}, dimensions={0} | all-to-all | bytes 393216 | tf_op jit(solution)/shard_map/all_to_all | solution.py:468
  155.6 0.7 total.1
  (26 shorter events, 1.7 us)
Async XLA Ops:
  1.6 0.7 collective-permute-start
  2.3 12.0 %collective-permute-start.3 = (bf16[48,1536]{1,0:T(8,128)(2,1)S(1)}, bf16[48,1536]{1,0:T(8,128)(2,1)S(1)}, u32[]{:S(2)}, u32[]{:S(2)}) collective-permute-start(bf16[48,1536]{1,0:T(8,128)(2,1)S(1)} %collective-permute-done), channel_id=1, source_target_pairs={{0,12},{1,13},{2,14},{3,15},{132,128},{133,129},{134,130},{135,131... | collective-permute-start | bytes 442376 | tf_op jit(solution)/shard_map/ppermute | solution.py:430
  3.6 10.7 %collective-permute-start.2 = (bf16[48,1536]{1,0:T(8,128)(2,1)S(1)}, bf16[48,1536]{1,0:T(8,128)(2,1)S(1)}, u32[]{:S(2)}, u32[]{:S(2)}) collective-permute-start(bf16[48,1536]{1,0:T(8,128)(2,1)S(1)} %collective-permute-done), channel_id=1, source_target_pairs={{0,8},{1,9},{2,10},{3,11},{132,140},{133,141},{134,142},{135,143},... | collective-permute-start | bytes 442376 | tf_op jit(solution)/shard_map/ppermute | solution.py:430
  4.2 10.1 %collective-permute-start.1 = (bf16[48,1536]{1,0:T(8,128)(2,1)S(1)}, bf16[48,1536]{1,0:T(8,128)(2,1)S(1)}, u32[]{:S(2)}, u32[]{:S(2)}) collective-permute-start(bf16[48,1536]{1,0:T(8,128)(2,1)S(1)} %collective-permute-done), channel_id=1, source_target_pairs={{0,4},{1,5},{2,6},{3,7},{132,136},{133,137},{134,138},{135,139},{7... | collective-permute-start | bytes 442376 | tf_op jit(solution)/shard_map/ppermute | solution.py:430
  4.9 13.2 %collective-permute-start.4 = (bf16[128,768]{1,0:T(8,128)(2,1)}, bf16[128,768]{1,0:T(8,128)(2,1)S(1)}, u32[]{:S(2)}, u32[]{:S(2)}) collective-permute-start(bf16[128,768]{1,0:T(8,128)(2,1)} %cls_ref.1), channel_id=1, source_target_pairs={{0,128},{64,192},{128,0},{192,64},{1,129},{65,193},{129,1},{193,65... | collective-permute-start | bytes 589832 | tf_op jit(solution)/shard_map/ppermute | solution.py:383
  19.3 6.2 %copy-start = (bf16[128,768]{1,0:T(8,128)(2,1)S(1)}, bf16[128,768]{1,0:T(8,128)(2,1)}, u32[]{:S(2)}) copy-start(bf16[128,768]{1,0:T(8,128)(2,1)} %cls_ref.1) | copy-start | bytes 589828
  19.3 8.3 %copy-start.6 = (bf16[1,768]{1,0:T(2,128)(2,1)S(1)}, bf16[1,768]{1,0:T(2,128)(2,1)}, u32[]{:S(2)}) copy-start(bf16[1,768]{1,0:T(2,128)(2,1)} %param.14) | copy-start | bytes 4612
  19.3 8.3 %copy-start.4 = (s32[64,64]{1,0:T(8,128)S(1)}, s32[64,64]{1,0:T(8,128)}, u32[]{:S(2)}) copy-start(s32[64,64]{1,0:T(8,128)} %param.16) | copy-start | bytes 49156
  19.3 8.3 %copy-start.5 = (s32[64,64]{1,0:T(8,128)S(1)}, s32[64,64]{1,0:T(8,128)}, u32[]{:S(2)}) copy-start(s32[64,64]{1,0:T(8,128)} %param.15) | copy-start | bytes 49156
  19.3 25.0 %all-to-all-start = ((bf16[8,48,1536]{2,1,0:T(8,128)(2,1)}), bf16[8,48,1536]{2,1,0:T(8,128)(2,1)S(1)}, u32[]{:S(2)}, u32[]{:S(2)}) async-start(bf16[8,48,1536]{2,1,0:T(8,128)(2,1)} %broadcast_in_dim.2), calls=%async_computation | async-start | bytes 2359296 | tf_op jit(solution)/shard_map/all_to_all | solution.py:360
  25.5 5.8 %collective-permute-start.5 = (bf16[128,768]{1,0:T(8,128)(2,1)S(1)}, bf16[128,768]{1,0:T(8,128)(2,1)S(1)}, u32[]{:S(2)}, u32[]{:S(2)}) collective-permute-start(bf16[128,768]{1,0:T(8,128)(2,1)S(1)} %copy-done), channel_id=1, source_target_pairs={{0,2},{1,3},{2,0},{3,1},{4,6},{5,7},{6,4},{7,5},{8,10},{9,11},{10,... | collective-permute-start | bytes 589832 | tf_op jit(solution)/shard_map/ppermute | solution.py:386
  26.6 8.5 %collective-permute-start.6 = (bf16[128,768]{1,0:T(8,128)(2,1)S(1)}, bf16[128,768]{1,0:T(8,128)(2,1)S(1)}, u32[]{:S(2)}, u32[]{:S(2)}) collective-permute-start(bf16[128,768]{1,0:T(8,128)(2,1)S(1)} %collective-permute-done.4.across_ref.refs_0_), channel_id=1, source_target_pairs={{0,2},{1,3},{2,0},{3,1},{4,6},{5,7},{6,4},{7,5},{8,10},{9,11},{10,... | collective-permute-start | bytes 589832 | tf_op jit(solution)/shard_map/ppermute | solution.py:386
  44.3 3.5 %collective-permute-start.7 = (bf16[384,1536]{1,0:T(8,128)(2,1)S(1)}, bf16[384,1536]{1,0:T(8,128)(2,1)S(1)}, u32[]{:S(2)}, u32[]{:S(2)}) collective-permute-start(bf16[384,1536]{1,0:T(8,128)(2,1)S(1)} %bitcast.17), channel_id=1, source_target_pairs={{0,64},{64,0},{128,192},{192,128},{1,65},{65,1},{129,193},{193,129... | collective-permute-start | bytes 3538952 | tf_op jit(solution)/shard_map/ppermute | solution.py:380
  48.9 7.3 %collective-permute-start.8 = (bf16[128,768]{1,0:T(8,128)(2,1)S(1)}, bf16[128,768]{1,0:T(8,128)(2,1)S(1)}, u32[]{:S(2)}, u32[]{:S(2)}) collective-permute-start(bf16[128,768]{1,0:T(8,128)(2,1)S(1)} %get-tuple-element.34), channel_id=1, source_target_pairs={{0,128},{64,192},{128,0},{192,64},{1,129},{65,193},{129,1},{193,65... | collective-permute-start | bytes 589832 | tf_op jit(solution)/shard_map/ppermute | solution.py:383
  51.0 7.8 %collective-permute-start.9 = (bf16[128,768]{1,0:T(8,128)(2,1)S(1)}, bf16[128,768]{1,0:T(8,128)(2,1)S(1)}, u32[]{:S(2)}, u32[]{:S(2)}) collective-permute-start(bf16[128,768]{1,0:T(8,128)(2,1)S(1)} %get-tuple-element.35), channel_id=1, source_target_pairs={{0,2},{1,3},{2,0},{3,1},{4,6},{5,7},{6,4},{7,5},{8,10},{9,11},{10,... | collective-permute-start | bytes 589832 | tf_op jit(solution)/shard_map/ppermute | solution.py:386
  53.0 8.7 %copy-start.3 = (s32[64,1]{0,1:T(1,128)S(1)}, s32[64,1]{0,1:T(1,128)}, u32[]{:S(2)}) copy-start(s32[64,1]{0,1:T(1,128)} %param.13) | copy-start | bytes 772
  53.0 8.7 %collective-permute-start.10 = (bf16[128,768]{1,0:T(8,128)(2,1)S(1)}, bf16[128,768]{1,0:T(8,128)(2,1)S(1)}, u32[]{:S(2)}, u32[]{:S(2)}) collective-permute-start(bf16[128,768]{1,0:T(8,128)(2,1)S(1)} %encode_rest.5), channel_id=1, source_target_pairs={{0,130},{1,131},{2,128},{3,129},{4,134},{5,135},{6,132},{7,133},{8... | collective-permute-start | bytes 589832 | tf_op jit(solution)/shard_map/ppermute | solution.py:396
  61.7 26.7 %copy-start.1 = (bf16[256,768]{1,0:T(8,128)(2,1)S(1)}, bf16[256,768]{1,0:T(8,128)(2,1)}, u32[]{:S(2)}) copy-start(bf16[256,768]{1,0:T(8,128)(2,1)} %stale_ref.1) | copy-start | bytes 1179652
  63.0 44.1 %copy-start.2 = (f32[32,128]{1,0:T(8,128)S(1)}, f32[32,128]{1,0:T(8,128)}, u32[]{:S(2)}) copy-start(f32[32,128]{1,0:T(8,128)} %constant.5.clone.discount_ref) | copy-start | bytes 49156

commit v12 on v11

--- a/solution.py
+++ b/solution.py
@@ -68,7 +68,7 @@
 
 
 def place_kernel(
-    cls_ref, own_ref, across_ref, along_ref, diagonal_ref, owner_ref, query_ref, out_ref
+    cls_ref, own_ref, across_ref, along_ref, diagonal_ref, owner_ref, query_ref, out_ref, placed_s, tiles_s
 ):
     rows, width = cls_ref.shape
     blocks = owner_ref.shape[1]
@@ -97,33 +97,37 @@
     )
     both = jnp.dot(both.astype(bf16), widen, preferred_element_type=f32)
     parity = lax.broadcasted_iota(jnp.int32, (1, rows), 1) & 1
-    target = both[0:1] * (2.0 * CAP * chunks) + (both[8:9] * 2.0 + parity.astype(f32)) * chunks
-
-    passage_rows = 2 * CAP * chunks
-    row = lax.broadcasted_iota(jnp.int32, (shards * passage_rows, rows), 0).astype(f32)
-    placed = jnp.zeros((shards * passage_rows, LANES), f32)
-    taken = jnp.zeros((shards * passage_rows, rows), f32)
+    target = both[0:1] * (2.0 * CAP) + both[8:9] * 2.0 + parity.astype(f32)
+
+    row = lax.broadcasted_iota(jnp.int32, (shards * 2 * CAP, rows), 0).astype(f32)
+    onto = (row == target).astype(f32)
+    filled = jnp.sum(onto, 1, keepdims=True) > 0.5
+    placed = jnp.dot(onto.astype(bf16), fresh, preferred_element_type=f32)
+    placed = jnp.where(filled, placed, EMPTY)
     for j in range(chunks):
-        onto = (row == target + float(j)).astype(f32)
-        taken = taken + onto
-        placed = placed + jnp.dot(
-            onto.astype(bf16), fresh[:, j * LANES : (j + 1) * LANES], preferred_element_type=f32
-        )
-    filled = jnp.dot(taken.astype(bf16), jnp.ones((rows, LANES), bf16), preferred_element_type=f32)
-    placed = jnp.where(filled > 0.5, placed, EMPTY).reshape(shards, passage_rows, LANES)
+        placed_s[j] = placed[:, j * LANES : (j + 1) * LANES]
+        for c in range(2 * CAP):
+            r = c * chunks + j
+            tiles_s[r // SUB, pl.ds(r % SUB, shards, stride=SUB), :] = placed_s[
+                j, pl.ds(c, shards, stride=2 * CAP), :
+            ]
     for tile in range(ROWS // SUB):
-        if tile < passage_rows // SUB:
-            part = placed[:, tile * SUB : (tile + 1) * SUB]
+        if tile < 2 * CAP * chunks // SUB:
+            part = tiles_s[tile]
         else:
             part = jnp.broadcast_to(query_ref[...].astype(f32)[None], (shards, SUB, LANES))
-        part = part.reshape(shards * SUB, LANES).astype(bf16)
-        out_ref[:, tile * LANES : (tile + 1) * LANES] = part
+            part = part.reshape(shards * SUB, LANES)
+        out_ref[:, tile * LANES : (tile + 1) * LANES] = part.astype(bf16)
 
 
 def place(cls_states, own, across, along, diagonal, owner, query, shards):
     return pl.pallas_call(
         place_kernel,
         out_shape=jax.ShapeDtypeStruct((shards * SUB, ROWS // SUB * LANES), bf16),
+        scratch_shapes=[
+            pltpu.VMEM((cls_states.shape[1] // LANES, shards * 2 * CAP, LANES), f32),
+            pltpu.VMEM((ROWS // SUB - 1, shards * SUB, LANES), f32),
+        ],
         compiler_params=params(),
         name="place",
     )(cls_states, own, across, along, diagonal, owner, query)
@@ -324,7 +328,7 @@
 
 
 def total_kernel(x_ref, out_ref):
-    out_ref[...] = jnp.sum(x_ref[...], 0)
+    out_ref[...] = jnp.sum(x_ref[...].astype(f32), 0)
 
 
 def total(x):

time: 157 us -> 156 us (level)
  no operation moved by 1% of the time
where the time goes in v12:
time: 156 us
  blocking collectives  74.7 us (48%)
  waiting for transfers between devices  28.7 us (18%)
  starting transfers between devices  25.8 us (17%)
  Pallas kernels  23.4 us (15%)
    all_to_all x1, blocking collectives, per_device(): lax.all_to_all(outgoing.reshape(shards, SUB, -1), 'shard', split_axis=0,...  25.4 us
    all_to_all x1, blocking collectives, per_device(): lax.all_to_all(packed, 'shard', split_axis=0, concat_axis=0, tiled=True)  17.5 us
    all_to_all x1, blocking collectives, per_device(): lax.all_to_all(shares, 'shard', split_axis=0, concat_axis=0, tiled=True)  16.2 us
    all_to_all x1, blocking collectives, per_device(): lax.all_to_all(grads, 'shard', split_axis=0, concat_axis=0, tiled=True)  15.7 us
    pallas_call x1, Pallas kernels, pair(): pl.pallas_call(pair_kernel, out_shape=(jax.ShapeDtypeStruct(x.shape, f32)...  14.5 us
    ppermute x2, starting transfers between devices, to_across(): return lax.ppermute(v, 'role', [(0, 2), (1, 3), (2, 0), (3, 1)])  11.5 us
    ppermute x3, waiting for transfers between devices, to_along(): lax.ppermute(v, 'shard', [(shard_at(y, zz, zl, x), shard_at(y, zz, 1 - zl...  9.94 us
    all_to_all x1, waiting for transfers between devices, gather_units(): lax.all_to_all(jnp.broadcast_to(block[None], (parts, units, width)), 'sha...  9.22 us
  transfers between devices with their start and end apart: 12, of which 8 were waited for; matrix products, arithmetic and copies ran while one was open for 0% of the time, Pallas kernels for 2%

profile of v12, /device:TPU:2, one launch (start us, length us, event | category | flops | bytes accessed | tf_op | source)
XLA Modules:
  0.0 155.7 jit_solution(3822230187947624863)
XLA Ops:
  0.6 0.9 pad_maximum_fusion
  1.6 0.7 collective-permute-start
  2.3 1.3 collective-permute-start.3
  3.6 0.7 collective-permute-start.2
  4.2 0.7 collective-permute-start.1
  4.9 9.4 %collective-permute-start.4 = (bf16[128,768]{1,0:T(8,128)(2,1)}, bf16[128,768]{1,0:T(8,128)(2,1)S(1)}, u32[]{:S(2)}, u32[]{:S(2)}) collective-permute-start(bf16[128,768]{1,0:T(8,128)(2,1)} %cls_ref.1), channel_id=1, source_target_pairs={{0,128},{64,192},{128,0},{192,64},{1,129},{65,193},{129,1},{193,65... | collective-permute-start | bytes 589832 | tf_op jit(solution)/shard_map/ppermute | solution.py:387
  14.3 3.8 %collective-permute-done.4.across_ref.refs_0_ = bf16[128,768]{1,0:T(8,128)(2,1)S(1)} collective-permute-done((bf16[128,768]{1,0:T(8,128)(2,1)}, bf16[128,768]{1,0:T(8,128)(2,1)S(1)}, u32[]{:S(2)}, u32[]{:S(2)}) %collective-permute-start.4) | collective-permute-done | bytes 196640 | tf_op jit(solution)/shard_map/ppermute | solution.py:387
  18.2 1.1 broadcast_in_dim.2
  19.3 6.1 %all-to-all-start = ((bf16[8,48,1536]{2,1,0:T(8,128)(2,1)}), bf16[8,48,1536]{2,1,0:T(8,128)(2,1)S(1)}, u32[]{:S(2)}, u32[]{:S(2)}) async-start(bf16[8,48,1536]{2,1,0:T(8,128)(2,1)} %broadcast_in_dim.2), calls=%async_computation | async-start | bytes 2359296 | tf_op jit(solution)/shard_map/all_to_all | solution.py:364
  25.5 1.1 collective-permute-start.5
  26.6 1.0 collective-permute-start.6
  27.7 3.5 %collective-permute-done.5.along_ref.refs_1_ = bf16[128,768]{1,0:T(8,128)(2,1)S(1)} collective-permute-done((bf16[128,768]{1,0:T(8,128)(2,1)S(1)}, bf16[128,768]{1,0:T(8,128)(2,1)S(1)}, u32[]{:S(2)}, u32[]{:S(2)}) %collective-permute-start.5) | collective-permute-done | bytes 196640 | tf_op jit(solution)/shard_map/ppermute | solution.py:390
  31.2 3.8 %collective-permute-done.6.diagonal_ref.refs_0_ = bf16[128,768]{1,0:T(8,128)(2,1)S(1)} collective-permute-done((bf16[128,768]{1,0:T(8,128)(2,1)S(1)}, bf16[128,768]{1,0:T(8,128)(2,1)S(1)}, u32[]{:S(2)}, u32[]{:S(2)}) %collective-permute-start.6) | collective-permute-done | bytes 196640 | tf_op jit(solution)/shard_map/ppermute | solution.py:390
  35.1 9.2 %all-to-all-done = bf16[8,48,1536]{2,1,0:T(8,128)(2,1)S(1)} async-done(((bf16[8,48,1536]{2,1,0:T(8,128)(2,1)}), bf16[8,48,1536]{2,1,0:T(8,128)(2,1)S(1)}, u32[]{:S(2)}, u32[]{:S(2)}) %all-to-all-start) | async-done | bytes 1179680 | tf_op jit(solution)/shard_map/all_to_all | solution.py:364
  44.3 1.1 collective-permute-start.7
  45.3 2.0 %encode.1.refs_2_.refs_3_ = f32[4,128,768]{2,1,0:T(8,128)S(1)} custom-call(bf16[128,768]{1,0:T(8,128)(2,1)S(1)} %copy-done, bf16[128,768]{1,0:T(8,128)(2,1)S(1)} %collective-permute-done.4.across_ref.refs_0_, bf16[128,768]{1,0:T(8,128)(2,1)S(1)} %collective-permute-done.5.along_ref.refs_1_, bf16[128,768]{1,0:T(8,128)(2,1)S(1)} %collective-permute-done.6.diagonal_ref.refs_0_, ...), custom_call_target="tpu_custom_call" | custom-call | tf_op jit(solution)/shard_map/encode/pallas_call | solution.py:43
  47.8 1.1 encode_rest.4
  48.9 2.1 %collective-permute-start.8 = (bf16[128,768]{1,0:T(8,128)(2,1)S(1)}, bf16[128,768]{1,0:T(8,128)(2,1)S(1)}, u32[]{:S(2)}, u32[]{:S(2)}) collective-permute-start(bf16[128,768]{1,0:T(8,128)(2,1)S(1)} %get-tuple-element.34), channel_id=1, source_target_pairs={{0,128},{64,192},{128,0},{192,64},{1,129},{65,193},{129,1},{193,65... | collective-permute-start | bytes 589832 | tf_op jit(solution)/shard_map/ppermute | solution.py:387
  51.0 1.3 collective-permute-start.9
  52.4 0.6 encode_rest.5
  53.9 2.3 %collective-permute-done.8.across_ref = bf16[128,768]{1,0:T(8,128)(2,1)S(1)} collective-permute-done((bf16[128,768]{1,0:T(8,128)(2,1)S(1)}, bf16[128,768]{1,0:T(8,128)(2,1)S(1)}, u32[]{:S(2)}, u32[]{:S(2)}) %collective-permute-start.8) | collective-permute-done | bytes 196640 | tf_op jit(solution)/shard_map/ppermute | solution.py:387
  56.2 2.6 %collective-permute-done.9.along_ref = bf16[128,768]{1,0:T(8,128)(2,1)S(1)} collective-permute-done((bf16[128,768]{1,0:T(8,128)(2,1)S(1)}, bf16[128,768]{1,0:T(8,128)(2,1)S(1)}, u32[]{:S(2)}, u32[]{:S(2)}) %collective-permute-start.9) | collective-permute-done | bytes 196640 | tf_op jit(solution)/shard_map/ppermute | solution.py:390
  58.8 2.9 %collective-permute-done.10.diagonal_ref = bf16[128,768]{1,0:T(8,128)(2,1)S(1)} collective-permute-done((bf16[128,768]{1,0:T(8,128)(2,1)S(1)}, bf16[128,768]{1,0:T(8,128)(2,1)S(1)}, u32[]{:S(2)}, u32[]{:S(2)}) %collective-permute-start.10) | collective-permute-done | bytes 196640 | tf_op jit(solution)/shard_map/ppermute | solution.py:400
  61.7 0.7 place.1
  62.4 25.4 %all_to_all.37 = bf16[64,8,512]{2,1,0:T(8,128)(2,1)S(1)} all-to-all(bf16[64,8,512]{2,1,0:T(8,128)(2,1)S(1)} %bitcast.19), channel_id=1, replica_groups=mesh['role'=4,'shard'=64] {'shard'}, dimensions={0} | all-to-all | bytes 1048576 | tf_op jit(solution)/shard_map/all_to_all | solution.py:461
  87.8 1.2 score.1
  89.0 17.5 %all_to_all.38 = f32[64,1,128]{2,1,0:T(1,128)S(1)} all-to-all(f32[64,1,128]{2,1,0:T(1,128)S(1)} %bitcast.23), channel_id=1, replica_groups=mesh['role'=4,'shard'=64] {'shard'}, dimensions={0} | all-to-all | bytes 65536 | tf_op jit(solution)/shard_map/all_to_all | solution.py:465
  106.5 14.5 %pair.1 = (f32[64,128]{1,0:T(8,128)S(1)}, f32[1,128]{1,0:T(1,128)}) custom-call(f32[64,128]{1,0:T(8,128)S(1)} %bitcast.22, f32[32,128]{1,0:T(8,128)S(1)} %copy-done.2), custom_call_target="tpu_custom_call" | custom-call | tf_op jit(solution)/shard_map/pair/pallas_call | solution.py:273
  121.0 15.7 %all_to_all.39 = f32[64,1,128]{2,1,0:T(1,128)S(1)} all-to-all(f32[64,1,128]{2,1,0:T(1,128)S(1)} %bitcast.24), channel_id=1, replica_groups=mesh['role'=4,'shard'=64] {'shard'}, dimensions={0} | all-to-all | bytes 65536 | tf_op jit(solution)/shard_map/all_to_all | solution.py:470
  136.7 2.0 %share.1 = f32[64,768]{1,0:T(8,128)S(1)} custom-call(f32[64,128]{1,0:T(8,128)S(1)} %bitcast.21, s32[64,128]{1,0:T(8,128)S(1)} %pad_add_fusion.idsg_ref, bf16[256,768]{1,0:T(8,128)(2,1)S(1)} %get-tuple-element.43.refreshed_ref), custom_call_target="tpu_custom_call" | custom-call | tf_op jit(solution)/shard_map/share/pallas_call | solution.py:321
  138.8 16.2 %all_to_all.40.x_ref = f32[64,1,768]{2,1,0:T(1,128)S(1)} all-to-all(f32[64,1,768]{2,1,0:T(1,128)S(1)} %reshape.34), channel_id=1, replica_groups=mesh['role'=4,'shard'=64] {'shard'}, dimensions={0} | all-to-all | bytes 393216 | tf_op jit(solution)/shard_map/all_to_all | solution.py:472
  155.0 0.7 total.1
  (26 shorter events, 1.7 us)
Async XLA Ops:
  1.6 0.7 collective-permute-start
  2.3 12.0 %collective-permute-start.3 = (bf16[48,1536]{1,0:T(8,128)(2,1)S(1)}, bf16[48,1536]{1,0:T(8,128)(2,1)S(1)}, u32[]{:S(2)}, u32[]{:S(2)}) collective-permute-start(bf16[48,1536]{1,0:T(8,128)(2,1)S(1)} %collective-permute-done), channel_id=1, source_target_pairs={{0,12},{1,13},{2,14},{3,15},{132,128},{133,129},{134,130},{135,131... | collective-permute-start | bytes 442376 | tf_op jit(solution)/shard_map/ppermute | solution.py:434
  3.6 10.7 %collective-permute-start.2 = (bf16[48,1536]{1,0:T(8,128)(2,1)S(1)}, bf16[48,1536]{1,0:T(8,128)(2,1)S(1)}, u32[]{:S(2)}, u32[]{:S(2)}) collective-permute-start(bf16[48,1536]{1,0:T(8,128)(2,1)S(1)} %collective-permute-done), channel_id=1, source_target_pairs={{0,8},{1,9},{2,10},{3,11},{132,140},{133,141},{134,142},{135,143},... | collective-permute-start | bytes 442376 | tf_op jit(solution)/shard_map/ppermute | solution.py:434
  4.2 10.1 %collective-permute-start.1 = (bf16[48,1536]{1,0:T(8,128)(2,1)S(1)}, bf16[48,1536]{1,0:T(8,128)(2,1)S(1)}, u32[]{:S(2)}, u32[]{:S(2)}) collective-permute-start(bf16[48,1536]{1,0:T(8,128)(2,1)S(1)} %collective-permute-done), channel_id=1, source_target_pairs={{0,4},{1,5},{2,6},{3,7},{132,136},{133,137},{134,138},{135,139},{7... | collective-permute-start | bytes 442376 | tf_op jit(solution)/shard_map/ppermute | solution.py:434
  4.9 13.2 %collective-permute-start.4 = (bf16[128,768]{1,0:T(8,128)(2,1)}, bf16[128,768]{1,0:T(8,128)(2,1)S(1)}, u32[]{:S(2)}, u32[]{:S(2)}) collective-permute-start(bf16[128,768]{1,0:T(8,128)(2,1)} %cls_ref.1), channel_id=1, source_target_pairs={{0,128},{64,192},{128,0},{192,64},{1,129},{65,193},{129,1},{193,65... | collective-permute-start | bytes 589832 | tf_op jit(solution)/shard_map/ppermute | solution.py:387
  19.3 6.2 %copy-start = (bf16[128,768]{1,0:T(8,128)(2,1)S(1)}, bf16[128,768]{1,0:T(8,128)(2,1)}, u32[]{:S(2)}) copy-start(bf16[128,768]{1,0:T(8,128)(2,1)} %cls_ref.1) | copy-start | bytes 589828
  19.3 8.3 %copy-start.6 = (bf16[1,768]{1,0:T(2,128)(2,1)S(1)}, bf16[1,768]{1,0:T(2,128)(2,1)}, u32[]{:S(2)}) copy-start(bf16[1,768]{1,0:T(2,128)(2,1)} %param.14) | copy-start | bytes 4612
  19.3 8.3 %copy-start.4 = (s32[64,64]{1,0:T(8,128)S(1)}, s32[64,64]{1,0:T(8,128)}, u32[]{:S(2)}) copy-start(s32[64,64]{1,0:T(8,128)} %param.16) | copy-start | bytes 49156
  19.3 8.3 %copy-start.5 = (s32[64,64]{1,0:T(8,128)S(1)}, s32[64,64]{1,0:T(8,128)}, u32[]{:S(2)}) copy-start(s32[64,64]{1,0:T(8,128)} %param.15) | copy-start | bytes 49156
  19.3 25.0 %all-to-all-start = ((bf16[8,48,1536]{2,1,0:T(8,128)(2,1)}), bf16[8,48,1536]{2,1,0:T(8,128)(2,1)S(1)}, u32[]{:S(2)}, u32[]{:S(2)}) async-start(bf16[8,48,1536]{2,1,0:T(8,128)(2,1)} %broadcast_in_dim.2), calls=%async_computation | async-start | bytes 2359296 | tf_op jit(solution)/shard_map/all_to_all | solution.py:364
  25.5 5.8 %collective-permute-start.5 = (bf16[128,768]{1,0:T(8,128)(2,1)S(1)}, bf16[128,768]{1,0:T(8,128)(2,1)S(1)}, u32[]{:S(2)}, u32[]{:S(2)}) collective-permute-start(bf16[128,768]{1,0:T(8,128)(2,1)S(1)} %copy-done), channel_id=1, source_target_pairs={{0,2},{1,3},{2,0},{3,1},{4,6},{5,7},{6,4},{7,5},{8,10},{9,11},{10,... | collective-permute-start | bytes 589832 | tf_op jit(solution)/shard_map/ppermute | solution.py:390
  26.6 8.5 %collective-permute-start.6 = (bf16[128,768]{1,0:T(8,128)(2,1)S(1)}, bf16[128,768]{1,0:T(8,128)(2,1)S(1)}, u32[]{:S(2)}, u32[]{:S(2)}) collective-permute-start(bf16[128,768]{1,0:T(8,128)(2,1)S(1)} %collective-permute-done.4.across_ref.refs_0_), channel_id=1, source_target_pairs={{0,2},{1,3},{2,0},{3,1},{4,6},{5,7},{6,4},{7,5},{8,10},{9,11},{10,... | collective-permute-start | bytes 589832 | tf_op jit(solution)/shard_map/ppermute | solution.py:390
  44.3 3.5 %collective-permute-start.7 = (bf16[384,1536]{1,0:T(8,128)(2,1)S(1)}, bf16[384,1536]{1,0:T(8,128)(2,1)S(1)}, u32[]{:S(2)}, u32[]{:S(2)}) collective-permute-start(bf16[384,1536]{1,0:T(8,128)(2,1)S(1)} %bitcast.17), channel_id=1, source_target_pairs={{0,64},{64,0},{128,192},{192,128},{1,65},{65,1},{129,193},{193,129... | collective-permute-start | bytes 3538952 | tf_op jit(solution)/shard_map/ppermute | solution.py:384
  48.9 7.3 %collective-permute-start.8 = (bf16[128,768]{1,0:T(8,128)(2,1)S(1)}, bf16[128,768]{1,0:T(8,128)(2,1)S(1)}, u32[]{:S(2)}, u32[]{:S(2)}) collective-permute-start(bf16[128,768]{1,0:T(8,128)(2,1)S(1)} %get-tuple-element.34), channel_id=1, source_target_pairs={{0,128},{64,192},{128,0},{192,64},{1,129},{65,193},{129,1},{193,65... | collective-permute-start | bytes 589832 | tf_op jit(solution)/shard_map/ppermute | solution.py:387
  51.0 7.8 %collective-permute-start.9 = (bf16[128,768]{1,0:T(8,128)(2,1)S(1)}, bf16[128,768]{1,0:T(8,128)(2,1)S(1)}, u32[]{:S(2)}, u32[]{:S(2)}) collective-permute-start(bf16[128,768]{1,0:T(8,128)(2,1)S(1)} %get-tuple-element.35), channel_id=1, source_target_pairs={{0,2},{1,3},{2,0},{3,1},{4,6},{5,7},{6,4},{7,5},{8,10},{9,11},{10,... | collective-permute-start | bytes 589832 | tf_op jit(solution)/shard_map/ppermute | solution.py:390
  53.0 8.7 %copy-start.3 = (s32[64,1]{0,1:T(1,128)S(1)}, s32[64,1]{0,1:T(1,128)}, u32[]{:S(2)}) copy-start(s32[64,1]{0,1:T(1,128)} %param.13) | copy-start | bytes 772
  53.0 8.7 %collective-permute-start.10 = (bf16[128,768]{1,0:T(8,128)(2,1)S(1)}, bf16[128,768]{1,0:T(8,128)(2,1)S(1)}, u32[]{:S(2)}, u32[]{:S(2)}) collective-permute-start(bf16[128,768]{1,0:T(8,128)(2,1)S(1)} %encode_rest.5), channel_id=1, source_target_pairs={{0,130},{1,131},{2,128},{3,129},{4,134},{5,135},{6,132},{7,133},{8... | collective-permute-start | bytes 589832 | tf_op jit(solution)/shard_map/ppermute | solution.py:400
  61.7 26.1 %copy-start.1 = (bf16[256,768]{1,0:T(8,128)(2,1)S(1)}, bf16[256,768]{1,0:T(8,128)(2,1)}, u32[]{:S(2)}) copy-start(bf16[256,768]{1,0:T(8,128)(2,1)} %stale_ref.1) | copy-start | bytes 1179652
  62.4 44.1 %copy-start.2 = (f32[32,128]{1,0:T(8,128)S(1)}, f32[32,128]{1,0:T(8,128)}, u32[]{:S(2)}) copy-start(f32[32,128]{1,0:T(8,128)} %constant.5.clone.discount_ref) | copy-start | bytes 49156
